TPU v7x, 512 devices: a whole 4x8x8 slice. The times are simulated.
512 devices in a mesh: dp: 512 (over z, x, y, core).
Axes of the slice: x: 4, y: 8, z: 8, core: 2. Of those that a mesh axis runs over, the one named last changes fastest.
Arguments:
- images: bfloat16 [163840, 1152], P('dp'), may hold values from -6 to 6
- texts: bfloat16 [163840, 640], P('dp'), may hold values from -6 to 6
- head: bfloat16 [1152, 640], replicated, may hold values from -0.1875 to 0.1875
- log_scale: float32 [1], replicated, may hold values from 2 to 2.6
- bias: float32 [1], replicated, may hold values from -4 to -2
Outputs:
- grad_image: bfloat16 [163840, 1152], P('dp')
- grad_text: bfloat16 [163840, 640], P('dp')
- grad_head: bfloat16 [1152, 640], replicated
All inputs are finite; a program needn't handle non-finite values.
Results may differ from a plain program's by a relative error of at most 0.0065.
Values may be sent and summed in bfloat16 or wider, within the bound.
No kernel may reach another device: no remote copies, remote signals or barrier semaphores. Data moves between devices by JAX's collectives and lax.ppermute only.
A program may use at most 64 MiB of HBM per device.

v0:
```python
import jax
import jax.numpy as jnp
from jax import lax
from jax.sharding import PartitionSpec as P

ROWS = 320
STEPS = 4


def shifted(value, axis, steps):
    count = lax.axis_size(axis)
    pairs = [(source, (source + steps) % count) for source in range(count)]
    return lax.ppermute(value, axis, pairs)


def normalize(values):
    inverse = lax.rsqrt(jnp.sum(values * values, axis=-1, keepdims=True) + 1e-06)
    return (values * inverse, inverse)


def pair_tile(img_b, other, temper, offset, diagonal):
    dots = jnp.einsum("re,qe->rq", img_b, other, preferred_element_type=jnp.float32)
    logit = temper * dots + offset
    slope = (temper * (jax.nn.sigmoid(logit) - diagonal)).astype(jnp.bfloat16)
    d_img = jnp.dot(slope, other, preferred_element_type=jnp.float32)
    d_other = jnp.einsum("rq,re->qe", slope, img_b, preferred_element_type=jnp.float32)
    return (d_img, d_other)


def shards(images, texts, head, log_scale, bias):
    temper = jnp.exp(log_scale[0])
    offset = bias[0]
    proj = jnp.dot(images, head, preferred_element_type=jnp.float32)
    img_n, img_inv = normalize(proj)
    img_b = img_n.astype(jnp.bfloat16)
    txt_n, txt_inv = normalize(texts.astype(jnp.float32))
    txt_b = txt_n.astype(jnp.bfloat16)
    count = images.shape[0]
    identity = jnp.eye(count, dtype=jnp.float32)
    zeroed = jnp.zeros_like(identity)
    moving = txt_b
    d_img = jnp.zeros(txt_n.shape, jnp.float32)
    carried = d_img
    for step in range(STEPS):
        if step > 0:
            moving = shifted(moving, "dp", 1)
        diagonal = identity if step == 0 else zeroed
        part_img, part_txt = pair_tile(img_b, moving, temper, offset, diagonal)
        d_img = d_img + part_img
        if step > 0:
            carried = shifted(carried, "dp", 1) + part_txt
        else:
            carried = part_txt
    d_txt = shifted(carried, "dp", -(STEPS - 1))
    d_proj = ((d_img - img_n * jnp.sum(img_n * d_img, axis=-1, keepdims=True)) * img_inv).astype(
        jnp.bfloat16
    )
    grad_image = lax.dot_general(
        d_proj, head, (((1,), (1,)), ((), ())), preferred_element_type=jnp.float32
    ).astype(jnp.bfloat16)
    grad_text = ((d_txt - txt_n * jnp.sum(txt_n * d_txt, axis=-1, keepdims=True)) * txt_inv).astype(
        jnp.bfloat16
    )
    head_part = lax.dot_general(
        images, d_proj, (((0,), (0,)), ((), ())), preferred_element_type=jnp.float32
    )
    factor = 1.0 / jnp.sqrt(jnp.float32(ROWS))
    head_total = lax.psum(head_part, "dp")
    grad_head = (head_total * factor).astype(jnp.bfloat16)
    return (grad_image, grad_text, grad_head)


def solution(mesh):
    in_specs = (P("dp", None), P("dp", None), P(), P(), P())
    out_specs = (P("dp", None), P("dp", None), P())
    return jax.shard_map(shards, mesh=mesh, in_specs=in_specs, out_specs=out_specs, check_vma=False)
```

profile of v0, /device:TPU:1, one launch (start us, length us, event | category | flops | bytes accessed | tf_op | source)
XLA Modules:
  0.0 360.9 jit_solution(10139486562838607624)
XLA Ops:
  7.2 0.0 copy-start
  7.2 0.0 all-reduce.2.cloned.1.call-start
  7.2 1.3 fusion.36
  8.5 1.1 fusion.31
  9.7 4.6 %collective-permute-start = (bf16[320,640]{1,0:T(8,128)(2,1)S(1)}, bf16[320,640]{1,0:T(8,128)(2,1)S(1)}, u32[]{:S(2)}, u32[]{:S(2)}) collective-permute-start(bf16[320,640]{1,0:T(8,128)(2,1)S(1)} %fusion.31), channel_id=1, source_target_pairs={{0,1},{1,2},{2,3},{3,4},{4,5},{5,6},{6,7},{7,8},{8,9},{9,10},{10,1... | collective-permute-start | bytes 1228808 | tf_op jit(solution)/shard_map/ppermute | solution.py:13
  14.3 0.0 copy-done
  14.3 2.0 multiply_reduce_fusion.1
  17.6 0.1 multiply_convert_fusion.2
  17.8 0.5 fusion.25
  18.3 0.4 fusion.38
  18.7 1.9 collective-permute-start.3
  20.6 0.4 fusion.37
  21.0 0.0 collective-permute-done
  21.0 3.6 collective-permute-start.1
  24.6 0.5 fusion.26
  25.1 0.4 convolution_add_fusion.3
  25.5 4.4 %collective-permute-done.3 = f32[320,640]{1,0:T(8,128)S(1)} collective-permute-done((f32[320,640]{1,0:T(8,128)S(1)}, f32[320,640]{1,0:T(8,128)S(1)}, u32[]{:S(2)}, u32[]{:S(2)}) %collective-permute-start.3) | collective-permute-done | bytes 819232 | tf_op jit(solution)/shard_map/ppermute | solution.py:13
  29.9 1.3 convolution_add_fusion
  31.2 4.4 %collective-permute-start.4 = (f32[320,640]{1,0:T(8,128)}, f32[320,640]{1,0:T(8,128)}, u32[]{:S(2)}, u32[]{:S(2)}) collective-permute-start(f32[320,640]{1,0:T(8,128)} %convolution_add_fusion), channel_id=1, source_target_pairs={{0,1},{1,2},{2,3},{3,4},{4,5},{5,6},{6,7},{7,8},{8,9},{9,10},{10,1... | collective-permute-start | bytes 2457608 | tf_op jit(solution)/shard_map/ppermute | solution.py:13
  35.6 0.0 collective-permute-done.1
  35.6 3.0 collective-permute-start.2
  38.7 0.5 fusion.27
  39.1 0.4 convolution_add_fusion.2
  39.5 11.0 %collective-permute-done.2 = bf16[320,640]{1,0:T(8,128)(2,1)S(1)} collective-permute-done((bf16[320,640]{1,0:T(8,128)(2,1)S(1)}, bf16[320,640]{1,0:T(8,128)(2,1)S(1)}, u32[]{:S(2)}, u32[]{:S(2)}) %collective-permute-start.2) | collective-permute-done | bytes 409632 | tf_op jit(solution)/shard_map/ppermute | solution.py:13
  50.5 0.5 fusion.28
  51.0 0.5 multiply_reduce_fusion
  51.5 0.0 copy-start.2
  51.5 0.2 multiply_convert_fusion.1
  51.7 0.9 copy-done.2
  52.6 2.6 convolution_bitcast_fusion
  55.3 0.0 all-reduce.2.cloned.1.call-update
  55.3 0.4 fusion.39
  55.7 0.0 collective-permute-done.4
  55.7 1.2 add.81
  57.0 3.3 collective-permute-start.5
  60.3 0.4 fusion.40
  60.7 17.5 %collective-permute-done.5 = f32[320,640]{1,0:T(8,128)S(1)} collective-permute-done((f32[320,640]{1,0:T(8,128)S(1)}, f32[320,640]{1,0:T(8,128)S(1)}, u32[]{:S(2)}, u32[]{:S(2)}) %collective-permute-start.5) | collective-permute-done | bytes 819232 | tf_op jit(solution)/shard_map/ppermute | solution.py:13
  78.2 1.0 add.82
  79.2 8.3 %collective-permute-start.6 = (f32[320,640]{1,0:T(8,128)}, f32[320,640]{1,0:T(8,128)}, u32[]{:S(2)}, u32[]{:S(2)}) collective-permute-start(f32[320,640]{1,0:T(8,128)} %add.82), channel_id=1, source_target_pairs={{0,509},{1,510},{2,511},{3,0},{4,1},{5,2},{6,3},{7,4},{8,5},{9,6},... | collective-permute-start | bytes 2457608 | tf_op jit(solution)/shard_map/ppermute | solution.py:13
  87.5 1.7 convolution_convert_fusion
  89.1 257.2 %all-reduce.2.cloned.1.call-done = f32[1152,640]{0,1:T(8,128)} async-done(((f32[1152,640]{0,1:T(8,128)}), f32[1152,640]{0,1:T(8,128)}) %all-reduce.2.cloned.1.call-update) | async-done | bytes 2949136 | tf_op jit(solution)/shard_map/psum | solution.py:68
  346.3 2.1 multiply_convert_fusion
  348.4 0.0 copy-start.1
  348.4 2.1 copy.8
  350.5 0.0 collective-permute-done.6
  350.5 0.0 copy-done.1
  350.5 1.4 fusion.32
  351.9 2.1 fusion.35
  (2 shorter events, 0.0 us)
Async XLA Ops:
  7.2 7.1 %copy-start = (bf16[1152,640]{1,0:T(8,128)(2,1)S(1)}, bf16[1152,640]{1,0:T(8,128)(2,1)}, u32[]{:S(2)}) copy-start(bf16[1152,640]{1,0:T(8,128)(2,1)} %param.7) | copy-start | bytes 4423684
  7.2 339.1 %all-reduce.2.cloned.1.call-start = ((), (), s32[]{:S(2)}) async-start(), calls=%async_computation | async-start | bytes 5898240 | tf_op jit(solution)/shard_map/psum | solution.py:68
  9.7 11.3 %collective-permute-start = (bf16[320,640]{1,0:T(8,128)(2,1)S(1)}, bf16[320,640]{1,0:T(8,128)(2,1)S(1)}, u32[]{:S(2)}, u32[]{:S(2)}) collective-permute-start(bf16[320,640]{1,0:T(8,128)(2,1)S(1)} %fusion.31), channel_id=1, source_target_pairs={{0,1},{1,2},{2,3},{3,4},{4,5},{5,6},{6,7},{7,8},{8,9},{9,10},{10,1... | collective-permute-start | bytes 1228808 | tf_op jit(solution)/shard_map/ppermute | solution.py:13
  18.7 11.2 %collective-permute-start.3 = (f32[320,640]{1,0:T(8,128)S(1)}, f32[320,640]{1,0:T(8,128)S(1)}, u32[]{:S(2)}, u32[]{:S(2)}) collective-permute-start(f32[320,640]{1,0:T(8,128)S(1)} %fusion.38), channel_id=1, source_target_pairs={{0,1},{1,2},{2,3},{3,4},{4,5},{5,6},{6,7},{7,8},{8,9},{9,10},{10,1... | collective-permute-start | bytes 2457608 | tf_op jit(solution)/shard_map/ppermute | solution.py:13
  21.0 14.6 %collective-permute-start.1 = (bf16[320,640]{1,0:T(8,128)(2,1)S(1)}, bf16[320,640]{1,0:T(8,128)(2,1)S(1)}, u32[]{:S(2)}, u32[]{:S(2)}) collective-permute-start(bf16[320,640]{1,0:T(8,128)(2,1)S(1)} %collective-permute-done), channel_id=1, source_target_pairs={{0,1},{1,2},{2,3},{3,4},{4,5},{5,6},{6,7},{7,8},{8,9},{9,10},{10,1... | collective-permute-start | bytes 1228808 | tf_op jit(solution)/shard_map/ppermute | solution.py:13
  31.2 24.5 %collective-permute-start.4 = (f32[320,640]{1,0:T(8,128)}, f32[320,640]{1,0:T(8,128)}, u32[]{:S(2)}, u32[]{:S(2)}) collective-permute-start(f32[320,640]{1,0:T(8,128)} %convolution_add_fusion), channel_id=1, source_target_pairs={{0,1},{1,2},{2,3},{3,4},{4,5},{5,6},{6,7},{7,8},{8,9},{9,10},{10,1... | collective-permute-start | bytes 2457608 | tf_op jit(solution)/shard_map/ppermute | solution.py:13
  35.6 14.9 %collective-permute-start.2 = (bf16[320,640]{1,0:T(8,128)(2,1)S(1)}, bf16[320,640]{1,0:T(8,128)(2,1)S(1)}, u32[]{:S(2)}, u32[]{:S(2)}) collective-permute-start(bf16[320,640]{1,0:T(8,128)(2,1)S(1)} %collective-permute-done.1), channel_id=1, source_target_pairs={{0,1},{1,2},{2,3},{3,4},{4,5},{5,6},{6,7},{7,8},{8,9},{9,10},{10,1... | collective-permute-start | bytes 1228808 | tf_op jit(solution)/shard_map/ppermute | solution.py:13
  51.5 1.1 copy-start.2
  57.0 21.2 %collective-permute-start.5 = (f32[320,640]{1,0:T(8,128)S(1)}, f32[320,640]{1,0:T(8,128)S(1)}, u32[]{:S(2)}, u32[]{:S(2)}) collective-permute-start(f32[320,640]{1,0:T(8,128)S(1)} %add.81), channel_id=1, source_target_pairs={{0,1},{1,2},{2,3},{3,4},{4,5},{5,6},{6,7},{7,8},{8,9},{9,10},{10,1... | collective-permute-start | bytes 2457608 | tf_op jit(solution)/shard_map/ppermute | solution.py:13
  79.2 271.3 %collective-permute-start.6 = (f32[320,640]{1,0:T(8,128)}, f32[320,640]{1,0:T(8,128)}, u32[]{:S(2)}, u32[]{:S(2)}) collective-permute-start(f32[320,640]{1,0:T(8,128)} %add.82), channel_id=1, source_target_pairs={{0,509},{1,510},{2,511},{3,0},{4,1},{5,2},{6,3},{7,4},{8,5},{9,6},... | collective-permute-start | bytes 2457608 | tf_op jit(solution)/shard_map/ppermute | solution.py:13
  348.4 2.1 copy-start.1
Sparse Core Ops, SparseCore 0:
  55.4 290.8 all-reduce.1
where the time goes:
time: 362 us; the launch traced here: 361 us
  waiting for transfers between devices  290 us (80%)
  starting transfers between devices  29.2 us (8%)
  between operations  15.6 us (4%)
  matrix products  12.4 us (3%)
  other arithmetic  10.6 us (3%)
    psum x1, waiting for transfers between devices, shards(): head_total = lax.psum(head_part, 'dp')  257 us
    ppermute x7, waiting for transfers between devices, shifted(): return lax.ppermute(value, axis, pairs)  32.9 us
    ppermute x7, starting transfers between devices, shifted(): return lax.ppermute(value, axis, pairs)  29.1 us
  transfers between devices with their start and end apart: 8, of which 4 were waited for; matrix products, arithmetic and copies ran while one was open for 5% of the time, Pallas kernels for 0%

commit v1 on v0

v1 whole, which is shorter than its diff:
```python
import jax
import jax.numpy as jnp
from jax import lax
from jax.sharding import Mesh, PartitionSpec as P

ROWS = 320
AXES = ("z", "x", "y", "c")
SIZES = (8, 4, 8, 2)
f32 = jnp.float32
bf16 = jnp.bfloat16


def shifted(value, steps, sources=None):
    count = 512
    sources = range(count) if sources is None else sources
    return lax.ppermute(value, AXES, [(s, (s + steps) % count) for s in sources])


def swapped(value):
    return lax.ppermute(value, "c", [(0, 1), (1, 0)])


def inverse_norm(values):
    return lax.rsqrt(jnp.sum(values * values, axis=-1, keepdims=True) + 1e-06)


def exchange(value, axes):
    return lax.all_to_all(value, axes, 0, 0)


def spread(value, axes, count):
    return exchange(jnp.broadcast_to(value, (count,) + value.shape), axes)


def total(value):
    return jnp.sum(value.astype(f32), axis=0)


def embed(images, head):
    proj = jnp.dot(images, head, preferred_element_type=f32)
    inv = inverse_norm(proj)
    normed = proj * inv
    return normed, inv, normed.astype(bf16)


def dot_t(a, b):
    return lax.dot_general(a, b, (((1,), (1,)), ((), ())), preferred_element_type=f32)


def t_dot(a, b):
    return lax.dot_general(a, b, (((0,), (0,)), ((), ())), preferred_element_type=f32)


def tangent(grad, normed, inv):
    return (grad - normed * jnp.sum(normed * grad, axis=-1, keepdims=True)) * inv


def reduce_head(images_t, d_proj, core):
    rows = images_t.shape[0] // 2
    width = d_proj.shape[1]
    theirs = lax.dynamic_slice_in_dim(images_t, (1 - core) * rows, rows, 0)
    mine = lax.dynamic_slice_in_dim(images_t, core * rows, rows, 0)
    sent = jnp.dot(theirs, d_proj, preferred_element_type=f32).astype(bf16)
    got = swapped(sent)
    part = jnp.dot(mine, d_proj, preferred_element_type=f32)
    part = (part + got.astype(f32)).astype(bf16)
    part = total(exchange(part.reshape(4, rows // 4, width), "x")).astype(bf16)
    tiles = part.reshape(9, 16, 5, 128).transpose(0, 2, 1, 3).reshape(45, 16, 128)
    tiles = jnp.pad(tiles, ((0, 19), (0, 0), (0, 0)))
    factor = 1.0 / jnp.sqrt(jnp.float32(ROWS))
    tile = (total(exchange(tiles, ("z", "y"))) * factor).astype(bf16)
    tiles = spread(tile, ("z", "y"), 64)[:45]
    part = tiles.reshape(9, 5, 16, 128).transpose(0, 2, 1, 3).reshape(rows // 4, width)
    part = spread(part, "x", 4).reshape(rows, width)
    return spread(part, "c", 2).reshape(2 * rows, width)


def shards(images, texts, head, log_scale, bias):
    temper = jnp.exp(log_scale[0])
    offset = bias[0]
    core = lax.axis_index("c")
    texts_prev = shifted(texts, 2)
    images_other = swapped(images)
    images_next = shifted(images, -1, range(0, 512, 2))

    stack = jnp.concatenate([images, images_other, images_next], 0)
    img_n, img_inv, img_b = embed(stack, head)
    images_t = stack.T

    def text(values):
        values = values.astype(f32)
        inv = inverse_norm(values)
        normed = values * inv
        return normed, inv, normed.astype(bf16)

    txt_n, txt_inv, txt_b = text(texts)
    prev_b = text(texts_prev)[2]

    near = 2 * ROWS
    row = lax.broadcasted_iota(jnp.int32, (near, ROWS), 0)
    col = lax.broadcasted_iota(jnp.int32, (near, ROWS), 1)
    target = (row == col).astype(f32)
    keep = jnp.where((row < ROWS) | (core == 0), 1.0, 0.0)
    logit = temper * dot_t(img_b[:near], txt_b) + offset
    slope = (temper * (jax.nn.sigmoid(logit) - target) * keep).astype(bf16)
    logit_prev = temper * dot_t(img_b, prev_b) + offset
    row3 = lax.broadcasted_iota(jnp.int32, (3 * ROWS, ROWS), 0)
    keep3 = jnp.where((row3 < near) | (core == 1), 1.0, 0.0)
    slope_prev = (temper * jax.nn.sigmoid(logit_prev) * keep3).astype(bf16)

    d_near = jnp.dot(slope, txt_b, preferred_element_type=f32)
    d_img = jnp.dot(slope_prev, prev_b, preferred_element_type=f32)
    d_img = d_img + jnp.pad(d_near, ((0, ROWS), (0, 0)))
    d_proj = tangent(d_img, img_n, img_inv).astype(bf16)
    grad_head = reduce_head(images_t, d_proj, core)

    d_txt = t_dot(slope, img_b[:near])
    d_txt_prev = t_dot(slope_prev, img_b)
    d_txt = d_txt + shifted(d_txt_prev, -2)
    grad_text = tangent(d_txt, txt_n, txt_inv).astype(bf16)

    d_own = d_img[:ROWS] + swapped(d_img[ROWS:near]) + shifted(d_img[near:], 1, range(1, 512, 2))
    d_own_proj = tangent(d_own, img_n[:ROWS], img_inv[:ROWS]).astype(bf16)
    grad_image = dot_t(d_own_proj, head).astype(bf16)
    return (grad_image, grad_text, grad_head)


def solution(mesh):
    grid = Mesh(mesh.devices.reshape(SIZES), AXES)
    in_specs = (P(AXES, None), P(AXES, None), P(), P(), P())
    out_specs = (P(AXES, None), P(AXES, None), P())
    return jax.shard_map(shards, mesh=grid, in_specs=in_specs, out_specs=out_specs, check_vma=False)
```

time: 362 us -> 148 us (0.41)
  waiting for transfers between devices: 290 us -> 26.6 us
  starting transfers between devices: 29.2 us -> 54.7 us
  blocking collectives: 0 us -> 18.8 us
  between operations: 15.6 us -> 2.3 us
  local copies, waits for them, and re-layouts: 3.02 us -> 15.8 us
  matrix products: 12.4 us -> 21.1 us
    psum x1 -> x0, waiting for transfers between devices: 257 us -> none  [shards(): head_total = lax.psum(head_part, 'dp')]
    ppermute x7, waiting for transfers between devices: 32.9 us -> 11.6 us  [the longest x4 9.42 us: shifted(): lax.ppermute(value, AXES, [(s, (s + steps) % count) for s in sources])]
    all_to_all x0 -> x2, blocking collectives: none -> 18.8 us  [exchange(): return lax.all_to_all(value, axes, 0, 0)]
    all_to_all x0 -> x3, starting transfers between devices: none -> 18.3 us  [exchange(): return lax.all_to_all(value, axes, 0, 0)]
    all_to_all x0 -> x3, waiting for transfers between devices: none -> 15 us  [exchange(): return lax.all_to_all(value, axes, 0, 0)]
    dot_general x15 -> x10, matrix products: 12.4 us -> 21.1 us  [the longest x3 5.15 us: dot_t(): lax.dot_general(a, b, (((1,), (1,)), ((), ())), preferred_element_type=f32)]
    ppermute x7, starting transfers between devices: 29.1 us -> 36.4 us  [the longest x3 23.9 us: swapped(): return lax.ppermute(value, 'c', [(0, 1), (1, 0)])]
    unnamed x7 -> x26, local copies, waits for them, and re-layouts: 3.02 us -> 7.17 us
  transfers between devices with their start and end apart: 8 -> 10, of which waited for: 4 -> 4; matrix products, arithmetic and copies ran while one was open for 5% -> 14% of each run, Pallas kernels for 0% -> 0%
where the time goes in v1:
time: 148 us; the launch traced here: 147 us
  starting transfers between devices  54.7 us (37%)
  waiting for transfers between devices  26.6 us (18%)
  matrix products  21.1 us (14%)
  blocking collectives  18.8 us (13%)
  local copies, waits for them, and re-layouts  15.8 us (11%)
  other arithmetic  8.18 us (6%)
  between operations  2.3 us (2%)
    ppermute x3, starting transfers between devices, swapped(): return lax.ppermute(value, 'c', [(0, 1), (1, 0)])  23.9 us
    all_to_all x2, blocking collectives, exchange(): return lax.all_to_all(value, axes, 0, 0)  18.8 us
    all_to_all x3, starting transfers between devices, exchange(): return lax.all_to_all(value, axes, 0, 0)  18.3 us
    all_to_all x3, waiting for transfers between devices, exchange(): return lax.all_to_all(value, axes, 0, 0)  15 us
    ppermute x4, starting transfers between devices, shifted(): lax.ppermute(value, AXES, [(s, (s + steps) % count) for s in sources])  12.5 us
    ppermute x4, waiting for transfers between devices, shifted(): lax.ppermute(value, AXES, [(s, (s + steps) % count) for s in sources])  9.42 us
    unnamed x26, local copies, waits for them, and re-layouts  7.17 us
    dot_general x3, matrix products, dot_t(): lax.dot_general(a, b, (((1,), (1,)), ((), ())), preferred_element_type=f32)  5.15 us
  transfers between devices with their start and end apart: 10, of which 4 were waited for; matrix products, arithmetic and copies ran while one was open for 14% of the time, Pallas kernels for 0%

profile of v1, /device:TPU:1, one launch (start us, length us, event | category | flops | bytes accessed | tf_op | source)
XLA Modules:
  0.0 147.5 jit_solution(8360721292615383630)
XLA Ops:
  0.6 0.0 copy-start
  0.6 8.9 %collective-permute-start = (bf16[320,1152]{1,0:T(8,128)(2,1)}, bf16[320,1152]{1,0:T(8,128)(2,1)S(1)}, u32[]{:S(2)}, u32[]{:S(2)}) collective-permute-start(bf16[320,1152]{1,0:T(8,128)(2,1)} %param.5), channel_id=1, source_target_pairs={{0,1},{1,0},{2,3},{3,2},{4,5},{5,4},{6,7},{7,6},{8,9},{9,8},{10,11... | collective-permute-start | bytes 2211848 | tf_op jit(solution)/shard_map/ppermute | solution.py:20
  9.6 1.3 collective-permute-start.1
  10.9 1.9 %collective-permute-start.2 = (bf16[320,640]{1,0:T(8,128)(2,1)}, bf16[320,640]{1,0:T(8,128)(2,1)S(1)}, u32[]{:S(2)}, u32[]{:S(2)}) collective-permute-start(bf16[320,640]{1,0:T(8,128)(2,1)} %param.6), channel_id=1, source_target_pairs={{0,2},{1,3},{2,4},{3,5},{4,6},{5,7},{6,8},{7,9},{8,10},{9,11},{10,... | collective-permute-start | bytes 1228808 | tf_op jit(solution)/shard_map/ppermute | solution.py:16
  12.8 1.2 fusion.28
  14.0 2.0 %constant_dynamic-update-slice_fusion.2 = bf16[960,1152]{1,0:T(8,128)(2,1)} fusion(bf16[320,1152]{1,0:T(8,128)(2,1)} %param.5), kind=kLoop, calls=%fused_computation.58 | loop fusion | bytes 1474560
  17.4 9.4 %collective-permute-done.2 = bf16[320,640]{1,0:T(8,128)(2,1)S(1)} collective-permute-done((bf16[320,640]{1,0:T(8,128)(2,1)}, bf16[320,640]{1,0:T(8,128)(2,1)S(1)}, u32[]{:S(2)}, u32[]{:S(2)}) %collective-permute-start.2) | collective-permute-done | bytes 409632 | tf_op jit(solution)/shard_map/ppermute | solution.py:16
  26.8 0.2 fusion.22
  27.0 0.0 collective-permute-done
  27.0 0.9 constant_dynamic-update-slice_fusion.1
  27.9 0.0 collective-permute-done.1
  27.9 0.9 constant_dynamic-update-slice_fusion
  28.9 3.8 %multiply_reduce_fusion.1 = (f32[960]{0:T(1024)S(1)}, f32[960,640]{1,0:T(8,128)S(1)}) fusion(bf16[960,1152]{1,0:T(8,128)(2,1)} %constant_dynamic-update-slice_fusion, bf16[1152,640]{1,0:T(8,128)(2,1)S(1)} %copy-done), kind=kOutput, calls=%fused_computation.4 | convolution fusion | flops 1416805376 | bytes 6147840 | tf_op jit(solution)/shard_map/dot_general | solution.py:40
  32.7 0.0 copy-start.10
  32.7 0.0 copy-start.4
  32.7 0.3 fusion.46
  33.0 0.0 copy-start.1
  33.0 0.7 copy-done.4
  33.7 0.6 fusion.16
  34.3 0.0 copy-start.6
  34.3 0.7 fusion.36
  35.1 0.2 copy-done.6
  35.3 0.9 fusion.7
  36.2 1.2 multiply_reduce_fusion
  37.4 0.0 copy-done.8
  37.5 0.4 multiply_convert_fusion
  37.9 1.0 copy-done.2
  38.9 1.1 copy-done.9
  40.0 2.3 %convolution_convert_fusion.1 = bf16[576,640]{1,0:T(8,128)(2,1)} fusion(bf16[960,640]{1,0:T(8,128)(2,1)S(1)} %multiply_convert_fusion, bf16[960,1152]{1,0:T(8,128)(2,1)S(1)} %copy-done.9, s32[]{:T(128)S(6)} %select_n.19), kind=kOutput, calls=%fused_computation.14 | convolution fusion | flops 708157440 | bytes 3194884 | tf_op jit(solution)/shard_map/dot_general | solution.py:63
  42.3 11.0 %collective-permute-start.6 = (bf16[576,640]{1,0:T(8,128)(2,1)}, bf16[576,640]{1,0:T(8,128)(2,1)}, u32[]{:S(2)}, u32[]{:S(2)}) collective-permute-start(bf16[576,640]{1,0:T(8,128)(2,1)} %convolution_convert_fusion.1), channel_id=1, source_target_pairs={{0,1},{1,0},{2,3},{3,2},{4,5},{5,4},{6,7},{7,6},{8,9},{9,8},{10,11... | collective-permute-start | bytes 2211848 | tf_op jit(solution)/shard_map/ppermute | solution.py:20
  53.3 2.2 %collective-permute-done.6 = bf16[576,640]{1,0:T(8,128)(2,1)} collective-permute-done((bf16[576,640]{1,0:T(8,128)(2,1)}, bf16[576,640]{1,0:T(8,128)(2,1)}, u32[]{:S(2)}, u32[]{:S(2)}) %collective-permute-start.6) | collective-permute-done | bytes 737312 | tf_op jit(solution)/shard_map/ppermute | solution.py:20
  55.5 3.3 %add_convert_fusion = bf16[576,640]{1,0:T(8,128)(2,1)S(1)} fusion(bf16[576,640]{1,0:T(8,128)(2,1)} %collective-permute-done.6, bf16[960,640]{1,0:T(8,128)(2,1)} %copy-done.7, bf16[960,1152]{1,0:T(8,128)(2,1)} %constant_dynamic-update-slice_fusion, s32[]{:T(128)S(6)} %select_n.18), kind=kOutput, calls=%fused_computation.5 | convolution fusion | flops 708894720 | bytes 3932164 | tf_op jit(solution)/shard_map/dot_general | solution.py:65
  58.8 14.2 %all_to_all.25 = bf16[4,144,640]{2,1,0:T(8,128)(2,1)} all-to-all(bf16[4,144,640]{2,1,0:T(8,128)(2,1)S(1)} %bitcast.33), channel_id=1, replica_groups=mesh['z'=8,'x'=4,'y'=8,'c'=2] {'x'}, dimensions={0} | all-to-all | bytes 1474560 | tf_op jit(solution)/shard_map/all_to_all | solution.py:28
  73.0 1.9 %reduce_sum.81 = bf16[144,640]{1,0:T(8,128)(2,1)} reduce(bf16[4,144,640]{2,1,0:T(8,128)(2,1)} %all_to_all.25, bf16[]{:T(256)} %constant.11.clone.1), dimensions={0}, to_apply=%region_6.7 | reduce | flops 276480 | bytes 921602 | tf_op jit(solution)/shard_map/reduce_sum | solution.py:36
  75.0 1.9 %reshape.61 = bf16[9,16,5,128]{3,2,1,0:T(8,128)(2,1)} reshape(bf16[144,640]{1,0:T(8,128)(2,1)} %reduce_sum.81) | data formatting | bytes 368640 | tf_op jit(solution)/shard_map/reshape | solution.py:68
  76.8 1.0 copy.8
  77.8 0.7 pad.9
  78.6 5.5 %all-to-all-start.1 = ((bf16[64,16,128]{2,1,0:T(8,128)(2,1)}), bf16[64,16,128]{2,1,0:T(8,128)(2,1)}, u32[]{:S(2)}, u32[]{:S(2)}) async-start(bf16[64,16,128]{2,1,0:T(8,128)(2,1)} %pad.9), calls=%async_computation.1 | async-start | bytes 524288 | tf_op jit(solution)/shard_map/all_to_all | solution.py:28
  84.1 2.8 %fusion.48 = f32[320,640]{1,0:T(8,128)} fusion(bf16[960,320]{0,1:T(8,128)(2,1)} %copy-done.8, bf16[960,640]{1,0:T(8,128)(2,1)S(1)} %get-tuple-element.3), kind=kOutput, calls=%fused_computation.73 | convolution fusion | flops 393216000 | bytes 2662400 | tf_op jit(solution)/shard_map/dot_general | solution.py:51
  86.9 7.1 %collective-permute-start.5 = (f32[320,640]{1,0:T(8,128)}, f32[320,640]{1,0:T(8,128)}, u32[]{:S(2)}, u32[]{:S(2)}) collective-permute-start(f32[320,640]{1,0:T(8,128)} %fusion.48), channel_id=1, source_target_pairs={{0,510},{1,511},{2,0},{3,1},{4,2},{5,3},{6,4},{7,5},{8,6},{9,7},{1... | collective-permute-start | bytes 2457608 | tf_op jit(solution)/shard_map/ppermute | solution.py:16
  94.0 1.3 fusion.47
  95.3 4.0 %collective-permute-start.3 = (f32[320,640]{1,0:T(8,128)}, f32[320,640]{1,0:T(8,128)}, u32[]{:S(2)}, u32[]{:S(2)}) collective-permute-start(f32[320,640]{1,0:T(8,128)} %get-tuple-element.5), channel_id=1, source_target_pairs={{0,1},{1,0},{2,3},{3,2},{4,5},{5,4},{6,7},{7,6},{8,9},{9,8},{10,11... | collective-permute-start | bytes 2457608 | tf_op jit(solution)/shard_map/ppermute | solution.py:20
  99.3 2.2 %collective-permute-start.4 = (f32[320,640]{1,0:T(8,128)}, f32[320,640]{1,0:T(8,128)}, u32[]{:S(2)}, u32[]{:S(2)}) collective-permute-start(f32[320,640]{1,0:T(8,128)} %get-tuple-element.6), channel_id=1, source_target_pairs={{1,2},{3,4},{5,6},{7,8},{9,10},{11,12},{13,14},{15,16},{17,18},{19... | collective-permute-start | bytes 2457608 | tf_op jit(solution)/shard_map/ppermute | solution.py:16
  101.5 0.0 all-to-all-done.1
  101.5 1.0 convert_reduce_fusion
  102.5 0.7 broadcast_in_dim.29
  103.3 9.3 %all-to-all-start.2 = ((bf16[64,16,128]{2,1,0:T(8,128)(2,1)}), bf16[64,16,128]{2,1,0:T(8,128)(2,1)}, u32[]{:S(2)}, u32[]{:S(2)}) async-start(bf16[64,16,128]{2,1,0:T(8,128)(2,1)} %broadcast_in_dim.29), calls=%async_computation.2 | async-start | bytes 524288 | tf_op jit(solution)/shard_map/all_to_all | solution.py:28
  112.6 0.0 collective-permute-done.5
  112.6 1.8 %fusion.24 = (f32[320]{0:T(512)S(1)}, f32[320,640]{1,0:T(8,128)S(1)}) fusion(bf16[320,640]{1,0:T(8,128)(2,1)S(1)} %copy-done.4, f32[320]{0:T(512)S(1)} %add_rsqrt_fusion.1, f32[320,640]{1,0:T(8,128)} %collective-permute-done.5, bf16[640,320]{0,1:T(8,128)(2,1)S(1)} %fusion.16, bf16[960,640]{1,0:T(8,128)(2,1)S(1)} %get-tuple-element.3), kind=kOutput, calls=%fused_computation.39 | convolution fusion | flops 263167680 | bytes 3280128 | tf_op jit(solution)/shard_map/dot_general | solution.py:51
  114.4 1.0 fusion.27
  115.4 10.4 %all-to-all-done.2 = bf16[64,16,128]{2,1,0:T(8,128)(2,1)} async-done(((bf16[64,16,128]{2,1,0:T(8,128)(2,1)}), bf16[64,16,128]{2,1,0:T(8,128)(2,1)}, u32[]{:S(2)}, u32[]{:S(2)}) %all-to-all-start.2) | async-done | bytes 262176 | tf_op jit(solution)/shard_map/all_to_all | solution.py:28
  125.8 0.9 slice.35
  126.7 0.1 copy.9
  126.9 0.9 broadcast_in_dim.30
  127.8 3.5 %all-to-all-start.3 = ((bf16[4,144,640]{2,1,0:T(8,128)(2,1)}), bf16[4,144,640]{2,1,0:T(8,128)(2,1)S(1)}, u32[]{:S(2)}, u32[]{:S(2)}) async-start(bf16[4,144,640]{2,1,0:T(8,128)(2,1)} %broadcast_in_dim.30), calls=%async_computation.3 | async-start | bytes 1474560 | tf_op jit(solution)/shard_map/all_to_all | solution.py:28
  131.3 0.0 slice-start
  131.3 0.0 collective-permute-done.3
  131.3 0.0 collective-permute-done.4
  131.3 2.1 %multiply_reduce_fusion.2 = f32[320]{0:T(512)S(1)} fusion(f32[960,640]{1,0:T(8,128)} %copy-done.1, f32[320,640]{1,0:T(8,128)} %collective-permute-done.4, f32[320,640]{1,0:T(8,128)} %collective-permute-done.3, f32[960,640]{1,0:T(8,128)} %copy-done.2), kind=kLoop, calls=%fused_computation.47 | loop fusion | flops 818880 | bytes 3278080 | tf_op jit(solution)/shard_map/reduce_sum | solution.py:55
  133.5 3.6 %convolution_convert_fusion = bf16[320,1152]{1,0:T(8,128)(2,1)} fusion(bf16[1152,640]{1,0:T(8,128)(2,1)S(1)} %copy-done, f32[960,640]{1,0:T(8,128)} %copy-done.1, f32[320]{0:T(512)S(1)} %slice-done, f32[320]{0:T(512)S(1)} %multiply_reduce_fusion.2, f32[320,640]{1,0:T(8,128)} %collective-permute-done.4, f32[320,640]{1,0:T(8,128)} %collective-permute-done.3, ...), kind=kOutput, calls=%fused_computation | convolution fusion | flops 473456640 | bytes 5491200 | tf_op jit(solution)/shard_map/dot_general | solution.py:47
  137.1 4.6 %all-to-all-done.3 = bf16[4,144,640]{2,1,0:T(8,128)(2,1)S(1)} async-done(((bf16[4,144,640]{2,1,0:T(8,128)(2,1)}), bf16[4,144,640]{2,1,0:T(8,128)(2,1)S(1)}, u32[]{:S(2)}, u32[]{:S(2)}) %all-to-all-start.3) | async-done | bytes 737312 | tf_op jit(solution)/shard_map/all_to_all | solution.py:28
  141.7 0.1 broadcast_in_dim.31
  141.8 4.5 %all_to_all.26 = bf16[2,576,640]{2,1,0:T(8,128)(2,1)S(1)} all-to-all(bf16[2,576,640]{2,1,0:T(8,128)(2,1)S(1)} %broadcast_in_dim.31), channel_id=1, replica_groups=mesh['z'=8,'x'=4,'y'=8,'c'=2] {'c'}, dimensions={0} | all-to-all | bytes 2949120 | tf_op jit(solution)/shard_map/all_to_all | solution.py:28
  146.3 1.1 copy.18
  (20 shorter events, 0.1 us)
Async XLA Ops:
  0.6 28.3 %copy-start = (bf16[1152,640]{1,0:T(8,128)(2,1)S(1)}, bf16[1152,640]{1,0:T(8,128)(2,1)}, u32[]{:S(2)}) copy-start(bf16[1152,640]{1,0:T(8,128)(2,1)} %param.7) | copy-start | bytes 4423684
  0.6 26.4 %collective-permute-start = (bf16[320,1152]{1,0:T(8,128)(2,1)}, bf16[320,1152]{1,0:T(8,128)(2,1)S(1)}, u32[]{:S(2)}, u32[]{:S(2)}) collective-permute-start(bf16[320,1152]{1,0:T(8,128)(2,1)} %param.5), channel_id=1, source_target_pairs={{0,1},{1,0},{2,3},{3,2},{4,5},{5,4},{6,7},{7,6},{8,9},{9,8},{10,11... | collective-permute-start | bytes 2211848 | tf_op jit(solution)/shard_map/ppermute | solution.py:20
  9.6 18.4 %collective-permute-start.1 = (bf16[320,1152]{1,0:T(8,128)(2,1)}, bf16[320,1152]{1,0:T(8,128)(2,1)S(1)}, u32[]{:S(2)}, u32[]{:S(2)}) collective-permute-start(bf16[320,1152]{1,0:T(8,128)(2,1)} %param.5), channel_id=1, source_target_pairs={{0,511},{2,1},{4,3},{6,5},{8,7},{10,9},{12,11},{14,13},{16,15},{18... | collective-permute-start | bytes 2211848 | tf_op jit(solution)/shard_map/ppermute | solution.py:16
  10.9 15.9 %collective-permute-start.2 = (bf16[320,640]{1,0:T(8,128)(2,1)}, bf16[320,640]{1,0:T(8,128)(2,1)S(1)}, u32[]{:S(2)}, u32[]{:S(2)}) collective-permute-start(bf16[320,640]{1,0:T(8,128)(2,1)} %param.6), channel_id=1, source_target_pairs={{0,2},{1,3},{2,4},{3,5},{4,6},{5,7},{6,8},{7,9},{8,10},{9,11},{10,... | collective-permute-start | bytes 1228808 | tf_op jit(solution)/shard_map/ppermute | solution.py:16
  26.8 2.1 %copy-start.5 = (bf16[320,640]{1,0:T(8,128)(2,1)}, bf16[320,640]{1,0:T(8,128)(2,1)S(1)}, u32[]{:S(2)}) copy-start(bf16[320,640]{1,0:T(8,128)(2,1)S(1)} %collective-permute-done.2) | copy-start | bytes 1228804
  32.7 61.3 %copy-start.10 = (f32[960]{0:T(1024)}, f32[960]{0:T(1024)S(1)}, u32[]{:S(2)}) copy-start(f32[960]{0:T(1024)S(1)} %add_rsqrt_fusion) | copy-start | bytes 11524
  32.7 1.0 copy-start.4
  33.0 4.5 %copy-start.1 = (f32[960,640]{1,0:T(8,128)}, f32[960,640]{1,0:T(8,128)S(1)}, u32[]{:S(2)}) copy-start(f32[960,640]{1,0:T(8,128)S(1)} %get-tuple-element.4) | copy-start | bytes 7372804
  34.3 1.0 copy-start.6
  36.2 1.2 copy-start.8
  37.4 1.4 copy-start.2
  37.5 2.5 %copy-start.9 = (bf16[960,1152]{1,0:T(8,128)(2,1)S(1)}, bf16[960,1152]{1,0:T(8,128)(2,1)}, u32[]{:S(2)}) copy-start(bf16[960,1152]{1,0:T(8,128)(2,1)} %constant_dynamic-update-slice_fusion) | copy-start | bytes 6635524
  40.0 2.3 %copy-start.7 = (bf16[960,640]{1,0:T(8,128)(2,1)}, bf16[960,640]{1,0:T(8,128)(2,1)S(1)}, u32[]{:S(2)}) copy-start(bf16[960,640]{1,0:T(8,128)(2,1)S(1)} %multiply_convert_fusion) | copy-start | bytes 3686404
  42.3 13.2 %collective-permute-start.6 = (bf16[576,640]{1,0:T(8,128)(2,1)}, bf16[576,640]{1,0:T(8,128)(2,1)}, u32[]{:S(2)}, u32[]{:S(2)}) collective-permute-start(bf16[576,640]{1,0:T(8,128)(2,1)} %convolution_convert_fusion.1), channel_id=1, source_target_pairs={{0,1},{1,0},{2,3},{3,2},{4,5},{5,4},{6,7},{7,6},{8,9},{9,8},{10,11... | collective-permute-start | bytes 2211848 | tf_op jit(solution)/shard_map/ppermute | solution.py:20
  78.6 22.9 %all-to-all-start.1 = ((bf16[64,16,128]{2,1,0:T(8,128)(2,1)}), bf16[64,16,128]{2,1,0:T(8,128)(2,1)}, u32[]{:S(2)}, u32[]{:S(2)}) async-start(bf16[64,16,128]{2,1,0:T(8,128)(2,1)} %pad.9), calls=%async_computation.1 | async-start | bytes 524288 | tf_op jit(solution)/shard_map/all_to_all | solution.py:28
  84.1 9.9 %copy-start.3 = (f32[960,640]{1,0:T(8,128)S(1)}, f32[960,640]{1,0:T(8,128)}, u32[]{:S(2)}) copy-start(f32[960,640]{1,0:T(8,128)} %copy-done.2) | copy-start | bytes 7372804
  86.9 25.7 %collective-permute-start.5 = (f32[320,640]{1,0:T(8,128)}, f32[320,640]{1,0:T(8,128)}, u32[]{:S(2)}, u32[]{:S(2)}) collective-permute-start(f32[320,640]{1,0:T(8,128)} %fusion.48), channel_id=1, source_target_pairs={{0,510},{1,511},{2,0},{3,1},{4,2},{5,3},{6,4},{7,5},{8,6},{9,7},{1... | collective-permute-start | bytes 2457608 | tf_op jit(solution)/shard_map/ppermute | solution.py:16
  95.3 36.0 %collective-permute-start.3 = (f32[320,640]{1,0:T(8,128)}, f32[320,640]{1,0:T(8,128)}, u32[]{:S(2)}, u32[]{:S(2)}) collective-permute-start(f32[320,640]{1,0:T(8,128)} %get-tuple-element.5), channel_id=1, source_target_pairs={{0,1},{1,0},{2,3},{3,2},{4,5},{5,4},{6,7},{7,6},{8,9},{9,8},{10,11... | collective-permute-start | bytes 2457608 | tf_op jit(solution)/shard_map/ppermute | solution.py:20
  99.3 32.0 %collective-permute-start.4 = (f32[320,640]{1,0:T(8,128)}, f32[320,640]{1,0:T(8,128)}, u32[]{:S(2)}, u32[]{:S(2)}) collective-permute-start(f32[320,640]{1,0:T(8,128)} %get-tuple-element.6), channel_id=1, source_target_pairs={{1,2},{3,4},{5,6},{7,8},{9,10},{11,12},{13,14},{15,16},{17,18},{19... | collective-permute-start | bytes 2457608 | tf_op jit(solution)/shard_map/ppermute | solution.py:16
  103.3 22.5 %all-to-all-start.2 = ((bf16[64,16,128]{2,1,0:T(8,128)(2,1)}), bf16[64,16,128]{2,1,0:T(8,128)(2,1)}, u32[]{:S(2)}, u32[]{:S(2)}) async-start(bf16[64,16,128]{2,1,0:T(8,128)(2,1)} %broadcast_in_dim.29), calls=%async_computation.2 | async-start | bytes 524288 | tf_op jit(solution)/shard_map/all_to_all | solution.py:28
  127.8 13.9 %all-to-all-start.3 = ((bf16[4,144,640]{2,1,0:T(8,128)(2,1)}), bf16[4,144,640]{2,1,0:T(8,128)(2,1)S(1)}, u32[]{:S(2)}, u32[]{:S(2)}) async-start(bf16[4,144,640]{2,1,0:T(8,128)(2,1)} %broadcast_in_dim.30), calls=%async_computation.3 | async-start | bytes 1474560 | tf_op jit(solution)/shard_map/all_to_all | solution.py:28
  131.3 2.2 %slice-start = ((f32[960]{0:T(1024)}), f32[320]{0:T(512)S(1)}, s32[]{:S(2)}) async-start(f32[960]{0:T(1024)} %copy-done.10), calls=%async_computation.5 | async-start | bytes 4096 | tf_op jit(solution)/shard_map/slice | solution.py:123

commit v2 on v1

v2 whole, which is shorter than its diff:
```python
import jax
import jax.numpy as jnp
from jax import lax
from jax.experimental import pallas as pl
from jax.experimental.pallas import tpu as pltpu
from jax.sharding import Mesh, PartitionSpec as P

ROWS = 320
NEAR = 2 * ROWS
ALL = 3 * ROWS
D = 1152
E = 640
HALF = D // 2
AXES = ("zh", "zl", "x", "yh", "yl", "c")
SIZES = (4, 2, 4, 4, 2, 2)
CUBE = ("zl", "x", "yl")
GRID = ("zh", "yh")
SIDE = 16
TILES = 12
COUNT = 512
f32 = jnp.float32
bf16 = jnp.bfloat16


def shifted(value, steps, sources=None):
    sources = range(COUNT) if sources is None else sources
    return lax.ppermute(value, AXES, [(s, (s + steps) % COUNT) for s in sources])


def swapped(value):
    return lax.ppermute(value, "c", [(0, 1), (1, 0)])


def exchange(value, axes):
    return lax.all_to_all(value, axes, 0, 0)


VMEM = pl.BlockSpec(memory_space=pltpu.VMEM)
SMEM = pl.BlockSpec(memory_space=pltpu.SMEM)


def call(body, name, ins, outs, scratch=(), flops=0, after=(), mark=False):
    size = sum(a.size * a.dtype.itemsize for s, a in ins if s is not SMEM)
    if mark:
        outs = (*outs, (SMEM, (1,), jnp.int32))
    n_in, n_after, n_out = len(ins), len(after), len(outs)

    def run(*refs):
        refs = list(refs)
        if mark:
            refs.pop(n_in + n_after + n_out - 1)[0] = 0
        body(*refs[:n_in], *refs[n_in + n_after :])

    got = pl.pallas_call(
        run,
        out_shape=tuple(jax.ShapeDtypeStruct(dims, dtype) for _, dims, dtype in outs),
        in_specs=[s for s, _ in ins] + [SMEM] * n_after,
        out_specs=tuple(s for s, _, _ in outs),
        scratch_shapes=list(scratch),
        compiler_params=pltpu.CompilerParams(vmem_limit_bytes=16_000_000),
        cost_estimate=pl.CostEstimate(flops=flops, bytes_accessed=size, transcendentals=0),
        name=name,
    )(*(a for _, a in ins), *after)
    return got[0] if len(outs) == 1 else got


def dot(a, b):
    return jnp.dot(a, b, preferred_element_type=f32)


def dot_t(a, b):
    return lax.dot_general(a, b, (((1,), (1,)), ((), ())), preferred_element_type=f32)


def t_dot(a, b):
    return lax.dot_general(a, b, (((0,), (0,)), ((), ())), preferred_element_type=f32)


def normalize(values):
    inv = lax.rsqrt(jnp.sum(values * values, axis=-1, keepdims=True) + 1e-06)
    return values * inv, inv


def tangent(grad, normed, inv):
    return (grad - normed * jnp.sum(normed * grad, axis=-1, keepdims=True)) * inv


def slope_of(img_b, txt_b, scal):
    return scal[0] * jax.nn.sigmoid(scal[0] * dot_t(img_b, txt_b) + scal[1])


def near_body(scal, core, images, other, texts, head, img_n, img_inv, img_b, d_near, d_txt, turned, im):
    im[0:ROWS, :] = images[...]
    im[ROWS:NEAR, :] = other[...]
    txt_b = normalize(texts[...].astype(f32))[0].astype(bf16)
    norm, inv = normalize(dot(im[...], head[...]))
    img_n[...] = norm
    img_inv[...] = inv
    img_b[...] = norm.astype(bf16)
    row = lax.broadcasted_iota(jnp.int32, (NEAR, ROWS), 0)
    col = lax.broadcasted_iota(jnp.int32, (NEAR, ROWS), 1)
    target = jnp.where(row == col, scal[0], 0.0)
    slope = slope_of(img_b[...], txt_b, scal) - target
    slope = jnp.where((row < ROWS) | (core[0] == 0), slope, 0.0).astype(bf16)
    d_near[...] = dot(slope, txt_b)
    d_txt[...] = t_dot(slope, img_b[...])
    turned[...] = im[...].T


def next_body(nxt, head, img_n, img_inv, img_b, turned):
    norm, inv = normalize(dot(nxt[...], head[...]))
    img_n[...] = norm
    img_inv[...] = inv
    img_b[...] = norm.astype(bf16)
    turned[...] = nxt[...].T


def prev_body(scal, core, texts, img_n, img_inv, img_b, d_near, turned, next_n, next_inv, next_b, turned_next,
              sent, d_proj, d_own, d_other, d_next, slope):
    text = normalize(texts[...].astype(f32))[0].astype(bf16)
    slope[0:NEAR, :] = slope_of(img_b[...], text, scal).astype(bf16)
    on_second = jnp.where(core[0] == 1, 1.0, 0.0)
    slope[NEAR:ALL, :] = (slope_of(next_b[...], text, scal) * on_second).astype(bf16)
    grad = dot(slope[0:NEAR, :], text) + d_near[...]
    d_own[...] = grad[0:ROWS]
    d_other[...] = grad[ROWS:NEAR]
    d_proj[0:NEAR, :] = tangent(grad, img_n[...], img_inv[...]).astype(bf16)
    grad = dot(slope[NEAR:ALL, :], text)
    d_next[...] = grad.astype(bf16)
    d_proj[NEAR:ALL, :] = tangent(grad, next_n[...], next_inv[...]).astype(bf16)
    rows = pl.ds(pl.multiple_of((1 - core[0]) * HALF, HALF), HALF)
    part = dot(turned[rows, :], d_proj[0:NEAR, :]) + dot(turned_next[rows, :], d_proj[NEAR:ALL, :])
    sent[...] = part.astype(bf16)


def half_body(core, d_proj, turned, turned_next, out):
    rows = pl.ds(pl.multiple_of(core[0] * HALF, HALF), HALF)
    out[...] = dot(turned[rows, :], d_proj[0:NEAR, :]) + dot(turned_next[rows, :], d_proj[NEAR:ALL, :])


def tiles_of():
    for tile in range(HALF // 16 * (E // 128)):
        r, c = divmod(tile, E // 128)
        p, t = divmod(tile, TILES)
        yield r * 16, slice(c * 128, c * 128 + 128), p, slice(t * 16, t * 16 + 16)


def add_body(mine, got, out):
    total = (mine[...] + got[...].astype(f32)).astype(bf16)
    for row, cols, p, rows in tiles_of():
        out[p, rows, :] = total[row : row + 16, cols]
    out[SIDE - 1] = jnp.zeros((TILES * 16, 128), bf16)


def back_body(slope, img_b, next_b, out):
    grad = t_dot(slope[0:NEAR, :], img_b[...]) + t_dot(slope[NEAR:ALL, :], next_b[...])
    out[...] = grad.astype(bf16)


def cube_sum_body(parts, out):
    total = jnp.sum(parts[...].astype(f32), axis=0).astype(bf16)
    for t in range(TILES):
        out[t] = total[t * 16 : t * 16 + 16]
    out[TILES:] = jnp.zeros((SIDE - TILES, 16, 128), bf16)


def grid_sum_body(tiles, out):
    total = jnp.sum(tiles[...].astype(f32), axis=0) * (1.0 / jnp.sqrt(f32(ROWS)))
    out[...] = jnp.broadcast_to(total.astype(bf16)[None], (SIDE, 16, 128))


def cube_spread_body(tiles, out):
    for t in range(TILES):
        out[:, t * 16 : t * 16 + 16, :] = jnp.broadcast_to(tiles[t][None], (SIDE, 16, 128))


def finish_body(d_own, got, late, images, head, d_txt, back, texts, image_out, text_out):
    norm, inv = normalize(dot(images[...], head[...]))
    d_proj = tangent(d_own[...] + got[...] + late[...].astype(f32), norm, inv).astype(bf16)
    image_out[...] = dot_t(d_proj, head[...]).astype(bf16)
    norm, inv = normalize(texts[...].astype(f32))
    text_out[...] = tangent(d_txt[...] + back[...].astype(f32), norm, inv).astype(bf16)


def halves_body(core, mine, got, out):
    first = core[0] * HALF
    second = HALF - first
    for row, cols, p, rows in tiles_of():
        out[pl.ds(pl.multiple_of(first + row, 16), 16), cols] = mine[p, rows, :]
        out[pl.ds(pl.multiple_of(second + row, 16), 16), cols] = got[p, rows, :]


def shards(images, texts, head, log_scale, bias):
    scal = jnp.concatenate([jnp.exp(log_scale), bias])
    core = lax.axis_index("c").astype(jnp.int32).reshape(1)
    other = swapped(images)
    nxt = shifted(images, -1, range(0, COUNT, 2))
    prev = shifted(texts, 2)

    block = (VMEM, (ROWS, E), f32)
    img_n, img_inv, img_b, d_near, d_txt, turned, mark = call(
        near_body, "near",
        ((SMEM, scal), (SMEM, core), (VMEM, images), (VMEM, other), (VMEM, texts), (VMEM, head)),
        ((VMEM, (NEAR, E), f32), (VMEM, (NEAR, 1), f32), (VMEM, (NEAR, E), bf16), (VMEM, (NEAR, E), f32),
         block, (VMEM, (D, NEAR), bf16)),
        (pltpu.VMEM((NEAR, D), bf16),), 1_730_000_000, mark=True)
    next_n, next_inv, next_b, turned_next = call(
        next_body, "next",
        ((VMEM, nxt), (VMEM, head)),
        (block, (VMEM, (ROWS, 1), f32), (VMEM, (ROWS, E), bf16), (VMEM, (D, ROWS), bf16)),
        flops=470_000_000, after=(mark,))
    sent, d_proj, d_own, d_other, d_next, slope = call(
        prev_body, "prev",
        ((SMEM, scal), (SMEM, core), (VMEM, prev), (VMEM, img_n), (VMEM, img_inv), (VMEM, img_b), (VMEM, d_near),
         (VMEM, turned), (VMEM, next_n), (VMEM, next_inv), (VMEM, next_b), (VMEM, turned_next)),
        ((VMEM, (HALF, E), bf16), (VMEM, (ALL, E), bf16), block, block, (VMEM, (ROWS, E), bf16), (VMEM, (ALL, ROWS), bf16)),
        flops=1_530_000_000)
    mine = call(
        half_body, "half",
        ((SMEM, core), (VMEM, d_proj), (VMEM, turned), (VMEM, turned_next)),
        ((VMEM, (HALF, E), f32),), flops=710_000_000)
    part, mark = call(
        add_body, "add", ((VMEM, mine), (VMEM, swapped(sent))), ((VMEM, (SIDE, TILES * 16, 128), bf16),), mark=True)
    d_prev, mark = call(
        back_body, "back", ((VMEM, slope), (VMEM, img_b), (VMEM, next_b)), ((VMEM, (ROWS, E), bf16),),
        flops=400_000_000, after=(mark,), mark=True)
    d_beside = swapped(d_other)
    d_late = shifted(d_next, 1, range(1, COUNT, 2))
    d_back = shifted(d_prev, -2)
    tiles = call(
        cube_sum_body, "cube_sum", ((VMEM, exchange(part, CUBE)),), ((VMEM, (SIDE, 16, 128), bf16),), after=(mark,))
    tiles, mark = call(
        grid_sum_body, "grid_sum", ((VMEM, exchange(tiles, GRID)),), ((VMEM, (SIDE, 16, 128), bf16),),
        flops=40_000_000_000, mark=True)
    grad_image, grad_text, mark = call(
        finish_body, "finish",
        ((VMEM, d_own), (VMEM, d_beside), (VMEM, d_late), (VMEM, images), (VMEM, head), (VMEM, d_txt),
         (VMEM, d_back), (VMEM, texts)),
        ((VMEM, (ROWS, D), bf16), (VMEM, (ROWS, E), bf16)), flops=960_000_000, after=(mark,), mark=True)
    part = call(
        cube_spread_body, "cube_spread", ((VMEM, exchange(tiles, GRID)),),
        ((VMEM, (SIDE, TILES * 16, 128), bf16),), after=(mark,))
    part = exchange(part, CUBE)
    grad_head = call(
        halves_body, "halves", ((SMEM, core), (VMEM, part), (VMEM, swapped(part))), ((VMEM, (D, E), bf16),))
    return (grad_image, grad_text, grad_head)


def solution(mesh):
    grid = Mesh(mesh.devices.reshape(SIZES), AXES)
    in_specs = (P(AXES, None), P(AXES, None), P(), P(), P())
    out_specs = (P(AXES, None), P(AXES, None), P())
    return jax.shard_map(shards, mesh=grid, in_specs=in_specs, out_specs=out_specs, check_vma=False)
```

time: 148 us -> 131 us (0.89)
  Pallas kernels: 0 us -> 23.9 us
  matrix products: 21.1 us -> 0 us
  waiting for transfers between devices: 26.6 us -> 18.1 us
  other arithmetic: 8.18 us -> 0.08 us
  starting transfers between devices: 54.7 us -> 61.9 us
  local copies, waits for them, and re-layouts: 15.8 us -> 9.97 us
  blocking collectives: 18.8 us -> 13.6 us
    pallas_call x0 -> x11, Pallas kernels: none -> 23.9 us  [call(): pl.pallas_call(run, out_shape=tuple((jax.ShapeDtypeStruct(dims, dtype) fo...]
    dot_general x10 -> x0, matrix products: 21.1 us -> none  [the longest x3 5.15 us: dot_t(): lax.dot_general(a, b, (((1,), (1,)), ((), ())), preferred_element_type=f32)]
    ppermute x4, waiting for transfers between devices: 9.42 us -> 1.57 us  [shifted(): lax.ppermute(value, AXES, [(s, (s + steps) % COUNT) for s in sources])]
    reduce_sum x5 -> x0, other arithmetic: 6.45 us -> none  [the longest x2 2.97 us: total(): return jnp.sum(value.astype(f32), axis=0)]
    all_to_all x2 -> x1, blocking collectives: 18.8 us -> 13.6 us  [exchange(): return lax.all_to_all(value, axes, 0, 0)]
    ppermute x4, starting transfers between devices: 12.5 us -> 16.4 us  [shifted(): lax.ppermute(value, AXES, [(s, (s + steps) % COUNT) for s in sources])]
    ppermute x3 -> x4, starting transfers between devices: 23.9 us -> 27 us  [swapped(): return lax.ppermute(value, 'c', [(0, 1), (1, 0)])]
    unnamed x26 -> x38, local copies, waits for them, and re-layouts: 7.17 us -> 9.97 us
  transfers between devices with their start and end apart: 10 -> 11, of which waited for: 4 -> 5; matrix products, arithmetic and copies ran while one was open for 14% -> 0% of each run, Pallas kernels for 0% -> 11%
where the time goes in v2:
time: 131 us; the launch traced here: 130 us
  starting transfers between devices  61.9 us (47%)
  Pallas kernels  23.9 us (18%)
  waiting for transfers between devices  18.1 us (14%)
  blocking collectives  13.6 us (10%)
  local copies, waits for them, and re-layouts  9.97 us (8%)
  between operations  2.34 us (2%)
    ppermute x4, starting transfers between devices, swapped(): return lax.ppermute(value, 'c', [(0, 1), (1, 0)])  27 us
    pallas_call x11, Pallas kernels, call(): pl.pallas_call(run, out_shape=tuple((jax.ShapeDtypeStruct(dims, dtype) fo...  23.9 us
    all_to_all x3, starting transfers between devices, exchange(): return lax.all_to_all(value, axes, 0, 0)  18.6 us
    ppermute x4, starting transfers between devices, shifted(): lax.ppermute(value, AXES, [(s, (s + steps) % COUNT) for s in sources])  16.4 us
    all_to_all x3, waiting for transfers between devices, exchange(): return lax.all_to_all(value, axes, 0, 0)  14.1 us
    all_to_all x1, blocking collectives, exchange(): return lax.all_to_all(value, axes, 0, 0)  13.6 us
    unnamed x38, local copies, waits for them, and re-layouts  9.97 us
  transfers between devices with their start and end apart: 11, of which 5 were waited for; matrix products, arithmetic and copies ran while one was open for 0% of the time, Pallas kernels for 11%

profile of v2, /device:TPU:1, one launch (start us, length us, event | category | flops | bytes accessed | tf_op | source)
XLA Modules:
  0.0 129.9 jit_solution(3221821342853612427)
XLA Ops:
  0.6 8.8 %collective-permute-start.1 = (bf16[320,1152]{1,0:T(8,128)(2,1)}, bf16[320,1152]{1,0:T(8,128)(2,1)S(1)}, u32[]{:S(2)}, u32[]{:S(2)}) collective-permute-start(bf16[320,1152]{1,0:T(8,128)(2,1)} %refs_3_.1), channel_id=1, source_target_pairs={{0,1},{1,0},{2,3},{3,2},{4,5},{5,4},{6,7},{7,6},{8,9},{9,8},{10,11... | collective-permute-start | bytes 2211848 | tf_op jit(solution)/shard_map/ppermute | solution.py:31
  9.4 1.3 collective-permute-start.2
  10.7 1.9 %collective-permute-start = (bf16[320,640]{1,0:T(8,128)(2,1)}, bf16[320,640]{1,0:T(8,128)(2,1)}, u32[]{:S(2)}, u32[]{:S(2)}) collective-permute-start(bf16[320,640]{1,0:T(8,128)(2,1)} %refs_7_.1), channel_id=1, source_target_pairs={{0,2},{1,3},{2,4},{3,5},{4,6},{5,7},{6,8},{7,9},{8,10},{9,11},{10,... | collective-permute-start | bytes 1228808 | tf_op jit(solution)/shard_map/ppermute | solution.py:27
  14.0 0.1 pad_maximum_fusion.refs_0_
  14.1 0.0 collective-permute-done.1.refs_3_
  14.1 0.9 copy-done.15
  14.9 1.4 %copy-done = bf16[1152,640]{1,0:T(8,128)(2,1)S(1)} copy-done((bf16[1152,640]{1,0:T(8,128)(2,1)S(1)}, bf16[1152,640]{1,0:T(8,128)(2,1)}, u32[]{:S(2)}) %copy-start) | copy-done | bytes 1474584
  16.3 1.1 copy-done.7
  17.4 1.0 copy-done.11
  18.4 1.1 copy-done.16
  19.5 4.0 %near.1 = (f32[640,640]{1,0:T(8,128)S(1)}, f32[640,1]{1,0:T(8,128)S(1)}, bf16[640,640]{1,0:T(8,128)(2,1)S(1)}, f32[640,640]{1,0:T(8,128)S(1)}, f32[320,640]{1,0:...) custom-call(f32[2]{0:T(128)S(1)} %pad_maximum_fusion.refs_0_, s32[1]{0:T(128)} %bitcast.refs_1_.refs_0_, ...), custom_call_target="tpu_custom_call" | custom-call | flops 1730000000 | bytes 3358720 | tf_op jit(solution)/shard_map/near/pallas_call | solution.py:54
  23.6 0.0 copy-start.2
  23.6 0.0 collective-permute-done.2.refs_0_
  23.6 0.0 copy-done.1
  23.6 1.6 %next.1 = (f32[320,640]{1,0:T(8,128)S(1)}, f32[320,1]{1,0:T(8,128)S(1)}, bf16[320,640]{1,0:T(8,128)(2,1)S(1)}, bf16[1152,320]{1,0:T(8,128)(2,1)S(1)}) custom-call(bf16[320,1152]{1,0:T(8,128)(2,1)S(1)} %collective-permute-done.2.refs_0_, bf16[1152,640]{1,0:T(8,128)(2,1)S(1)} %copy-done.1, s32[1]{0:T(128)} %get-tuple-element.34.refs_2_), custom_call_target="tpu_custom_call" | custom-call | flops 470000000 | bytes 2211840 | tf_op jit(solution)/shard_map/next/pallas_call | solution.py:54
  25.2 1.6 %collective-permute-done.refs_2_ = bf16[320,640]{1,0:T(8,128)(2,1)} collective-permute-done((bf16[320,640]{1,0:T(8,128)(2,1)}, bf16[320,640]{1,0:T(8,128)(2,1)}, u32[]{:S(2)}, u32[]{:S(2)}) %collective-permute-start) | collective-permute-done | bytes 409632 | tf_op jit(solution)/shard_map/ppermute | solution.py:27
  26.8 4.3 %prev.1 = (bf16[576,640]{1,0:T(8,128)(2,1)S(1)}, bf16[960,640]{1,0:T(8,128)(2,1)S(1)}, f32[320,640]{1,0:T(8,128)S(1)}, f32[320,640]{1,0:T(8,128)S(1)}, bf16[320,...) custom-call(f32[2]{0:T(128)S(1)} %pad_maximum_fusion.refs_0_, s32[1]{0:T(128)} %bitcast.refs_1_.refs_0_, ...), custom_call_target="tpu_custom_call" | custom-call | flops 1530000000 | bytes 7950080 | tf_op jit(solution)/shard_map/prev/pallas_call | solution.py:54
  31.0 0.0 copy-done.2
  31.1 0.0 copy-start.4
  31.1 0.0 copy-start.9
  31.1 0.0 copy-start.14
  31.1 0.0 copy-start.17
  31.1 11.0 %collective-permute-start.5 = (bf16[576,640]{1,0:T(8,128)(2,1)S(1)}, bf16[576,640]{1,0:T(8,128)(2,1)S(1)}, u32[]{:S(2)}, u32[]{:S(2)}) collective-permute-start(bf16[576,640]{1,0:T(8,128)(2,1)S(1)} %get-tuple-element.45), channel_id=1, source_target_pairs={{0,1},{1,0},{2,3},{3,2},{4,5},{5,4},{6,7},{7,6},{8,9},{9,8},{10,11... | collective-permute-start | bytes 2211848 | tf_op jit(solution)/shard_map/ppermute | solution.py:31
  42.1 1.2 half.1.refs_0_
  43.4 0.0 copy-done.4
  43.4 0.0 copy-done.9
  43.4 0.0 copy-done.14
  43.4 0.0 copy-done.17
  43.4 0.5 collective-permute-done.5.refs_1_
  43.9 0.6 add.1
  44.5 0.0 copy-start.6
  44.6 0.9 copy-done.6
  45.4 3.6 %all-to-all-start = ((bf16[16,192,128]{2,1,0:T(8,128)(2,1)}), bf16[16,192,128]{2,1,0:T(8,128)(2,1)S(1)}, u32[]{:S(2)}, u32[]{:S(2)}) async-start(bf16[16,192,128]{2,1,0:T(8,128)(2,1)} %copy-done.6), calls=%async_computation | async-start | bytes 1572864 | tf_op jit(solution)/shard_map/all_to_all | solution.py:35
  49.0 0.0 copy-start.10
  49.1 1.1 copy-done.10
  50.2 1.5 %back.1 = (bf16[320,640]{1,0:T(8,128)(2,1)S(1)}, s32[1]{0:T(128)}) custom-call(bf16[960,320]{1,0:T(8,128)(2,1)S(1)} %copy-done.10, bf16[640,640]{1,0:T(8,128)(2,1)S(1)} %get-tuple-element.31.refs_5_.refs_1_, bf16[320,640]{1,0:T(8,128)(2,1)S(1)} %get-tuple-element.37.refs_10_.refs_2_, s32[1]{0:T(128)} %get-tuple-element.46.refs_3_), custom_call_target="tpu_custom_call" | custom-call | flops 400000000 | bytes 1843200 | tf_op jit(solution)/shard_map/back/pallas_call | solution.py:54
  51.7 0.0 copy-start.18
  51.7 0.7 copy-done.18
  52.4 8.9 %all-to-all-done.refs_0_ = bf16[16,192,128]{2,1,0:T(8,128)(2,1)S(1)} async-done(((bf16[16,192,128]{2,1,0:T(8,128)(2,1)}), bf16[16,192,128]{2,1,0:T(8,128)(2,1)S(1)}, u32[]{:S(2)}, u32[]{:S(2)}) %all-to-all-start) | async-done | bytes 786464 | tf_op jit(solution)/shard_map/all_to_all | solution.py:35
  61.3 1.3 cube_sum.1
  62.6 7.4 %all-to-all-start.1 = ((bf16[16,16,128]{2,1,0:T(8,128)(2,1)}), bf16[16,16,128]{2,1,0:T(8,128)(2,1)}, u32[]{:S(2)}, u32[]{:S(2)}) async-start(bf16[16,16,128]{2,1,0:T(8,128)(2,1)} %cube_sum.1), calls=%async_computation.1 | async-start | bytes 131072 | tf_op jit(solution)/shard_map/all_to_all | solution.py:35
  70.0 5.4 %collective-permute-start.4 = (bf16[320,640]{1,0:T(8,128)(2,1)}, bf16[320,640]{1,0:T(8,128)(2,1)}, u32[]{:S(2)}, u32[]{:S(2)}) collective-permute-start(bf16[320,640]{1,0:T(8,128)(2,1)} %copy-done.17), channel_id=1, source_target_pairs={{1,2},{3,4},{5,6},{7,8},{9,10},{11,12},{13,14},{15,16},{17,18},{19... | collective-permute-start | bytes 1228808 | tf_op jit(solution)/shard_map/ppermute | solution.py:27
  75.5 1.9 %collective-permute-start.3 = (f32[320,640]{1,0:T(8,128)}, f32[320,640]{1,0:T(8,128)}, u32[]{:S(2)}, u32[]{:S(2)}) collective-permute-start(f32[320,640]{1,0:T(8,128)} %copy-done.14), channel_id=1, source_target_pairs={{0,1},{1,0},{2,3},{3,2},{4,5},{5,4},{6,7},{7,6},{8,9},{9,8},{10,11... | collective-permute-start | bytes 2457608 | tf_op jit(solution)/shard_map/ppermute | solution.py:31
  77.4 0.0 copy-start.3
  77.4 0.0 copy-start.5
  77.4 0.0 copy-start.12
  77.4 7.8 %collective-permute-start.6 = (bf16[320,640]{1,0:T(8,128)(2,1)}, bf16[320,640]{1,0:T(8,128)(2,1)}, u32[]{:S(2)}, u32[]{:S(2)}) collective-permute-start(bf16[320,640]{1,0:T(8,128)(2,1)} %copy-done.18), channel_id=1, source_target_pairs={{0,510},{1,511},{2,0},{3,1},{4,2},{5,3},{6,4},{7,5},{8,6},{9,7},{1... | collective-permute-start | bytes 1228808 | tf_op jit(solution)/shard_map/ppermute | solution.py:27
  85.2 0.0 all-to-all-done.1.refs_0_
  85.2 1.4 %grid_sum.1 = (bf16[16,16,128]{2,1,0:T(8,128)(2,1)S(1)}, s32[1]{0:T(128)}) custom-call(bf16[16,16,128]{2,1,0:T(8,128)(2,1)} %all-to-all-done.1.refs_0_), custom_call_target="tpu_custom_call" | custom-call | flops 40000000000 | bytes 65536 | tf_op jit(solution)/shard_map/grid_sum/pallas_call | solution.py:54
  86.6 0.0 copy-start.13
  86.6 0.6 copy-done.13
  87.2 7.5 %all-to-all-start.2 = ((bf16[16,16,128]{2,1,0:T(8,128)(2,1)}), bf16[16,16,128]{2,1,0:T(8,128)(2,1)}, u32[]{:S(2)}, u32[]{:S(2)}) async-start(bf16[16,16,128]{2,1,0:T(8,128)(2,1)} %copy-done.13), calls=%async_computation.2 | async-start | bytes 131072 | tf_op jit(solution)/shard_map/all_to_all | solution.py:35
  94.7 0.0 collective-permute-done.4.refs_2_
  94.7 0.0 collective-permute-done.3.refs_1_
  94.7 0.0 collective-permute-done.6.refs_6_
  94.8 0.0 copy-start.8
  94.8 1.1 copy-done.8
  95.9 5.0 %finish.1 = (bf16[320,1152]{1,0:T(8,128)(2,1)}, bf16[320,640]{1,0:T(8,128)(2,1)}, s32[1]{0:T(128)}) custom-call(f32[320,640]{1,0:T(8,128)S(1)} %copy-done.5, f32[320,640]{1,0:T(8,128)} %collective-permute-done.3.refs_1_, bf16[320,640]{1,0:T(8,128)(2,1)} %collective-permute-done.4.refs_2_, bf16[320,1152]{1,0:T(8,128)(2,1)S(1)} %copy-done.8, ...), custom_call_target="tpu_custom_call" | custom-call | flops 960000000 | bytes 5898240 | tf_op jit(solution)/shard_map/finish/pallas_call | solution.py:54
  100.9 5.2 %all-to-all-done.2.refs_0_ = bf16[16,16,128]{2,1,0:T(8,128)(2,1)} async-done(((bf16[16,16,128]{2,1,0:T(8,128)(2,1)}), bf16[16,16,128]{2,1,0:T(8,128)(2,1)}, u32[]{:S(2)}, u32[]{:S(2)}) %all-to-all-start.2) | async-done | bytes 65568 | tf_op jit(solution)/shard_map/all_to_all | solution.py:35
  106.1 1.6 %cube_spread.1 = bf16[16,192,128]{2,1,0:T(8,128)(2,1)S(1)} custom-call(bf16[16,16,128]{2,1,0:T(8,128)(2,1)} %all-to-all-done.2.refs_0_, s32[1]{0:T(128)} %get-tuple-element.54.refs_1_), custom_call_target="tpu_custom_call" | custom-call | bytes 65536 | tf_op jit(solution)/shard_map/cube_spread/pallas_call | solution.py:54
  107.8 13.6 %all_to_all.20.refs_1_ = bf16[16,192,128]{2,1,0:T(8,128)(2,1)S(1)} all-to-all(bf16[16,192,128]{2,1,0:T(8,128)(2,1)S(1)} %cube_spread.1), channel_id=1, replica_groups=mesh['zh'=4,'zl'=2,'x'=4,'yh'=4,'yl'=2,'c'=2] {'zl','x','yl'}, dimensions={0} | all-to-all | bytes 1572864 | tf_op jit(solution)/shard_map/all_to_all | solution.py:35
  121.4 5.3 %collective-permute-start.7 = (bf16[16,192,128]{2,1,0:T(8,128)(2,1)S(1)}, bf16[16,192,128]{2,1,0:T(8,128)(2,1)S(1)}, u32[]{:S(2)}, u32[]{:S(2)}) collective-permute-start(bf16[16,192,128]{2,1,0:T(8,128)(2,1)S(1)} %all_to_all.20.refs_1_), channel_id=1, source_target_pairs={{0,1},{1,0},{2,3},{3,2},{4,5},{5,4},{6,7},{7,6},{8,9},{9,8},{10,11... | collective-permute-start | bytes 2359304 | tf_op jit(solution)/shard_map/ppermute | solution.py:31
  126.6 1.9 %collective-permute-done.7.refs_2_ = bf16[16,192,128]{2,1,0:T(8,128)(2,1)S(1)} collective-permute-done((bf16[16,192,128]{2,1,0:T(8,128)(2,1)S(1)}, bf16[16,192,128]{2,1,0:T(8,128)(2,1)S(1)}, u32[]{:S(2)}, u32[]{:S(2)}) %collective-permute-start.7) | collective-permute-done | bytes 786464 | tf_op jit(solution)/shard_map/ppermute | solution.py:31
  128.5 1.4 %halves.1 = bf16[1152,640]{1,0:T(8,128)(2,1)} custom-call(s32[1]{0:T(128)} %bitcast.refs_1_.refs_0_, bf16[16,192,128]{2,1,0:T(8,128)(2,1)S(1)} %all_to_all.20.refs_1_, bf16[16,192,128]{2,1,0:T(8,128)(2,1)S(1)} %collective-permute-done.7.refs_2_), custom_call_target="tpu_custom_call" | custom-call | bytes 1572864 | tf_op jit(solution)/shard_map/halves/pallas_call | solution.py:54
  (9 shorter events, 0.0 us)
Async XLA Ops:
  0.6 13.4 %collective-permute-start.1 = (bf16[320,1152]{1,0:T(8,128)(2,1)}, bf16[320,1152]{1,0:T(8,128)(2,1)S(1)}, u32[]{:S(2)}, u32[]{:S(2)}) collective-permute-start(bf16[320,1152]{1,0:T(8,128)(2,1)} %refs_3_.1), channel_id=1, source_target_pairs={{0,1},{1,0},{2,3},{3,2},{4,5},{5,4},{6,7},{7,6},{8,9},{9,8},{10,11... | collective-permute-start | bytes 2211848 | tf_op jit(solution)/shard_map/ppermute | solution.py:31
  9.4 14.1 %collective-permute-start.2 = (bf16[320,1152]{1,0:T(8,128)(2,1)}, bf16[320,1152]{1,0:T(8,128)(2,1)S(1)}, u32[]{:S(2)}, u32[]{:S(2)}) collective-permute-start(bf16[320,1152]{1,0:T(8,128)(2,1)} %refs_3_.1), channel_id=1, source_target_pairs={{0,511},{2,1},{4,3},{6,5},{8,7},{10,9},{12,11},{14,13},{16,15},{18... | collective-permute-start | bytes 2211848 | tf_op jit(solution)/shard_map/ppermute | solution.py:27
  10.7 16.0 %collective-permute-start = (bf16[320,640]{1,0:T(8,128)(2,1)}, bf16[320,640]{1,0:T(8,128)(2,1)}, u32[]{:S(2)}, u32[]{:S(2)}) collective-permute-start(bf16[320,640]{1,0:T(8,128)(2,1)} %refs_7_.1), channel_id=1, source_target_pairs={{0,2},{1,3},{2,4},{3,5},{4,6},{5,7},{6,8},{7,9},{8,10},{9,11},{10,... | collective-permute-start | bytes 1228808 | tf_op jit(solution)/shard_map/ppermute | solution.py:27
  14.1 0.9 copy-start.15
  14.9 1.4 %copy-start = (bf16[1152,640]{1,0:T(8,128)(2,1)S(1)}, bf16[1152,640]{1,0:T(8,128)(2,1)}, u32[]{:S(2)}) copy-start(bf16[1152,640]{1,0:T(8,128)(2,1)} %refs_4_.3) | copy-start | bytes 4423684
  16.3 1.1 copy-start.7
  17.4 1.0 copy-start.11
  18.4 1.1 copy-start.16
  19.5 4.0 %copy-start.1 = (bf16[1152,640]{1,0:T(8,128)(2,1)S(1)}, bf16[1152,640]{1,0:T(8,128)(2,1)}, u32[]{:S(2)}) copy-start(bf16[1152,640]{1,0:T(8,128)(2,1)} %refs_4_.3) | copy-start | bytes 4423684
  23.6 7.5 %copy-start.2 = (f32[320,640]{1,0:T(8,128)}, f32[320,640]{1,0:T(8,128)S(1)}, u32[]{:S(2)}) copy-start(f32[320,640]{1,0:T(8,128)S(1)} %get-tuple-element.42.refs_5_) | copy-start | bytes 2457604
  31.1 12.3 %copy-start.4 = (f32[320,640]{1,0:T(8,128)}, f32[320,640]{1,0:T(8,128)S(1)}, u32[]{:S(2)}) copy-start(f32[320,640]{1,0:T(8,128)S(1)} %get-tuple-element.39.refs_0_) | copy-start | bytes 2457604
  31.1 12.3 %copy-start.9 = (bf16[960,320]{1,0:T(8,128)(2,1)}, bf16[960,320]{1,0:T(8,128)(2,1)S(1)}, u32[]{:S(2)}) copy-start(bf16[960,320]{1,0:T(8,128)(2,1)S(1)} %get-tuple-element.43.refs_0_) | copy-start | bytes 1843204
  31.1 12.3 %copy-start.14 = (f32[320,640]{1,0:T(8,128)}, f32[320,640]{1,0:T(8,128)S(1)}, u32[]{:S(2)}) copy-start(f32[320,640]{1,0:T(8,128)S(1)} %get-tuple-element.40) | copy-start | bytes 2457604
  31.1 12.3 %copy-start.17 = (bf16[320,640]{1,0:T(8,128)(2,1)}, bf16[320,640]{1,0:T(8,128)(2,1)S(1)}, u32[]{:S(2)}) copy-start(bf16[320,640]{1,0:T(8,128)(2,1)S(1)} %get-tuple-element.41) | copy-start | bytes 1228804
  31.1 12.8 %collective-permute-start.5 = (bf16[576,640]{1,0:T(8,128)(2,1)S(1)}, bf16[576,640]{1,0:T(8,128)(2,1)S(1)}, u32[]{:S(2)}, u32[]{:S(2)}) collective-permute-start(bf16[576,640]{1,0:T(8,128)(2,1)S(1)} %get-tuple-element.45), channel_id=1, source_target_pairs={{0,1},{1,0},{2,3},{3,2},{4,5},{5,4},{6,7},{7,6},{8,9},{9,8},{10,11... | collective-permute-start | bytes 2211848 | tf_op jit(solution)/shard_map/ppermute | solution.py:31
  44.5 0.9 copy-start.6
  45.4 15.9 %all-to-all-start = ((bf16[16,192,128]{2,1,0:T(8,128)(2,1)}), bf16[16,192,128]{2,1,0:T(8,128)(2,1)S(1)}, u32[]{:S(2)}, u32[]{:S(2)}) async-start(bf16[16,192,128]{2,1,0:T(8,128)(2,1)} %copy-done.6), calls=%async_computation | async-start | bytes 1572864 | tf_op jit(solution)/shard_map/all_to_all | solution.py:35
  49.0 1.1 copy-start.10
  51.7 0.8 copy-start.18
  62.6 22.6 %all-to-all-start.1 = ((bf16[16,16,128]{2,1,0:T(8,128)(2,1)}), bf16[16,16,128]{2,1,0:T(8,128)(2,1)}, u32[]{:S(2)}, u32[]{:S(2)}) async-start(bf16[16,16,128]{2,1,0:T(8,128)(2,1)} %cube_sum.1), calls=%async_computation.1 | async-start | bytes 131072 | tf_op jit(solution)/shard_map/all_to_all | solution.py:35
  70.0 24.7 %collective-permute-start.4 = (bf16[320,640]{1,0:T(8,128)(2,1)}, bf16[320,640]{1,0:T(8,128)(2,1)}, u32[]{:S(2)}, u32[]{:S(2)}) collective-permute-start(bf16[320,640]{1,0:T(8,128)(2,1)} %copy-done.17), channel_id=1, source_target_pairs={{1,2},{3,4},{5,6},{7,8},{9,10},{11,12},{13,14},{15,16},{17,18},{19... | collective-permute-start | bytes 1228808 | tf_op jit(solution)/shard_map/ppermute | solution.py:27
  75.5 19.2 %collective-permute-start.3 = (f32[320,640]{1,0:T(8,128)}, f32[320,640]{1,0:T(8,128)}, u32[]{:S(2)}, u32[]{:S(2)}) collective-permute-start(f32[320,640]{1,0:T(8,128)} %copy-done.14), channel_id=1, source_target_pairs={{0,1},{1,0},{2,3},{3,2},{4,5},{5,4},{6,7},{7,6},{8,9},{9,8},{10,11... | collective-permute-start | bytes 2457608 | tf_op jit(solution)/shard_map/ppermute | solution.py:31
  77.4 17.3 %copy-start.3 = (f32[320,640]{1,0:T(8,128)S(1)}, f32[320,640]{1,0:T(8,128)}, u32[]{:S(2)}) copy-start(f32[320,640]{1,0:T(8,128)} %copy-done.2) | copy-start | bytes 2457604
  77.4 17.3 %copy-start.5 = (f32[320,640]{1,0:T(8,128)S(1)}, f32[320,640]{1,0:T(8,128)}, u32[]{:S(2)}) copy-start(f32[320,640]{1,0:T(8,128)} %copy-done.4) | copy-start | bytes 2457604
  77.4 17.3 %copy-start.12 = (bf16[320,640]{1,0:T(8,128)(2,1)S(1)}, bf16[320,640]{1,0:T(8,128)(2,1)}, u32[]{:S(2)}) copy-start(bf16[320,640]{1,0:T(8,128)(2,1)} %refs_7_.1) | copy-start | bytes 1228804
  77.4 17.3 %collective-permute-start.6 = (bf16[320,640]{1,0:T(8,128)(2,1)}, bf16[320,640]{1,0:T(8,128)(2,1)}, u32[]{:S(2)}, u32[]{:S(2)}) collective-permute-start(bf16[320,640]{1,0:T(8,128)(2,1)} %copy-done.18), channel_id=1, source_target_pairs={{0,510},{1,511},{2,0},{3,1},{4,2},{5,3},{6,4},{7,5},{8,6},{9,7},{1... | collective-permute-start | bytes 1228808 | tf_op jit(solution)/shard_map/ppermute | solution.py:27
  86.6 0.6 copy-start.13
  87.2 19.0 %all-to-all-start.2 = ((bf16[16,16,128]{2,1,0:T(8,128)(2,1)}), bf16[16,16,128]{2,1,0:T(8,128)(2,1)}, u32[]{:S(2)}, u32[]{:S(2)}) async-start(bf16[16,16,128]{2,1,0:T(8,128)(2,1)} %copy-done.13), calls=%async_computation.2 | async-start | bytes 131072 | tf_op jit(solution)/shard_map/all_to_all | solution.py:35
  94.8 1.1 copy-start.8
  121.4 7.2 %collective-permute-start.7 = (bf16[16,192,128]{2,1,0:T(8,128)(2,1)S(1)}, bf16[16,192,128]{2,1,0:T(8,128)(2,1)S(1)}, u32[]{:S(2)}, u32[]{:S(2)}) collective-permute-start(bf16[16,192,128]{2,1,0:T(8,128)(2,1)S(1)} %all_to_all.20.refs_1_), channel_id=1, source_target_pairs={{0,1},{1,0},{2,3},{3,2},{4,5},{5,4},{6,7},{7,6},{8,9},{9,8},{10,11... | collective-permute-start | bytes 2359304 | tf_op jit(solution)/shard_map/ppermute | solution.py:31

commit v3 on v2

--- a/solution.py
+++ b/solution.py
@@ -89,7 +89,7 @@
     return scal[0] * jax.nn.sigmoid(scal[0] * dot_t(img_b, txt_b) + scal[1])
 
 
-def near_body(scal, core, images, other, texts, head, img_n, img_inv, img_b, d_near, d_txt, turned, im):
+def near_body(scal, core, images, other, texts, head, img_n, img_inv, img_b, d_near, own_slope, turned, im):
     im[0:ROWS, :] = images[...]
     im[ROWS:NEAR, :] = other[...]
     txt_b = normalize(texts[...].astype(f32))[0].astype(bf16)
@@ -101,41 +101,45 @@
     col = lax.broadcasted_iota(jnp.int32, (NEAR, ROWS), 1)
     target = jnp.where(row == col, scal[0], 0.0)
     slope = slope_of(img_b[...], txt_b, scal) - target
-    slope = jnp.where((row < ROWS) | (core[0] == 0), slope, 0.0).astype(bf16)
-    d_near[...] = dot(slope, txt_b)
-    d_txt[...] = t_dot(slope, img_b[...])
+    own_slope[...] = jnp.where((row < ROWS) | (core[0] == 0), slope, 0.0).astype(bf16)
+    d_near[...] = dot(own_slope[...], txt_b)
     turned[...] = im[...].T
 
 
-def next_body(nxt, head, img_n, img_inv, img_b, turned):
+def prev_body(scal, core, texts, img_n, img_inv, img_b, d_near, turned,
+              part_sent, d_proj, d_own, d_other, prev_b, slope):
+    text = normalize(texts[...].astype(f32))[0].astype(bf16)
+    prev_b[...] = text
+    slope[...] = slope_of(img_b[...], text, scal).astype(bf16)
+    grad = dot(slope[...], text) + d_near[...]
+    d_own[...] = grad[0:ROWS]
+    d_other[...] = grad[ROWS:NEAR].astype(bf16)
+    d_proj[...] = tangent(grad, img_n[...], img_inv[...]).astype(bf16)
+    second = pl.multiple_of((1 - core[0]) * HALF, HALF)
+    part_sent[...] = dot(turned[pl.ds(second, HALF), :], d_proj[...])
+
+
+def next_body(scal, core, nxt, head, prev_b, part_sent, d_other, sent, d_proj, turned, slope, next_b, d_next):
     norm, inv = normalize(dot(nxt[...], head[...]))
-    img_n[...] = norm
-    img_inv[...] = inv
-    img_b[...] = norm.astype(bf16)
+    next_b[...] = norm.astype(bf16)
+    on_second = jnp.where(core[0] == 1, 1.0, 0.0)
+    slope[...] = (slope_of(next_b[...], prev_b[...], scal) * on_second).astype(bf16)
+    grad = dot(slope[...], prev_b[...])
+    d_next[...] = grad.astype(bf16)
+    d_proj[...] = tangent(grad, norm, inv).astype(bf16)
     turned[...] = nxt[...].T
-
-
-def prev_body(scal, core, texts, img_n, img_inv, img_b, d_near, turned, next_n, next_inv, next_b, turned_next,
-              sent, d_proj, d_own, d_other, d_next, slope):
-    text = normalize(texts[...].astype(f32))[0].astype(bf16)
-    slope[0:NEAR, :] = slope_of(img_b[...], text, scal).astype(bf16)
-    on_second = jnp.where(core[0] == 1, 1.0, 0.0)
-    slope[NEAR:ALL, :] = (slope_of(next_b[...], text, scal) * on_second).astype(bf16)
-    grad = dot(slope[0:NEAR, :], text) + d_near[...]
-    d_own[...] = grad[0:ROWS]
-    d_other[...] = grad[ROWS:NEAR]
-    d_proj[0:NEAR, :] = tangent(grad, img_n[...], img_inv[...]).astype(bf16)
-    grad = dot(slope[NEAR:ALL, :], text)
-    d_next[...] = grad.astype(bf16)
-    d_proj[NEAR:ALL, :] = tangent(grad, next_n[...], next_inv[...]).astype(bf16)
-    rows = pl.ds(pl.multiple_of((1 - core[0]) * HALF, HALF), HALF)
-    part = dot(turned[rows, :], d_proj[0:NEAR, :]) + dot(turned_next[rows, :], d_proj[NEAR:ALL, :])
-    sent[...] = part.astype(bf16)
-
-
-def half_body(core, d_proj, turned, turned_next, out):
+    second = pl.multiple_of((1 - core[0]) * HALF, HALF)
+    sent[0:HALF, :] = (part_sent[...] + dot(turned[pl.ds(second, HALF), :], d_proj[...])).astype(bf16)
+    sent[HALF:, :] = d_other[...]
+
+
+def half_body(core, d_proj, turned, slope, own_slope, img_b, next_proj, next_turned, next_slope, next_b, d_next,
+              mine, back, d_txt, d_late):
     rows = pl.ds(pl.multiple_of(core[0] * HALF, HALF), HALF)
-    out[...] = dot(turned[rows, :], d_proj[0:NEAR, :]) + dot(turned_next[rows, :], d_proj[NEAR:ALL, :])
+    back[...] = (t_dot(slope[...], img_b[...]) + t_dot(next_slope[...], next_b[...])).astype(bf16)
+    d_late[...] = d_next[...]
+    d_txt[...] = t_dot(own_slope[...], img_b[...])
+    mine[...] = dot(turned[rows, :], d_proj[...]) + dot(next_turned[rows, :], next_proj[...])
 
 
 def tiles_of():
@@ -145,16 +149,12 @@
         yield r * 16, slice(c * 128, c * 128 + 128), p, slice(t * 16, t * 16 + 16)
 
 
-def add_body(mine, got, out):
-    total = (mine[...] + got[...].astype(f32)).astype(bf16)
+def add_body(mine, got, d_own, out, d_img):
+    total = (mine[...] + got[0:HALF, :].astype(f32)).astype(bf16)
     for row, cols, p, rows in tiles_of():
         out[p, rows, :] = total[row : row + 16, cols]
     out[SIDE - 1] = jnp.zeros((TILES * 16, 128), bf16)
-
-
-def back_body(slope, img_b, next_b, out):
-    grad = t_dot(slope[0:NEAR, :], img_b[...]) + t_dot(slope[NEAR:ALL, :], next_b[...])
-    out[...] = grad.astype(bf16)
+    d_img[...] = d_own[...] + got[HALF:, :].astype(f32)
 
 
 def cube_sum_body(parts, out):
@@ -174,9 +174,9 @@
         out[:, t * 16 : t * 16 + 16, :] = jnp.broadcast_to(tiles[t][None], (SIDE, 16, 128))
 
 
-def finish_body(d_own, got, late, images, head, d_txt, back, texts, image_out, text_out):
+def finish_body(d_img, late, images, head, d_txt, back, texts, image_out, text_out):
     norm, inv = normalize(dot(images[...], head[...]))
-    d_proj = tangent(d_own[...] + got[...] + late[...].astype(f32), norm, inv).astype(bf16)
+    d_proj = tangent(d_img[...] + late[...].astype(f32), norm, inv).astype(bf16)
     image_out[...] = dot_t(d_proj, head[...]).astype(bf16)
     norm, inv = normalize(texts[...].astype(f32))
     text_out[...] = tangent(d_txt[...] + back[...].astype(f32), norm, inv).astype(bf16)
@@ -197,46 +197,42 @@
     nxt = shifted(images, -1, range(0, COUNT, 2))
     prev = shifted(texts, 2)
 
-    block = (VMEM, (ROWS, E), f32)
-    img_n, img_inv, img_b, d_near, d_txt, turned, mark = call(
+    block, words = (VMEM, (ROWS, E), f32), (VMEM, (ROWS, E), bf16)
+    rows = (VMEM, (HALF, E), f32)
+    img_n, img_inv, img_b, d_near, own_slope, turned = call(
         near_body, "near",
         ((SMEM, scal), (SMEM, core), (VMEM, images), (VMEM, other), (VMEM, texts), (VMEM, head)),
         ((VMEM, (NEAR, E), f32), (VMEM, (NEAR, 1), f32), (VMEM, (NEAR, E), bf16), (VMEM, (NEAR, E), f32),
-         block, (VMEM, (D, NEAR), bf16)),
-        (pltpu.VMEM((NEAR, D), bf16),), 1_730_000_000, mark=True)
-    next_n, next_inv, next_b, turned_next = call(
-        next_body, "next",
-        ((VMEM, nxt), (VMEM, head)),
-        (block, (VMEM, (ROWS, 1), f32), (VMEM, (ROWS, E), bf16), (VMEM, (D, ROWS), bf16)),
-        flops=470_000_000, after=(mark,))
-    sent, d_proj, d_own, d_other, d_next, slope = call(
+         (VMEM, (NEAR, ROWS), bf16), (VMEM, (D, NEAR), bf16)),
+        (pltpu.VMEM((NEAR, D), bf16),), 1_730_000_000)
+    part_sent, d_proj, d_own, d_other, prev_b, slope = call(
         prev_body, "prev",
         ((SMEM, scal), (SMEM, core), (VMEM, prev), (VMEM, img_n), (VMEM, img_inv), (VMEM, img_b), (VMEM, d_near),
-         (VMEM, turned), (VMEM, next_n), (VMEM, next_inv), (VMEM, next_b), (VMEM, turned_next)),
-        ((VMEM, (HALF, E), bf16), (VMEM, (ALL, E), bf16), block, block, (VMEM, (ROWS, E), bf16), (VMEM, (ALL, ROWS), bf16)),
-        flops=1_530_000_000)
-    mine = call(
+         (VMEM, turned)),
+        (rows, (VMEM, (NEAR, E), bf16), block, words, words, (VMEM, (NEAR, ROWS), bf16)), flops=40_000_000_000)
+    sent, next_proj, next_turned, next_slope, next_b, d_next = call(
+        next_body, "next",
+        ((SMEM, scal), (SMEM, core), (VMEM, nxt), (VMEM, head), (VMEM, prev_b), (VMEM, part_sent), (VMEM, d_other)),
+        ((VMEM, (HALF + ROWS, E), bf16), words, (VMEM, (D, ROWS), bf16), (VMEM, (ROWS, ROWS), bf16), words, words),
+        flops=1_000_000_000)
+    mine, back, d_txt, d_next = call(
         half_body, "half",
-        ((SMEM, core), (VMEM, d_proj), (VMEM, turned), (VMEM, turned_next)),
-        ((VMEM, (HALF, E), f32),), flops=710_000_000)
-    part, mark = call(
-        add_body, "add", ((VMEM, mine), (VMEM, swapped(sent))), ((VMEM, (SIDE, TILES * 16, 128), bf16),), mark=True)
-    d_prev, mark = call(
-        back_body, "back", ((VMEM, slope), (VMEM, img_b), (VMEM, next_b)), ((VMEM, (ROWS, E), bf16),),
-        flops=400_000_000, after=(mark,), mark=True)
-    d_beside = swapped(d_other)
+        ((SMEM, core), (VMEM, d_proj), (VMEM, turned), (VMEM, slope), (VMEM, own_slope), (VMEM, img_b), (VMEM, next_proj),
+         (VMEM, next_turned), (VMEM, next_slope), (VMEM, next_b), (VMEM, d_next)),
+        (rows, words, block, words), flops=1_300_000_000)
+    part, d_img = call(
+        add_body, "add", ((VMEM, mine), (VMEM, swapped(sent)), (VMEM, d_own)),
+        ((VMEM, (SIDE, TILES * 16, 128), bf16), block))
+    tiles = call(cube_sum_body, "cube_sum", ((VMEM, exchange(part, CUBE)),), ((VMEM, (SIDE, 16, 128), bf16),))
     d_late = shifted(d_next, 1, range(1, COUNT, 2))
-    d_back = shifted(d_prev, -2)
+    d_back = shifted(back, -2)
     tiles = call(
-        cube_sum_body, "cube_sum", ((VMEM, exchange(part, CUBE)),), ((VMEM, (SIDE, 16, 128), bf16),), after=(mark,))
-    tiles, mark = call(
         grid_sum_body, "grid_sum", ((VMEM, exchange(tiles, GRID)),), ((VMEM, (SIDE, 16, 128), bf16),),
-        flops=40_000_000_000, mark=True)
+        flops=40_000_000_000)
     grad_image, grad_text, mark = call(
         finish_body, "finish",
-        ((VMEM, d_own), (VMEM, d_beside), (VMEM, d_late), (VMEM, images), (VMEM, head), (VMEM, d_txt),
-         (VMEM, d_back), (VMEM, texts)),
-        ((VMEM, (ROWS, D), bf16), (VMEM, (ROWS, E), bf16)), flops=960_000_000, after=(mark,), mark=True)
+        ((VMEM, d_img), (VMEM, d_late), (VMEM, images), (VMEM, head), (VMEM, d_txt), (VMEM, d_back), (VMEM, texts)),
+        ((VMEM, (ROWS, D), bf16), words), flops=960_000_000, mark=True)
     part = call(
         cube_spread_body, "cube_spread", ((VMEM, exchange(tiles, GRID)),),
         ((VMEM, (SIDE, TILES * 16, 128), bf16),), after=(mark,))

time: 131 us -> 123 us (0.939)
  blocking collectives: 13.6 us -> 31.2 us
  starting transfers between devices: 61.9 us -> 44.3 us
  local copies, waits for them, and re-layouts: 9.97 us -> 5.79 us
  Pallas kernels: 23.9 us -> 21.7 us
  waiting for transfers between devices: 18.1 us -> 16.7 us
    all_to_all x1 -> x2, blocking collectives: 13.6 us -> 31.2 us  [exchange(): return lax.all_to_all(value, axes, 0, 0)]
    ppermute x4 -> x3, starting transfers between devices: 27 us -> 13.9 us  [swapped(): return lax.ppermute(value, 'c', [(0, 1), (1, 0)])]
    all_to_all x3 -> x2, waiting for transfers between devices: 14.1 us -> 5.94 us  [exchange(): return lax.all_to_all(value, axes, 0, 0)]
    ppermute x4, waiting for transfers between devices: 1.57 us -> 8.82 us  [shifted(): lax.ppermute(value, AXES, [(s, (s + steps) % COUNT) for s in sources])]
    all_to_all x3 -> x2, starting transfers between devices: 18.6 us -> 13.7 us  [exchange(): return lax.all_to_all(value, axes, 0, 0)]
    unnamed x38 -> x16, local copies, waits for them, and re-layouts: 9.97 us -> 5.79 us
    pallas_call x11 -> x10, Pallas kernels: 23.9 us -> 21.7 us  [call(): pl.pallas_call(run, out_shape=tuple((jax.ShapeDtypeStruct(dims, dtype) fo...]
  transfers between devices with their start and end apart: 11 -> 9, of which waited for: 5 -> 4; matrix products, arithmetic and copies ran while one was open for 0% -> 0% of each run, Pallas kernels for 11% -> 12%
where the time goes in v3:
time: 123 us; the launch traced here: 122 us
  starting transfers between devices  44.3 us (36%)
  blocking collectives  31.2 us (25%)
  Pallas kernels  21.7 us (18%)
  waiting for transfers between devices  16.7 us (14%)
  local copies, waits for them, and re-layouts  5.79 us (5%)
  between operations  2.12 us (2%)
    all_to_all x2, blocking collectives, exchange(): return lax.all_to_all(value, axes, 0, 0)  31.2 us
    pallas_call x10, Pallas kernels, call(): pl.pallas_call(run, out_shape=tuple((jax.ShapeDtypeStruct(dims, dtype) fo...  21.7 us
    ppermute x4, starting transfers between devices, shifted(): lax.ppermute(value, AXES, [(s, (s + steps) % COUNT) for s in sources])  16.7 us
    ppermute x3, starting transfers between devices, swapped(): return lax.ppermute(value, 'c', [(0, 1), (1, 0)])  13.9 us
    all_to_all x2, starting transfers between devices, exchange(): return lax.all_to_all(value, axes, 0, 0)  13.7 us
    ppermute x4, waiting for transfers between devices, shifted(): lax.ppermute(value, AXES, [(s, (s + steps) % COUNT) for s in sources])  8.82 us
    all_to_all x2, waiting for transfers between devices, exchange(): return lax.all_to_all(value, axes, 0, 0)  5.94 us
    unnamed x16, local copies, waits for them, and re-layouts  5.79 us
  transfers between devices with their start and end apart: 9, of which 4 were waited for; matrix products, arithmetic and copies ran while one was open for 0% of the time, Pallas kernels for 12%

profile of v3, /device:TPU:1, one launch (start us, length us, event | category | flops | bytes accessed | tf_op | source)
XLA Modules:
  0.0 121.8 jit_solution(12529761397207045868)
XLA Ops:
  0.6 8.8 %collective-permute-start.1 = (bf16[320,1152]{1,0:T(8,128)(2,1)}, bf16[320,1152]{1,0:T(8,128)(2,1)S(1)}, u32[]{:S(2)}, u32[]{:S(2)}) collective-permute-start(bf16[320,1152]{1,0:T(8,128)(2,1)} %refs_2_.3), channel_id=1, source_target_pairs={{0,1},{1,0},{2,3},{3,2},{4,5},{5,4},{6,7},{7,6},{8,9},{9,8},{10,11... | collective-permute-start | bytes 2211848 | tf_op jit(solution)/shard_map/ppermute | solution.py:31
  9.4 1.9 %collective-permute-start = (bf16[320,640]{1,0:T(8,128)(2,1)}, bf16[320,640]{1,0:T(8,128)(2,1)S(1)}, u32[]{:S(2)}, u32[]{:S(2)}) collective-permute-start(bf16[320,640]{1,0:T(8,128)(2,1)} %refs_6_.1), channel_id=1, source_target_pairs={{0,2},{1,3},{2,4},{3,5},{4,6},{5,7},{6,8},{7,9},{8,10},{9,11},{10,... | collective-permute-start | bytes 1228808 | tf_op jit(solution)/shard_map/ppermute | solution.py:27
  11.4 1.3 %collective-permute-start.2 = (bf16[320,1152]{1,0:T(8,128)(2,1)}, bf16[320,1152]{1,0:T(8,128)(2,1)S(1)}, u32[]{:S(2)}, u32[]{:S(2)}) collective-permute-start(bf16[320,1152]{1,0:T(8,128)(2,1)} %refs_2_.3), channel_id=1, source_target_pairs={{0,511},{2,1},{4,3},{6,5},{8,7},{10,9},{12,11},{14,13},{16,15},{18... | collective-permute-start | bytes 2211848 | tf_op jit(solution)/shard_map/ppermute | solution.py:27
  14.0 0.1 pad_maximum_fusion.refs_0_
  14.1 0.0 collective-permute-done.1.refs_3_
  14.1 0.0 copy-start
  14.1 1.4 %copy-done = bf16[1152,640]{1,0:T(8,128)(2,1)S(1)} copy-done((bf16[1152,640]{1,0:T(8,128)(2,1)S(1)}, bf16[1152,640]{1,0:T(8,128)(2,1)}, u32[]{:S(2)}) %copy-start) | copy-done | bytes 1474584
  15.4 0.0 copy-start.2
  15.4 1.1 copy-done.2
  16.6 0.0 copy-start.4
  16.6 1.0 copy-done.4
  17.6 3.6 %near.1 = (f32[640,640]{1,0:T(8,128)S(1)}, f32[640,1]{1,0:T(8,128)S(1)}, bf16[640,640]{1,0:T(8,128)(2,1)S(1)}, f32[640,640]{1,0:T(8,128)S(1)}, bf16[640,320]{1,0...) custom-call(f32[2]{0:T(128)S(1)} %pad_maximum_fusion.refs_0_, s32[1]{0:T(128)} %bitcast.refs_1_.refs_0_, ...), custom_call_target="tpu_custom_call" | custom-call | flops 1730000000 | bytes 3358720 | tf_op jit(solution)/shard_map/near/pallas_call | solution.py:54
  21.2 8.7 %collective-permute-done.refs_2_ = bf16[320,640]{1,0:T(8,128)(2,1)S(1)} collective-permute-done((bf16[320,640]{1,0:T(8,128)(2,1)}, bf16[320,640]{1,0:T(8,128)(2,1)S(1)}, u32[]{:S(2)}, u32[]{:S(2)}) %collective-permute-start) | collective-permute-done | bytes 409632 | tf_op jit(solution)/shard_map/ppermute | solution.py:27
  29.9 0.0 copy-start.1
  29.9 3.1 %prev.1 = (f32[576,640]{1,0:T(8,128)S(1)}, bf16[640,640]{1,0:T(8,128)(2,1)S(1)}, f32[320,640]{1,0:T(8,128)S(1)}, bf16[320,640]{1,0:T(8,128)(2,1)S(1)}, bf16[320,...) custom-call(f32[2]{0:T(128)S(1)} %pad_maximum_fusion.refs_0_, s32[1]{0:T(128)} %bitcast.refs_1_.refs_0_, ...), custom_call_target="tpu_custom_call" | custom-call | flops 40000000000 | bytes 5982720 | tf_op jit(solution)/shard_map/prev/pallas_call | solution.py:54
  32.9 0.0 collective-permute-done.2.refs_2_
  33.0 0.0 copy-done.1
  33.0 3.1 %next.1 = (bf16[896,640]{1,0:T(8,128)(2,1)S(1)}, bf16[320,640]{1,0:T(8,128)(2,1)S(1)}, bf16[1152,320]{1,0:T(8,128)(2,1)S(1)}, bf16[320,320]{1,0:T(8,128)(2,1)S(1...) custom-call(f32[2]{0:T(128)S(1)} %pad_maximum_fusion.refs_0_, s32[1]{0:T(128)} %bitcast.refs_1_.refs_0_, ...), custom_call_target="tpu_custom_call" | custom-call | flops 1000000000 | bytes 4505600 | tf_op jit(solution)/shard_map/next/pallas_call | solution.py:54
  36.0 2.8 %collective-permute-start.3 = (bf16[896,640]{1,0:T(8,128)(2,1)S(1)}, bf16[896,640]{1,0:T(8,128)(2,1)S(1)}, u32[]{:S(2)}, u32[]{:S(2)}) collective-permute-start(bf16[896,640]{1,0:T(8,128)(2,1)S(1)} %get-tuple-element.47), channel_id=1, source_target_pairs={{0,1},{1,0},{2,3},{3,2},{4,5},{5,4},{6,7},{7,6},{8,9},{9,8},{10,11... | collective-permute-start | bytes 3440648 | tf_op jit(solution)/shard_map/ppermute | solution.py:31
  38.9 3.0 %half.1 = (f32[576,640]{1,0:T(8,128)S(1)}, bf16[320,640]{1,0:T(8,128)(2,1)S(1)}, f32[320,640]{1,0:T(8,128)S(1)}, bf16[320,640]{1,0:T(8,128)(2,1)}) custom-call(s32[1]{0:T(128)} %bitcast.refs_1_.refs_0_, bf16[640,640]{1,0:T(8,128)(2,1)S(1)} %get-tuple-element.35.refs_1_, bf16[1152,640]{1,0:T(8,128)(2,1)S(1)} %get-tuple-element.34.refs_7_.refs_2_, ...), custom_call_target="tpu_custom_call" | custom-call | flops 1300000000 | bytes 6103040 | tf_op jit(solution)/shard_map/half/pallas_call | solution.py:54
  41.9 0.0 copy-start.7
  41.9 0.0 collective-permute-done.3.refs_1_
  41.9 0.2 add.1
  42.1 0.6 copy-done.7
  42.6 15.1 %all_to_all.20.refs_0_ = bf16[16,192,128]{2,1,0:T(8,128)(2,1)S(1)} all-to-all(bf16[16,192,128]{2,1,0:T(8,128)(2,1)S(1)} %get-tuple-element.55), channel_id=1, replica_groups=mesh['zh'=4,'zl'=2,'x'=4,'yh'=4,'yl'=2,'c'=2] {'zl','x','yl'}, dimensions={0} | all-to-all | bytes 1572864 | tf_op jit(solution)/shard_map/all_to_all | solution.py:35
  57.7 0.7 cube_sum.1
  58.4 6.2 %all-to-all-start.1 = ((bf16[16,16,128]{2,1,0:T(8,128)(2,1)}), bf16[16,16,128]{2,1,0:T(8,128)(2,1)}, u32[]{:S(2)}, u32[]{:S(2)}) async-start(bf16[16,16,128]{2,1,0:T(8,128)(2,1)} %cube_sum.1), calls=%async_computation.1 | async-start | bytes 131072 | tf_op jit(solution)/shard_map/all_to_all | solution.py:35
  64.7 5.6 %collective-permute-start.4 = (bf16[320,640]{1,0:T(8,128)(2,1)}, bf16[320,640]{1,0:T(8,128)(2,1)}, u32[]{:S(2)}, u32[]{:S(2)}) collective-permute-start(bf16[320,640]{1,0:T(8,128)(2,1)} %get-tuple-element.50), channel_id=1, source_target_pairs={{1,2},{3,4},{5,6},{7,8},{9,10},{11,12},{13,14},{15,16},{17,18},{19... | collective-permute-start | bytes 1228808 | tf_op jit(solution)/shard_map/ppermute | solution.py:27
  70.2 0.0 copy-start.5
  70.2 7.9 %collective-permute-start.5 = (bf16[320,640]{1,0:T(8,128)(2,1)}, bf16[320,640]{1,0:T(8,128)(2,1)}, u32[]{:S(2)}, u32[]{:S(2)}) collective-permute-start(bf16[320,640]{1,0:T(8,128)(2,1)} %copy-done.7), channel_id=1, source_target_pairs={{0,510},{1,511},{2,0},{3,1},{4,2},{5,3},{6,4},{7,5},{8,6},{9,7},{1... | collective-permute-start | bytes 1228808 | tf_op jit(solution)/shard_map/ppermute | solution.py:27
  78.1 0.0 all-to-all-done.1.refs_0_
  78.1 0.9 grid_sum.1
  79.0 0.0 copy-start.6
  79.0 0.6 copy-done.6
  79.6 7.5 %all-to-all-start.2 = ((bf16[16,16,128]{2,1,0:T(8,128)(2,1)}), bf16[16,16,128]{2,1,0:T(8,128)(2,1)}, u32[]{:S(2)}, u32[]{:S(2)}) async-start(bf16[16,16,128]{2,1,0:T(8,128)(2,1)} %copy-done.6), calls=%async_computation.2 | async-start | bytes 131072 | tf_op jit(solution)/shard_map/all_to_all | solution.py:35
  87.1 0.0 collective-permute-done.4.refs_1_
  87.1 0.2 collective-permute-done.5.refs_5_
  87.3 0.0 copy-done.5
  87.3 0.0 copy-start.3
  87.3 1.1 copy-done.3
  88.4 4.1 %finish.1 = (bf16[320,1152]{1,0:T(8,128)(2,1)}, bf16[320,640]{1,0:T(8,128)(2,1)}, s32[1]{0:T(128)}) custom-call(f32[320,640]{1,0:T(8,128)S(1)} %get-tuple-element.49.refs_0_, bf16[320,640]{1,0:T(8,128)(2,1)} %collective-permute-done.4.refs_1_, bf16[320,1152]{1,0:T(8,128)(2,1)S(1)} %copy-done.3, bf16[1152,640]{1,0:T(8,128)(2,1)S(1)} %copy-done.1, ...), custom_call_target="tpu_custom_call" | custom-call | flops 960000000 | bytes 5079040 | tf_op jit(solution)/shard_map/finish/pallas_call | solution.py:54
  92.6 5.9 %all-to-all-done.2.refs_0_ = bf16[16,16,128]{2,1,0:T(8,128)(2,1)} async-done(((bf16[16,16,128]{2,1,0:T(8,128)(2,1)}), bf16[16,16,128]{2,1,0:T(8,128)(2,1)}, u32[]{:S(2)}, u32[]{:S(2)}) %all-to-all-start.2) | async-done | bytes 65568 | tf_op jit(solution)/shard_map/all_to_all | solution.py:35
  98.5 1.6 %cube_spread.1 = bf16[16,192,128]{2,1,0:T(8,128)(2,1)S(1)} custom-call(bf16[16,16,128]{2,1,0:T(8,128)(2,1)} %all-to-all-done.2.refs_0_, s32[1]{0:T(128)} %get-tuple-element.56.refs_1_), custom_call_target="tpu_custom_call" | custom-call | bytes 65536 | tf_op jit(solution)/shard_map/cube_spread/pallas_call | solution.py:54
  100.1 16.1 %all_to_all.21.refs_1_ = bf16[16,192,128]{2,1,0:T(8,128)(2,1)S(1)} all-to-all(bf16[16,192,128]{2,1,0:T(8,128)(2,1)S(1)} %cube_spread.1), channel_id=1, replica_groups=mesh['zh'=4,'zl'=2,'x'=4,'yh'=4,'yl'=2,'c'=2] {'zl','x','yl'}, dimensions={0} | all-to-all | bytes 1572864 | tf_op jit(solution)/shard_map/all_to_all | solution.py:35
  116.3 2.3 %collective-permute-start.6 = (bf16[16,192,128]{2,1,0:T(8,128)(2,1)S(1)}, bf16[16,192,128]{2,1,0:T(8,128)(2,1)S(1)}, u32[]{:S(2)}, u32[]{:S(2)}) collective-permute-start(bf16[16,192,128]{2,1,0:T(8,128)(2,1)S(1)} %all_to_all.21.refs_1_), channel_id=1, source_target_pairs={{0,1},{1,0},{2,3},{3,2},{4,5},{5,4},{6,7},{7,6},{8,9},{9,8},{10,11... | collective-permute-start | bytes 2359304 | tf_op jit(solution)/shard_map/ppermute | solution.py:31
  118.6 1.9 %collective-permute-done.6.refs_2_ = bf16[16,192,128]{2,1,0:T(8,128)(2,1)S(1)} collective-permute-done((bf16[16,192,128]{2,1,0:T(8,128)(2,1)S(1)}, bf16[16,192,128]{2,1,0:T(8,128)(2,1)S(1)}, u32[]{:S(2)}, u32[]{:S(2)}) %collective-permute-start.6) | collective-permute-done | bytes 786464 | tf_op jit(solution)/shard_map/ppermute | solution.py:31
  120.4 1.4 %halves.1 = bf16[1152,640]{1,0:T(8,128)(2,1)} custom-call(s32[1]{0:T(128)} %bitcast.refs_1_.refs_0_, bf16[16,192,128]{2,1,0:T(8,128)(2,1)S(1)} %all_to_all.21.refs_1_, bf16[16,192,128]{2,1,0:T(8,128)(2,1)S(1)} %collective-permute-done.6.refs_2_), custom_call_target="tpu_custom_call" | custom-call | bytes 1572864 | tf_op jit(solution)/shard_map/halves/pallas_call | solution.py:54
Async XLA Ops:
  0.6 13.4 %collective-permute-start.1 = (bf16[320,1152]{1,0:T(8,128)(2,1)}, bf16[320,1152]{1,0:T(8,128)(2,1)S(1)}, u32[]{:S(2)}, u32[]{:S(2)}) collective-permute-start(bf16[320,1152]{1,0:T(8,128)(2,1)} %refs_2_.3), channel_id=1, source_target_pairs={{0,1},{1,0},{2,3},{3,2},{4,5},{5,4},{6,7},{7,6},{8,9},{9,8},{10,11... | collective-permute-start | bytes 2211848 | tf_op jit(solution)/shard_map/ppermute | solution.py:31
  9.4 20.4 %collective-permute-start = (bf16[320,640]{1,0:T(8,128)(2,1)}, bf16[320,640]{1,0:T(8,128)(2,1)S(1)}, u32[]{:S(2)}, u32[]{:S(2)}) collective-permute-start(bf16[320,640]{1,0:T(8,128)(2,1)} %refs_6_.1), channel_id=1, source_target_pairs={{0,2},{1,3},{2,4},{3,5},{4,6},{5,7},{6,8},{7,9},{8,10},{9,11},{10,... | collective-permute-start | bytes 1228808 | tf_op jit(solution)/shard_map/ppermute | solution.py:27
  11.4 21.6 %collective-permute-start.2 = (bf16[320,1152]{1,0:T(8,128)(2,1)}, bf16[320,1152]{1,0:T(8,128)(2,1)S(1)}, u32[]{:S(2)}, u32[]{:S(2)}) collective-permute-start(bf16[320,1152]{1,0:T(8,128)(2,1)} %refs_2_.3), channel_id=1, source_target_pairs={{0,511},{2,1},{4,3},{6,5},{8,7},{10,9},{12,11},{14,13},{16,15},{18... | collective-permute-start | bytes 2211848 | tf_op jit(solution)/shard_map/ppermute | solution.py:27
  14.1 1.4 %copy-start = (bf16[1152,640]{1,0:T(8,128)(2,1)S(1)}, bf16[1152,640]{1,0:T(8,128)(2,1)}, u32[]{:S(2)}) copy-start(bf16[1152,640]{1,0:T(8,128)(2,1)} %refs_3_.3) | copy-start | bytes 4423684
  15.4 1.1 copy-start.2
  16.6 1.0 copy-start.4
  29.9 3.1 %copy-start.1 = (bf16[1152,640]{1,0:T(8,128)(2,1)S(1)}, bf16[1152,640]{1,0:T(8,128)(2,1)}, u32[]{:S(2)}) copy-start(bf16[1152,640]{1,0:T(8,128)(2,1)} %refs_3_.3) | copy-start | bytes 4423684
  36.0 5.8 %collective-permute-start.3 = (bf16[896,640]{1,0:T(8,128)(2,1)S(1)}, bf16[896,640]{1,0:T(8,128)(2,1)S(1)}, u32[]{:S(2)}, u32[]{:S(2)}) collective-permute-start(bf16[896,640]{1,0:T(8,128)(2,1)S(1)} %get-tuple-element.47), channel_id=1, source_target_pairs={{0,1},{1,0},{2,3},{3,2},{4,5},{5,4},{6,7},{7,6},{8,9},{9,8},{10,11... | collective-permute-start | bytes 3440648 | tf_op jit(solution)/shard_map/ppermute | solution.py:31
  41.9 0.8 copy-start.7
  58.4 19.7 %all-to-all-start.1 = ((bf16[16,16,128]{2,1,0:T(8,128)(2,1)}), bf16[16,16,128]{2,1,0:T(8,128)(2,1)}, u32[]{:S(2)}, u32[]{:S(2)}) async-start(bf16[16,16,128]{2,1,0:T(8,128)(2,1)} %cube_sum.1), calls=%async_computation.1 | async-start | bytes 131072 | tf_op jit(solution)/shard_map/all_to_all | solution.py:35
  64.7 22.5 %collective-permute-start.4 = (bf16[320,640]{1,0:T(8,128)(2,1)}, bf16[320,640]{1,0:T(8,128)(2,1)}, u32[]{:S(2)}, u32[]{:S(2)}) collective-permute-start(bf16[320,640]{1,0:T(8,128)(2,1)} %get-tuple-element.50), channel_id=1, source_target_pairs={{1,2},{3,4},{5,6},{7,8},{9,10},{11,12},{13,14},{15,16},{17,18},{19... | collective-permute-start | bytes 1228808 | tf_op jit(solution)/shard_map/ppermute | solution.py:27
  70.2 17.1 %copy-start.5 = (bf16[320,640]{1,0:T(8,128)(2,1)S(1)}, bf16[320,640]{1,0:T(8,128)(2,1)}, u32[]{:S(2)}) copy-start(bf16[320,640]{1,0:T(8,128)(2,1)} %refs_6_.1) | copy-start | bytes 1228804
  70.2 17.1 %collective-permute-start.5 = (bf16[320,640]{1,0:T(8,128)(2,1)}, bf16[320,640]{1,0:T(8,128)(2,1)}, u32[]{:S(2)}, u32[]{:S(2)}) collective-permute-start(bf16[320,640]{1,0:T(8,128)(2,1)} %copy-done.7), channel_id=1, source_target_pairs={{0,510},{1,511},{2,0},{3,1},{4,2},{5,3},{6,4},{7,5},{8,6},{9,7},{1... | collective-permute-start | bytes 1228808 | tf_op jit(solution)/shard_map/ppermute | solution.py:27
  79.0 0.6 copy-start.6
  79.6 18.9 %all-to-all-start.2 = ((bf16[16,16,128]{2,1,0:T(8,128)(2,1)}), bf16[16,16,128]{2,1,0:T(8,128)(2,1)}, u32[]{:S(2)}, u32[]{:S(2)}) async-start(bf16[16,16,128]{2,1,0:T(8,128)(2,1)} %copy-done.6), calls=%async_computation.2 | async-start | bytes 131072 | tf_op jit(solution)/shard_map/all_to_all | solution.py:35
  87.3 1.1 copy-start.3
  116.3 4.2 %collective-permute-start.6 = (bf16[16,192,128]{2,1,0:T(8,128)(2,1)S(1)}, bf16[16,192,128]{2,1,0:T(8,128)(2,1)S(1)}, u32[]{:S(2)}, u32[]{:S(2)}) collective-permute-start(bf16[16,192,128]{2,1,0:T(8,128)(2,1)S(1)} %all_to_all.21.refs_1_), channel_id=1, source_target_pairs={{0,1},{1,0},{2,3},{3,2},{4,5},{5,4},{6,7},{7,6},{8,9},{9,8},{10,11... | collective-permute-start | bytes 2359304 | tf_op jit(solution)/shard_map/ppermute | solution.py:31

commit v4 on v3

--- a/solution.py
+++ b/solution.py
@@ -89,10 +89,14 @@
     return scal[0] * jax.nn.sigmoid(scal[0] * dot_t(img_b, txt_b) + scal[1])
 
 
-def near_body(scal, core, images, other, texts, head, img_n, img_inv, img_b, d_near, own_slope, turned, im):
+def words_body(scal, core, texts, out):
+    out[...] = normalize(texts[...].astype(f32))[0].astype(bf16)
+
+
+def near_body(scal, core, images, other, words, head, img_n, img_inv, img_b, d_near, own_slope, turned, im):
     im[0:ROWS, :] = images[...]
     im[ROWS:NEAR, :] = other[...]
-    txt_b = normalize(texts[...].astype(f32))[0].astype(bf16)
+    txt_b = words[...]
     norm, inv = normalize(dot(im[...], head[...]))
     img_n[...] = norm
     img_inv[...] = inv
@@ -174,12 +178,15 @@
         out[:, t * 16 : t * 16 + 16, :] = jnp.broadcast_to(tiles[t][None], (SIDE, 16, 128))
 
 
-def finish_body(d_img, late, images, head, d_txt, back, texts, image_out, text_out):
+def image_body(d_img, late, images, head, out):
     norm, inv = normalize(dot(images[...], head[...]))
     d_proj = tangent(d_img[...] + late[...].astype(f32), norm, inv).astype(bf16)
-    image_out[...] = dot_t(d_proj, head[...]).astype(bf16)
+    out[...] = dot_t(d_proj, head[...]).astype(bf16)
+
+
+def text_body(d_txt, back, texts, out):
     norm, inv = normalize(texts[...].astype(f32))
-    text_out[...] = tangent(d_txt[...] + back[...].astype(f32), norm, inv).astype(bf16)
+    out[...] = tangent(d_txt[...] + back[...].astype(f32), norm, inv).astype(bf16)
 
 
 def halves_body(core, mine, got, out):
@@ -199,12 +206,14 @@
 
     block, words = (VMEM, (ROWS, E), f32), (VMEM, (ROWS, E), bf16)
     rows = (VMEM, (HALF, E), f32)
+    txt_b = call(
+        words_body, "words", ((SMEM, scal), (SMEM, core), (VMEM, texts)), (words,), flops=1_000_000_000)
     img_n, img_inv, img_b, d_near, own_slope, turned = call(
         near_body, "near",
-        ((SMEM, scal), (SMEM, core), (VMEM, images), (VMEM, other), (VMEM, texts), (VMEM, head)),
+        ((SMEM, scal), (SMEM, core), (VMEM, images), (VMEM, other), (VMEM, txt_b), (VMEM, head)),
         ((VMEM, (NEAR, E), f32), (VMEM, (NEAR, 1), f32), (VMEM, (NEAR, E), bf16), (VMEM, (NEAR, E), f32),
          (VMEM, (NEAR, ROWS), bf16), (VMEM, (D, NEAR), bf16)),
-        (pltpu.VMEM((NEAR, D), bf16),), 1_730_000_000)
+        (pltpu.VMEM((NEAR, D), bf16),), 100_000_000)
     part_sent, d_proj, d_own, d_other, prev_b, slope = call(
         prev_body, "prev",
         ((SMEM, scal), (SMEM, core), (VMEM, prev), (VMEM, img_n), (VMEM, img_inv), (VMEM, img_b), (VMEM, d_near),
@@ -229,13 +238,14 @@
     tiles = call(
         grid_sum_body, "grid_sum", ((VMEM, exchange(tiles, GRID)),), ((VMEM, (SIDE, 16, 128), bf16),),
         flops=40_000_000_000)
-    grad_image, grad_text, mark = call(
-        finish_body, "finish",
-        ((VMEM, d_img), (VMEM, d_late), (VMEM, images), (VMEM, head), (VMEM, d_txt), (VMEM, d_back), (VMEM, texts)),
-        ((VMEM, (ROWS, D), bf16), words), flops=960_000_000, mark=True)
+    grad_image, image_mark = call(
+        image_body, "image", ((VMEM, d_img), (VMEM, d_late), (VMEM, images), (VMEM, head)),
+        ((VMEM, (ROWS, D), bf16),), flops=960_000_000, mark=True)
+    grad_text, text_mark = call(
+        text_body, "text", ((VMEM, d_txt), (VMEM, d_back), (VMEM, texts)), (words,), after=(image_mark,), mark=True)
     part = call(
         cube_spread_body, "cube_spread", ((VMEM, exchange(tiles, GRID)),),
-        ((VMEM, (SIDE, TILES * 16, 128), bf16),), after=(mark,))
+        ((VMEM, (SIDE, TILES * 16, 128), bf16),), after=(text_mark,))
     part = exchange(part, CUBE)
     grad_head = call(
         halves_body, "halves", ((SMEM, core), (VMEM, part), (VMEM, swapped(part))), ((VMEM, (D, E), bf16),))

time: 123 us -> 120 us (0.976)
  local copies, waits for them, and re-layouts: 5.79 us -> 4.16 us
    unnamed x16, local copies, waits for them, and re-layouts: 5.79 us -> 4.16 us
    all_to_all x2, waiting for transfers between devices: 5.94 us -> 4.45 us  [exchange(): return lax.all_to_all(value, axes, 0, 0)]
    pallas_call x10 -> x12, Pallas kernels: 21.7 us -> 22.9 us  [call(): pl.pallas_call(run, out_shape=tuple((jax.ShapeDtypeStruct(dims, dtype) fo...]
  transfers between devices with their start and end apart: 9 -> 9, of which waited for: 4 -> 3; matrix products, arithmetic and copies ran while one was open for 0% -> 0% of each run, Pallas kernels for 12% -> 14%
where the time goes in v4:
time: 120 us
  starting transfers between devices  43.9 us (37%)
  blocking collectives  30.9 us (26%)
  Pallas kernels  22.9 us (19%)
  waiting for transfers between devices  15.5 us (13%)
  local copies, waits for them, and re-layouts  4.16 us (3%)
  between operations  2.15 us (2%)
    all_to_all x2, blocking collectives, exchange(): return lax.all_to_all(value, axes, 0, 0)  30.9 us
    pallas_call x12, Pallas kernels, call(): pl.pallas_call(run, out_shape=tuple((jax.ShapeDtypeStruct(dims, dtype) fo...  22.9 us
    ppermute x4, starting transfers between devices, shifted(): lax.ppermute(value, AXES, [(s, (s + steps) % COUNT) for s in sources])  16.8 us
    all_to_all x2, starting transfers between devices, exchange(): return lax.all_to_all(value, axes, 0, 0)  13.7 us
    ppermute x3, starting transfers between devices, swapped(): return lax.ppermute(value, 'c', [(0, 1), (1, 0)])  13.4 us
    ppermute x4, waiting for transfers between devices, shifted(): lax.ppermute(value, AXES, [(s, (s + steps) % COUNT) for s in sources])  8.97 us
    all_to_all x2, waiting for transfers between devices, exchange(): return lax.all_to_all(value, axes, 0, 0)  4.45 us
    unnamed x16, local copies, waits for them, and re-layouts  4.16 us
  transfers between devices with their start and end apart: 9, of which 3 were waited for; matrix products, arithmetic and copies ran while one was open for 0% of the time, Pallas kernels for 14%

profile of v4, /device:TPU:1, one launch (start us, length us, event | category | flops | bytes accessed | tf_op | source)
XLA Modules:
  0.0 119.6 jit_solution(15343928851918210993)
XLA Ops:
  0.6 8.8 %collective-permute-start.1 = (bf16[320,1152]{1,0:T(8,128)(2,1)}, bf16[320,1152]{1,0:T(8,128)(2,1)}, u32[]{:S(2)}, u32[]{:S(2)}) collective-permute-start(bf16[320,1152]{1,0:T(8,128)(2,1)} %refs_2_.6), channel_id=1, source_target_pairs={{0,1},{1,0},{2,3},{3,2},{4,5},{5,4},{6,7},{7,6},{8,9},{9,8},{10,11... | collective-permute-start | bytes 2211848 | tf_op jit(solution)/shard_map/ppermute | solution.py:31
  9.4 1.9 %collective-permute-start = (bf16[320,640]{1,0:T(8,128)(2,1)}, bf16[320,640]{1,0:T(8,128)(2,1)S(1)}, u32[]{:S(2)}, u32[]{:S(2)}) collective-permute-start(bf16[320,640]{1,0:T(8,128)(2,1)} %refs_2_.7), channel_id=1, source_target_pairs={{0,2},{1,3},{2,4},{3,5},{4,6},{5,7},{6,8},{7,9},{8,10},{9,11},{10,... | collective-permute-start | bytes 1228808 | tf_op jit(solution)/shard_map/ppermute | solution.py:27
  11.4 1.3 %collective-permute-start.2 = (bf16[320,1152]{1,0:T(8,128)(2,1)}, bf16[320,1152]{1,0:T(8,128)(2,1)S(1)}, u32[]{:S(2)}, u32[]{:S(2)}) collective-permute-start(bf16[320,1152]{1,0:T(8,128)(2,1)} %refs_2_.6), channel_id=1, source_target_pairs={{0,511},{2,1},{4,3},{6,5},{8,7},{10,9},{12,11},{14,13},{16,15},{18... | collective-permute-start | bytes 2211848 | tf_op jit(solution)/shard_map/ppermute | solution.py:27
  14.0 0.1 pad_maximum_fusion.refs_0_
  14.1 0.0 copy-start.2
  14.1 1.0 copy-done.2
  15.1 0.0 copy-start
  15.1 0.0 copy-start.1
  15.1 0.7 words.1.refs_4_
  15.8 0.0 collective-permute-done.1.refs_3_
  15.8 0.7 copy-done
  16.4 0.2 copy-done.1
  16.6 4.3 %near.1 = (f32[640,640]{1,0:T(8,128)S(1)}, f32[640,1]{1,0:T(8,128)S(1)}, bf16[640,640]{1,0:T(8,128)(2,1)S(1)}, f32[640,640]{1,0:T(8,128)S(1)}, bf16[640,320]{1,0...) custom-call(f32[2]{0:T(128)S(1)} %pad_maximum_fusion.refs_0_, s32[1]{0:T(128)} %bitcast.refs_1_.refs_0_, ...), custom_call_target="tpu_custom_call" | custom-call | flops 100000000 | bytes 3358720 | tf_op jit(solution)/shard_map/near/pallas_call | solution.py:54
  20.9 9.0 %collective-permute-done.refs_2_ = bf16[320,640]{1,0:T(8,128)(2,1)S(1)} collective-permute-done((bf16[320,640]{1,0:T(8,128)(2,1)}, bf16[320,640]{1,0:T(8,128)(2,1)S(1)}, u32[]{:S(2)}, u32[]{:S(2)}) %collective-permute-start) | collective-permute-done | bytes 409632 | tf_op jit(solution)/shard_map/ppermute | solution.py:27
  29.9 3.1 %prev.1 = (f32[576,640]{1,0:T(8,128)S(1)}, bf16[640,640]{1,0:T(8,128)(2,1)S(1)}, f32[320,640]{1,0:T(8,128)S(1)}, bf16[320,640]{1,0:T(8,128)(2,1)S(1)}, bf16[320,...) custom-call(f32[2]{0:T(128)S(1)} %pad_maximum_fusion.refs_0_, s32[1]{0:T(128)} %bitcast.refs_1_.refs_0_, ...), custom_call_target="tpu_custom_call" | custom-call | flops 40000000000 | bytes 5982720 | tf_op jit(solution)/shard_map/prev/pallas_call | solution.py:54
  32.9 0.0 collective-permute-done.2.refs_2_
  32.9 3.1 %next.1 = (bf16[896,640]{1,0:T(8,128)(2,1)S(1)}, bf16[320,640]{1,0:T(8,128)(2,1)S(1)}, bf16[1152,320]{1,0:T(8,128)(2,1)S(1)}, bf16[320,320]{1,0:T(8,128)(2,1)S(1...) custom-call(f32[2]{0:T(128)S(1)} %pad_maximum_fusion.refs_0_, s32[1]{0:T(128)} %bitcast.refs_1_.refs_0_, ...), custom_call_target="tpu_custom_call" | custom-call | flops 1000000000 | bytes 4505600 | tf_op jit(solution)/shard_map/next/pallas_call | solution.py:54
  36.0 2.5 %collective-permute-start.3 = (bf16[896,640]{1,0:T(8,128)(2,1)S(1)}, bf16[896,640]{1,0:T(8,128)(2,1)S(1)}, u32[]{:S(2)}, u32[]{:S(2)}) collective-permute-start(bf16[896,640]{1,0:T(8,128)(2,1)S(1)} %get-tuple-element.48), channel_id=1, source_target_pairs={{0,1},{1,0},{2,3},{3,2},{4,5},{5,4},{6,7},{7,6},{8,9},{9,8},{10,11... | collective-permute-start | bytes 3440648 | tf_op jit(solution)/shard_map/ppermute | solution.py:31
  38.6 3.0 %half.1 = (f32[576,640]{1,0:T(8,128)S(1)}, bf16[320,640]{1,0:T(8,128)(2,1)S(1)}, f32[320,640]{1,0:T(8,128)S(1)}, bf16[320,640]{1,0:T(8,128)(2,1)}) custom-call(s32[1]{0:T(128)} %bitcast.refs_1_.refs_0_, bf16[640,640]{1,0:T(8,128)(2,1)S(1)} %get-tuple-element.36.refs_1_, bf16[1152,640]{1,0:T(8,128)(2,1)S(1)} %get-tuple-element.35.refs_7_.refs_2_, ...), custom_call_target="tpu_custom_call" | custom-call | flops 1300000000 | bytes 6103040 | tf_op jit(solution)/shard_map/half/pallas_call | solution.py:54
  41.5 0.0 copy-start.7
  41.5 0.0 collective-permute-done.3.refs_1_
  41.5 0.2 add.1
  41.7 0.6 copy-done.7
  42.3 0.0 copy-start.5
  42.3 15.1 %all_to_all.20.refs_0_ = bf16[16,192,128]{2,1,0:T(8,128)(2,1)S(1)} all-to-all(bf16[16,192,128]{2,1,0:T(8,128)(2,1)S(1)} %get-tuple-element.57), channel_id=1, replica_groups=mesh['zh'=4,'zl'=2,'x'=4,'yh'=4,'yl'=2,'c'=2] {'zl','x','yl'}, dimensions={0} | all-to-all | bytes 1572864 | tf_op jit(solution)/shard_map/all_to_all | solution.py:35
  57.4 0.0 copy-done.5
  57.4 0.7 cube_sum.1
  58.1 6.2 %all-to-all-start.1 = ((bf16[16,16,128]{2,1,0:T(8,128)(2,1)}), bf16[16,16,128]{2,1,0:T(8,128)(2,1)S(1)}, u32[]{:S(2)}, u32[]{:S(2)}) async-start(bf16[16,16,128]{2,1,0:T(8,128)(2,1)} %cube_sum.1), calls=%async_computation.1 | async-start | bytes 131072 | tf_op jit(solution)/shard_map/all_to_all | solution.py:35
  64.3 5.9 %collective-permute-start.4 = (bf16[320,640]{1,0:T(8,128)(2,1)}, bf16[320,640]{1,0:T(8,128)(2,1)}, u32[]{:S(2)}, u32[]{:S(2)}) collective-permute-start(bf16[320,640]{1,0:T(8,128)(2,1)} %get-tuple-element.51), channel_id=1, source_target_pairs={{1,2},{3,4},{5,6},{7,8},{9,10},{11,12},{13,14},{15,16},{17,18},{19... | collective-permute-start | bytes 1228808 | tf_op jit(solution)/shard_map/ppermute | solution.py:27
  70.2 7.8 %collective-permute-start.5 = (bf16[320,640]{1,0:T(8,128)(2,1)}, bf16[320,640]{1,0:T(8,128)(2,1)S(1)}, u32[]{:S(2)}, u32[]{:S(2)}) collective-permute-start(bf16[320,640]{1,0:T(8,128)(2,1)} %copy-done.7), channel_id=1, source_target_pairs={{0,510},{1,511},{2,0},{3,1},{4,2},{5,3},{6,4},{7,5},{8,6},{9,7},{1... | collective-permute-start | bytes 1228808 | tf_op jit(solution)/shard_map/ppermute | solution.py:27
  77.9 0.0 all-to-all-done.1.refs_0_
  78.0 0.0 copy-start.4
  78.0 0.6 copy-done.4
  78.6 7.5 %all-to-all-start.2 = ((bf16[16,16,128]{2,1,0:T(8,128)(2,1)}), bf16[16,16,128]{2,1,0:T(8,128)(2,1)S(1)}, u32[]{:S(2)}, u32[]{:S(2)}) async-start(bf16[16,16,128]{2,1,0:T(8,128)(2,1)} %copy-done.4), calls=%async_computation.2 | async-start | bytes 131072 | tf_op jit(solution)/shard_map/all_to_all | solution.py:35
  86.1 0.0 collective-permute-done.4.refs_1_
  86.1 0.0 copy-start.6
  86.1 1.1 copy-done.6
  87.3 0.0 copy-start.3
  87.3 4.0 %image.1 = (bf16[320,1152]{1,0:T(8,128)(2,1)}, s32[1]{0:T(128)}) custom-call(f32[320,640]{1,0:T(8,128)S(1)} %copy-done.6, bf16[320,640]{1,0:T(8,128)(2,1)} %collective-permute-done.4.refs_1_, bf16[320,1152]{1,0:T(8,128)(2,1)S(1)} %copy-done.1, bf16[1152,640]{1,0:T(8,128)(2,1)S(1)} %copy-done), custom_call_target="tpu_custom_call" | custom-call | flops 960000000 | bytes 3440640 | tf_op jit(solution)/shard_map/image/pallas_call | solution.py:54
  91.2 0.0 collective-permute-done.5.refs_1_
  91.2 0.0 copy-done.3
  91.2 1.7 %text.1 = (bf16[320,640]{1,0:T(8,128)(2,1)}, s32[1]{0:T(128)}) custom-call(f32[320,640]{1,0:T(8,128)S(1)} %get-tuple-element.53.refs_0_, bf16[320,640]{1,0:T(8,128)(2,1)S(1)} %collective-permute-done.5.refs_1_, bf16[320,640]{1,0:T(8,128)(2,1)S(1)} %copy-done.3, s32[1]{0:T(128)} %get-tuple-element.55.refs_3_), custom_call_target="tpu_custom_call" | custom-call | bytes 1638400 | tf_op jit(solution)/shard_map/text/pallas_call | solution.py:54
  93.0 4.4 %all-to-all-done.2.refs_0_ = bf16[16,16,128]{2,1,0:T(8,128)(2,1)S(1)} async-done(((bf16[16,16,128]{2,1,0:T(8,128)(2,1)}), bf16[16,16,128]{2,1,0:T(8,128)(2,1)S(1)}, u32[]{:S(2)}, u32[]{:S(2)}) %all-to-all-start.2) | async-done | bytes 65568 | tf_op jit(solution)/shard_map/all_to_all | solution.py:35
  97.4 0.8 cube_spread.1
  98.3 15.8 %all_to_all.21.refs_1_ = bf16[16,192,128]{2,1,0:T(8,128)(2,1)S(1)} all-to-all(bf16[16,192,128]{2,1,0:T(8,128)(2,1)S(1)} %cube_spread.1), channel_id=1, replica_groups=mesh['zh'=4,'zl'=2,'x'=4,'yh'=4,'yl'=2,'c'=2] {'zl','x','yl'}, dimensions={0} | all-to-all | bytes 1572864 | tf_op jit(solution)/shard_map/all_to_all | solution.py:35
  114.1 2.1 %collective-permute-start.6 = (bf16[16,192,128]{2,1,0:T(8,128)(2,1)S(1)}, bf16[16,192,128]{2,1,0:T(8,128)(2,1)S(1)}, u32[]{:S(2)}, u32[]{:S(2)}) collective-permute-start(bf16[16,192,128]{2,1,0:T(8,128)(2,1)S(1)} %all_to_all.21.refs_1_), channel_id=1, source_target_pairs={{0,1},{1,0},{2,3},{3,2},{4,5},{5,4},{6,7},{7,6},{8,9},{9,8},{10,11... | collective-permute-start | bytes 2359304 | tf_op jit(solution)/shard_map/ppermute | solution.py:31
  116.2 2.0 %collective-permute-done.6.refs_2_ = bf16[16,192,128]{2,1,0:T(8,128)(2,1)S(1)} collective-permute-done((bf16[16,192,128]{2,1,0:T(8,128)(2,1)S(1)}, bf16[16,192,128]{2,1,0:T(8,128)(2,1)S(1)}, u32[]{:S(2)}, u32[]{:S(2)}) %collective-permute-start.6) | collective-permute-done | bytes 786464 | tf_op jit(solution)/shard_map/ppermute | solution.py:31
  118.2 1.4 %halves.1 = bf16[1152,640]{1,0:T(8,128)(2,1)} custom-call(s32[1]{0:T(128)} %bitcast.refs_1_.refs_0_, bf16[16,192,128]{2,1,0:T(8,128)(2,1)S(1)} %all_to_all.21.refs_1_, bf16[16,192,128]{2,1,0:T(8,128)(2,1)S(1)} %collective-permute-done.6.refs_2_), custom_call_target="tpu_custom_call" | custom-call | bytes 1572864 | tf_op jit(solution)/shard_map/halves/pallas_call | solution.py:54
  (1 shorter events, 0.0 us)
Async XLA Ops:
  0.6 15.2 %collective-permute-start.1 = (bf16[320,1152]{1,0:T(8,128)(2,1)}, bf16[320,1152]{1,0:T(8,128)(2,1)}, u32[]{:S(2)}, u32[]{:S(2)}) collective-permute-start(bf16[320,1152]{1,0:T(8,128)(2,1)} %refs_2_.6), channel_id=1, source_target_pairs={{0,1},{1,0},{2,3},{3,2},{4,5},{5,4},{6,7},{7,6},{8,9},{9,8},{10,11... | collective-permute-start | bytes 2211848 | tf_op jit(solution)/shard_map/ppermute | solution.py:31
  9.4 20.4 %collective-permute-start = (bf16[320,640]{1,0:T(8,128)(2,1)}, bf16[320,640]{1,0:T(8,128)(2,1)S(1)}, u32[]{:S(2)}, u32[]{:S(2)}) collective-permute-start(bf16[320,640]{1,0:T(8,128)(2,1)} %refs_2_.7), channel_id=1, source_target_pairs={{0,2},{1,3},{2,4},{3,5},{4,6},{5,7},{6,8},{7,9},{8,10},{9,11},{10,... | collective-permute-start | bytes 1228808 | tf_op jit(solution)/shard_map/ppermute | solution.py:27
  11.4 21.6 %collective-permute-start.2 = (bf16[320,1152]{1,0:T(8,128)(2,1)}, bf16[320,1152]{1,0:T(8,128)(2,1)S(1)}, u32[]{:S(2)}, u32[]{:S(2)}) collective-permute-start(bf16[320,1152]{1,0:T(8,128)(2,1)} %refs_2_.6), channel_id=1, source_target_pairs={{0,511},{2,1},{4,3},{6,5},{8,7},{10,9},{12,11},{14,13},{16,15},{18... | collective-permute-start | bytes 2211848 | tf_op jit(solution)/shard_map/ppermute | solution.py:27
  14.1 1.0 copy-start.2
  15.1 1.4 %copy-start = (bf16[1152,640]{1,0:T(8,128)(2,1)S(1)}, bf16[1152,640]{1,0:T(8,128)(2,1)}, u32[]{:S(2)}) copy-start(bf16[1152,640]{1,0:T(8,128)(2,1)} %refs_3_.3) | copy-start | bytes 4423684
  15.1 1.6 %copy-start.1 = (bf16[320,1152]{1,0:T(8,128)(2,1)S(1)}, bf16[320,1152]{1,0:T(8,128)(2,1)}, u32[]{:S(2)}) copy-start(bf16[320,1152]{1,0:T(8,128)(2,1)} %refs_2_.6) | copy-start | bytes 2211844
  36.0 5.5 %collective-permute-start.3 = (bf16[896,640]{1,0:T(8,128)(2,1)S(1)}, bf16[896,640]{1,0:T(8,128)(2,1)S(1)}, u32[]{:S(2)}, u32[]{:S(2)}) collective-permute-start(bf16[896,640]{1,0:T(8,128)(2,1)S(1)} %get-tuple-element.48), channel_id=1, source_target_pairs={{0,1},{1,0},{2,3},{3,2},{4,5},{5,4},{6,7},{7,6},{8,9},{9,8},{10,11... | collective-permute-start | bytes 3440648 | tf_op jit(solution)/shard_map/ppermute | solution.py:31
  41.5 0.8 copy-start.7
  42.3 15.1 %copy-start.5 = (f32[320,640]{1,0:T(8,128)}, f32[320,640]{1,0:T(8,128)S(1)}, u32[]{:S(2)}) copy-start(f32[320,640]{1,0:T(8,128)S(1)} %get-tuple-element.50.refs_0_) | copy-start | bytes 2457604
  58.1 19.8 %all-to-all-start.1 = ((bf16[16,16,128]{2,1,0:T(8,128)(2,1)}), bf16[16,16,128]{2,1,0:T(8,128)(2,1)S(1)}, u32[]{:S(2)}, u32[]{:S(2)}) async-start(bf16[16,16,128]{2,1,0:T(8,128)(2,1)} %cube_sum.1), calls=%async_computation.1 | async-start | bytes 131072 | tf_op jit(solution)/shard_map/all_to_all | solution.py:35
  64.3 21.8 %collective-permute-start.4 = (bf16[320,640]{1,0:T(8,128)(2,1)}, bf16[320,640]{1,0:T(8,128)(2,1)}, u32[]{:S(2)}, u32[]{:S(2)}) collective-permute-start(bf16[320,640]{1,0:T(8,128)(2,1)} %get-tuple-element.51), channel_id=1, source_target_pairs={{1,2},{3,4},{5,6},{7,8},{9,10},{11,12},{13,14},{15,16},{17,18},{19... | collective-permute-start | bytes 1228808 | tf_op jit(solution)/shard_map/ppermute | solution.py:27
  70.2 21.1 %collective-permute-start.5 = (bf16[320,640]{1,0:T(8,128)(2,1)}, bf16[320,640]{1,0:T(8,128)(2,1)S(1)}, u32[]{:S(2)}, u32[]{:S(2)}) collective-permute-start(bf16[320,640]{1,0:T(8,128)(2,1)} %copy-done.7), channel_id=1, source_target_pairs={{0,510},{1,511},{2,0},{3,1},{4,2},{5,3},{6,4},{7,5},{8,6},{9,7},{1... | collective-permute-start | bytes 1228808 | tf_op jit(solution)/shard_map/ppermute | solution.py:27
  78.0 0.6 copy-start.4
  78.6 18.8 %all-to-all-start.2 = ((bf16[16,16,128]{2,1,0:T(8,128)(2,1)}), bf16[16,16,128]{2,1,0:T(8,128)(2,1)S(1)}, u32[]{:S(2)}, u32[]{:S(2)}) async-start(bf16[16,16,128]{2,1,0:T(8,128)(2,1)} %copy-done.4), calls=%async_computation.2 | async-start | bytes 131072 | tf_op jit(solution)/shard_map/all_to_all | solution.py:35
  86.1 1.1 copy-start.6
  87.3 4.0 %copy-start.3 = (bf16[320,640]{1,0:T(8,128)(2,1)S(1)}, bf16[320,640]{1,0:T(8,128)(2,1)}, u32[]{:S(2)}) copy-start(bf16[320,640]{1,0:T(8,128)(2,1)} %refs_2_.7) | copy-start | bytes 1228804
  114.1 4.2 %collective-permute-start.6 = (bf16[16,192,128]{2,1,0:T(8,128)(2,1)S(1)}, bf16[16,192,128]{2,1,0:T(8,128)(2,1)S(1)}, u32[]{:S(2)}, u32[]{:S(2)}) collective-permute-start(bf16[16,192,128]{2,1,0:T(8,128)(2,1)S(1)} %all_to_all.21.refs_1_), channel_id=1, source_target_pairs={{0,1},{1,0},{2,3},{3,2},{4,5},{5,4},{6,7},{7,6},{8,9},{9,8},{10,11... | collective-permute-start | bytes 2359304 | tf_op jit(solution)/shard_map/ppermute | solution.py:31

commit v5 on v4

--- a/solution.py
+++ b/solution.py
@@ -13,7 +13,7 @@
 HALF = D // 2
 AXES = ("zh", "zl", "x", "yh", "yl", "c")
 SIZES = (4, 2, 4, 4, 2, 2)
-CUBE = ("zl", "x", "yl")
+CUBE = ("x", "yl", "zl")
 GRID = ("zh", "yh")
 SIDE = 16
 TILES = 12
@@ -110,17 +110,19 @@
     turned[...] = im[...].T
 
 
-def prev_body(scal, core, texts, img_n, img_inv, img_b, d_near, turned,
-              part_sent, d_proj, d_own, d_other, prev_b, slope):
+def prev_body(scal, core, texts, img_n, img_inv, img_b, d_near, own_slope, turned,
+              part_sent, d_proj, d_own, d_other, prev_b, part_back, d_txt):
     text = normalize(texts[...].astype(f32))[0].astype(bf16)
     prev_b[...] = text
-    slope[...] = slope_of(img_b[...], text, scal).astype(bf16)
-    grad = dot(slope[...], text) + d_near[...]
+    slope = slope_of(img_b[...], text, scal).astype(bf16)
+    grad = dot(slope, text) + d_near[...]
     d_own[...] = grad[0:ROWS]
     d_other[...] = grad[ROWS:NEAR].astype(bf16)
     d_proj[...] = tangent(grad, img_n[...], img_inv[...]).astype(bf16)
     second = pl.multiple_of((1 - core[0]) * HALF, HALF)
     part_sent[...] = dot(turned[pl.ds(second, HALF), :], d_proj[...])
+    part_back[...] = t_dot(slope, img_b[...])
+    d_txt[...] = t_dot(own_slope[...], img_b[...])
 
 
 def next_body(scal, core, nxt, head, prev_b, part_sent, d_other, sent, d_proj, turned, slope, next_b, d_next):
@@ -137,12 +139,10 @@
     sent[HALF:, :] = d_other[...]
 
 
-def half_body(core, d_proj, turned, slope, own_slope, img_b, next_proj, next_turned, next_slope, next_b, d_next,
-              mine, back, d_txt, d_late):
+def half_body(core, d_proj, turned, next_proj, next_turned, next_slope, next_b, part_back, d_next, mine, back, d_late):
     rows = pl.ds(pl.multiple_of(core[0] * HALF, HALF), HALF)
-    back[...] = (t_dot(slope[...], img_b[...]) + t_dot(next_slope[...], next_b[...])).astype(bf16)
+    back[...] = (part_back[...] + t_dot(next_slope[...], next_b[...])).astype(bf16)
     d_late[...] = d_next[...]
-    d_txt[...] = t_dot(own_slope[...], img_b[...])
     mine[...] = dot(turned[rows, :], d_proj[...]) + dot(next_turned[rows, :], next_proj[...])
 
 
@@ -187,6 +187,10 @@
 def text_body(d_txt, back, texts, out):
     norm, inv = normalize(texts[...].astype(f32))
     out[...] = tangent(d_txt[...] + back[...].astype(f32), norm, inv).astype(bf16)
+
+
+def pass_body(parts, out):
+    out[...] = parts[...]
 
 
 def halves_body(core, mine, got, out):
@@ -214,21 +218,21 @@
         ((VMEM, (NEAR, E), f32), (VMEM, (NEAR, 1), f32), (VMEM, (NEAR, E), bf16), (VMEM, (NEAR, E), f32),
          (VMEM, (NEAR, ROWS), bf16), (VMEM, (D, NEAR), bf16)),
         (pltpu.VMEM((NEAR, D), bf16),), 100_000_000)
-    part_sent, d_proj, d_own, d_other, prev_b, slope = call(
+    part_sent, d_proj, d_own, d_other, prev_b, part_back, d_txt = call(
         prev_body, "prev",
         ((SMEM, scal), (SMEM, core), (VMEM, prev), (VMEM, img_n), (VMEM, img_inv), (VMEM, img_b), (VMEM, d_near),
-         (VMEM, turned)),
-        (rows, (VMEM, (NEAR, E), bf16), block, words, words, (VMEM, (NEAR, ROWS), bf16)), flops=40_000_000_000)
+         (VMEM, own_slope), (VMEM, turned)),
+        (rows, (VMEM, (NEAR, E), bf16), block, words, words, block, block), flops=40_000_000_000)
     sent, next_proj, next_turned, next_slope, next_b, d_next = call(
         next_body, "next",
         ((SMEM, scal), (SMEM, core), (VMEM, nxt), (VMEM, head), (VMEM, prev_b), (VMEM, part_sent), (VMEM, d_other)),
         ((VMEM, (HALF + ROWS, E), bf16), words, (VMEM, (D, ROWS), bf16), (VMEM, (ROWS, ROWS), bf16), words, words),
         flops=1_000_000_000)
-    mine, back, d_txt, d_next = call(
+    mine, back, d_next = call(
         half_body, "half",
-        ((SMEM, core), (VMEM, d_proj), (VMEM, turned), (VMEM, slope), (VMEM, own_slope), (VMEM, img_b), (VMEM, next_proj),
-         (VMEM, next_turned), (VMEM, next_slope), (VMEM, next_b), (VMEM, d_next)),
-        (rows, words, block, words), flops=1_300_000_000)
+        ((SMEM, core), (VMEM, d_proj), (VMEM, turned), (VMEM, next_proj), (VMEM, next_turned), (VMEM, next_slope),
+         (VMEM, next_b), (VMEM, part_back), (VMEM, d_next)),
+        (rows, words, words), flops=900_000_000)
     part, d_img = call(
         add_body, "add", ((VMEM, mine), (VMEM, swapped(sent)), (VMEM, d_own)),
         ((VMEM, (SIDE, TILES * 16, 128), bf16), block))
@@ -238,15 +242,16 @@
     tiles = call(
         grid_sum_body, "grid_sum", ((VMEM, exchange(tiles, GRID)),), ((VMEM, (SIDE, 16, 128), bf16),),
         flops=40_000_000_000)
-    grad_image, image_mark = call(
-        image_body, "image", ((VMEM, d_img), (VMEM, d_late), (VMEM, images), (VMEM, head)),
-        ((VMEM, (ROWS, D), bf16),), flops=960_000_000, mark=True)
-    grad_text, text_mark = call(
-        text_body, "text", ((VMEM, d_txt), (VMEM, d_back), (VMEM, texts)), (words,), after=(image_mark,), mark=True)
+    grad_text, mark = call(
+        text_body, "text", ((VMEM, d_txt), (VMEM, d_back), (VMEM, texts)), (words,), mark=True)
     part = call(
         cube_spread_body, "cube_spread", ((VMEM, exchange(tiles, GRID)),),
-        ((VMEM, (SIDE, TILES * 16, 128), bf16),), after=(text_mark,))
-    part = exchange(part, CUBE)
+        ((VMEM, (SIDE, TILES * 16, 128), bf16),), flops=40_000_000_000, after=(mark,))
+    grad_image, mark = call(
+        image_body, "image", ((VMEM, d_img), (VMEM, d_late), (VMEM, images), (VMEM, head)),
+        ((VMEM, (ROWS, D), bf16),), flops=40_000_000_000, mark=True)
+    part = call(
+        pass_body, "pass", ((VMEM, exchange(part, CUBE)),), ((VMEM, (SIDE, TILES * 16, 128), bf16),), after=(mark,))
     grad_head = call(
         halves_body, "halves", ((SMEM, core), (VMEM, part), (VMEM, swapped(part))), ((VMEM, (D, E), bf16),))
     return (grad_image, grad_text, grad_head)

time: 120 us -> 118 us (0.983)
  blocking collectives: 30.9 us -> 15 us
  waiting for transfers between devices: 15.5 us -> 22.9 us
  starting transfers between devices: 43.9 us -> 50.8 us
    all_to_all x2 -> x1, blocking collectives: 30.9 us -> 15 us  [exchange(): return lax.all_to_all(value, axes, 0, 0)]
    all_to_all x2 -> x3, waiting for transfers between devices: 4.45 us -> 10.5 us  [exchange(): return lax.all_to_all(value, axes, 0, 0)]
    ppermute x3, starting transfers between devices: 13.4 us -> 18.8 us  [swapped(): return lax.ppermute(value, 'c', [(0, 1), (1, 0)])]
    ppermute x4, starting transfers between devices: 16.8 us -> 18.1 us  [shifted(): lax.ppermute(value, AXES, [(s, (s + steps) % COUNT) for s in sources])]
    unnamed x16 -> x18, local copies, waits for them, and re-layouts: 4.16 us -> 3.89 us
    all_to_all x2 -> x3, starting transfers between devices: 13.7 us -> 13.9 us  [exchange(): return lax.all_to_all(value, axes, 0, 0)]
    pallas_call x12 -> x13, Pallas kernels: 22.9 us -> 22.9 us  [call(): pl.pallas_call(run, out_shape=tuple((jax.ShapeDtypeStruct(dims, dtype) fo...]
  transfers between devices with their start and end apart: 9 -> 10, of which waited for: 3 -> 6; matrix products, arithmetic and copies ran while one was open for 0% -> 0% of each run, Pallas kernels for 14% -> 14%
where the time goes in v5:
time: 118 us
  starting transfers between devices  50.8 us (43%)
  Pallas kernels  22.9 us (19%)
  waiting for transfers between devices  22.9 us (19%)
  blocking collectives  15 us (13%)
  local copies, waits for them, and re-layouts  3.89 us (3%)
  between operations  2.19 us (2%)
    pallas_call x13, Pallas kernels, call(): pl.pallas_call(run, out_shape=tuple((jax.ShapeDtypeStruct(dims, dtype) fo...  22.9 us
    ppermute x3, starting transfers between devices, swapped(): return lax.ppermute(value, 'c', [(0, 1), (1, 0)])  18.8 us
    ppermute x4, starting transfers between devices, shifted(): lax.ppermute(value, AXES, [(s, (s + steps) % COUNT) for s in sources])  18.1 us
    all_to_all x1, blocking collectives, exchange(): return lax.all_to_all(value, axes, 0, 0)  15 us
    all_to_all x3, starting transfers between devices, exchange(): return lax.all_to_all(value, axes, 0, 0)  13.9 us
    all_to_all x3, waiting for transfers between devices, exchange(): return lax.all_to_all(value, axes, 0, 0)  10.5 us
    ppermute x4, waiting for transfers between devices, shifted(): lax.ppermute(value, AXES, [(s, (s + steps) % COUNT) for s in sources])  9.57 us
    unnamed x18, local copies, waits for them, and re-layouts  3.89 us
  transfers between devices with their start and end apart: 10, of which 6 were waited for; matrix products, arithmetic and copies ran while one was open for 0% of the time, Pallas kernels for 14%

profile of v5, /device:TPU:1, one launch (start us, length us, event | category | flops | bytes accessed | tf_op | source)
XLA Modules:
  0.0 117.8 jit_solution(4908237976305642517)
XLA Ops:
  0.6 8.8 %collective-permute-start.1 = (bf16[320,1152]{1,0:T(8,128)(2,1)}, bf16[320,1152]{1,0:T(8,128)(2,1)S(1)}, u32[]{:S(2)}, u32[]{:S(2)}) collective-permute-start(bf16[320,1152]{1,0:T(8,128)(2,1)} %refs_2_.6), channel_id=1, source_target_pairs={{0,1},{1,0},{2,3},{3,2},{4,5},{5,4},{6,7},{7,6},{8,9},{9,8},{10,11... | collective-permute-start | bytes 2211848 | tf_op jit(solution)/shard_map/ppermute | solution.py:31
  9.4 1.9 %collective-permute-start = (bf16[320,640]{1,0:T(8,128)(2,1)}, bf16[320,640]{1,0:T(8,128)(2,1)S(1)}, u32[]{:S(2)}, u32[]{:S(2)}) collective-permute-start(bf16[320,640]{1,0:T(8,128)(2,1)} %refs_2_.7), channel_id=1, source_target_pairs={{0,2},{1,3},{2,4},{3,5},{4,6},{5,7},{6,8},{7,9},{8,10},{9,11},{10,... | collective-permute-start | bytes 1228808 | tf_op jit(solution)/shard_map/ppermute | solution.py:27
  11.4 1.3 %collective-permute-start.2 = (bf16[320,1152]{1,0:T(8,128)(2,1)}, bf16[320,1152]{1,0:T(8,128)(2,1)S(1)}, u32[]{:S(2)}, u32[]{:S(2)}) collective-permute-start(bf16[320,1152]{1,0:T(8,128)(2,1)} %refs_2_.6), channel_id=1, source_target_pairs={{0,511},{2,1},{4,3},{6,5},{8,7},{10,9},{12,11},{14,13},{16,15},{18... | collective-permute-start | bytes 2211848 | tf_op jit(solution)/shard_map/ppermute | solution.py:27
  14.0 0.1 pad_maximum_fusion.refs_0_
  14.1 0.0 copy-start.3
  14.1 1.0 copy-done.3
  15.1 0.0 copy-start
  15.1 0.0 copy-start.1
  15.1 0.7 words.1.refs_4_
  15.8 0.0 collective-permute-done.1.refs_3_
  15.8 0.7 copy-done
  16.4 0.2 copy-done.1
  16.6 3.7 %near.1 = (f32[640,640]{1,0:T(8,128)S(1)}, f32[640,1]{1,0:T(8,128)S(1)}, bf16[640,640]{1,0:T(8,128)(2,1)S(1)}, f32[640,640]{1,0:T(8,128)S(1)}, bf16[640,320]{1,0...) custom-call(f32[2]{0:T(128)S(1)} %pad_maximum_fusion.refs_0_, s32[1]{0:T(128)} %bitcast.refs_1_.refs_0_, ...), custom_call_target="tpu_custom_call" | custom-call | flops 100000000 | bytes 3358720 | tf_op jit(solution)/shard_map/near/pallas_call | solution.py:54
  20.3 9.6 %collective-permute-done.refs_2_ = bf16[320,640]{1,0:T(8,128)(2,1)S(1)} collective-permute-done((bf16[320,640]{1,0:T(8,128)(2,1)}, bf16[320,640]{1,0:T(8,128)(2,1)S(1)}, u32[]{:S(2)}, u32[]{:S(2)}) %collective-permute-start) | collective-permute-done | bytes 409632 | tf_op jit(solution)/shard_map/ppermute | solution.py:27
  29.9 3.6 %prev.1 = (f32[576,640]{1,0:T(8,128)S(1)}, bf16[640,640]{1,0:T(8,128)(2,1)S(1)}, f32[320,640]{1,0:T(8,128)S(1)}, bf16[320,640]{1,0:T(8,128)(2,1)S(1)}, bf16[320,...) custom-call(f32[2]{0:T(128)S(1)} %pad_maximum_fusion.refs_0_, s32[1]{0:T(128)} %bitcast.refs_1_.refs_0_, ...), custom_call_target="tpu_custom_call" | custom-call | flops 40000000000 | bytes 6392320 | tf_op jit(solution)/shard_map/prev/pallas_call | solution.py:54
  33.5 0.0 collective-permute-done.2.refs_2_
  33.5 3.1 %next.1 = (bf16[896,640]{1,0:T(8,128)(2,1)S(1)}, bf16[320,640]{1,0:T(8,128)(2,1)S(1)}, bf16[1152,320]{1,0:T(8,128)(2,1)S(1)}, bf16[320,320]{1,0:T(8,128)(2,1)S(1...) custom-call(f32[2]{0:T(128)S(1)} %pad_maximum_fusion.refs_0_, s32[1]{0:T(128)} %bitcast.refs_1_.refs_0_, ...), custom_call_target="tpu_custom_call" | custom-call | flops 1000000000 | bytes 4505600 | tf_op jit(solution)/shard_map/next/pallas_call | solution.py:54
  36.6 2.5 %collective-permute-start.3 = (bf16[896,640]{1,0:T(8,128)(2,1)S(1)}, bf16[896,640]{1,0:T(8,128)(2,1)S(1)}, u32[]{:S(2)}, u32[]{:S(2)}) collective-permute-start(bf16[896,640]{1,0:T(8,128)(2,1)S(1)} %get-tuple-element.48), channel_id=1, source_target_pairs={{0,1},{1,0},{2,3},{3,2},{4,5},{5,4},{6,7},{7,6},{8,9},{9,8},{10,11... | collective-permute-start | bytes 3440648 | tf_op jit(solution)/shard_map/ppermute | solution.py:31
  39.1 1.5 %half.1 = (f32[576,640]{1,0:T(8,128)S(1)}, bf16[320,640]{1,0:T(8,128)(2,1)S(1)}, bf16[320,640]{1,0:T(8,128)(2,1)S(1)}) custom-call(s32[1]{0:T(128)} %bitcast.refs_1_.refs_0_, bf16[640,640]{1,0:T(8,128)(2,1)S(1)} %get-tuple-element.37.refs_1_, bf16[1152,640]{1,0:T(8,128)(2,1)S(1)} %get-tuple-element.36.refs_8_.refs_2_, ...), custom_call_target="tpu_custom_call" | custom-call | flops 900000000 | bytes 5283840 | tf_op jit(solution)/shard_map/half/pallas_call | solution.py:54
  40.6 0.0 copy-start.7
  40.6 0.0 copy-start.8
  40.7 0.9 collective-permute-done.3.refs_1_
  41.5 0.2 add.1
  41.7 0.0 copy-done.7
  41.7 0.0 copy-done.8
  41.7 0.0 copy-start.5
  41.8 0.9 copy-done.5
  42.6 15.0 %all_to_all.20.refs_0_ = bf16[16,192,128]{2,1,0:T(8,128)(2,1)S(1)} all-to-all(bf16[16,192,128]{2,1,0:T(8,128)(2,1)S(1)} %get-tuple-element.56), channel_id=1, replica_groups=mesh['zh'=4,'zl'=2,'x'=4,'yh'=4,'yl'=2,'c'=2] {'x','yl','zl'}, dimensions={0} | all-to-all | bytes 1572864 | tf_op jit(solution)/shard_map/all_to_all | solution.py:35
  57.6 0.7 cube_sum.1
  58.4 6.5 %all-to-all-start.1 = ((bf16[16,16,128]{2,1,0:T(8,128)(2,1)}), bf16[16,16,128]{2,1,0:T(8,128)(2,1)S(1)}, u32[]{:S(2)}, u32[]{:S(2)}) async-start(bf16[16,16,128]{2,1,0:T(8,128)(2,1)} %cube_sum.1), calls=%async_computation.1 | async-start | bytes 131072 | tf_op jit(solution)/shard_map/all_to_all | solution.py:35
  64.9 0.0 copy-start.4
  64.9 8.1 %collective-permute-start.5 = (bf16[320,640]{1,0:T(8,128)(2,1)}, bf16[320,640]{1,0:T(8,128)(2,1)S(1)}, u32[]{:S(2)}, u32[]{:S(2)}) collective-permute-start(bf16[320,640]{1,0:T(8,128)(2,1)} %copy-done.8), channel_id=1, source_target_pairs={{0,510},{1,511},{2,0},{3,1},{4,2},{5,3},{6,4},{7,5},{8,6},{9,7},{1... | collective-permute-start | bytes 1228808 | tf_op jit(solution)/shard_map/ppermute | solution.py:27
  73.0 3.2 %all-to-all-done.1.refs_0_ = bf16[16,16,128]{2,1,0:T(8,128)(2,1)S(1)} async-done(((bf16[16,16,128]{2,1,0:T(8,128)(2,1)}), bf16[16,16,128]{2,1,0:T(8,128)(2,1)S(1)}, u32[]{:S(2)}, u32[]{:S(2)}) %all-to-all-start.1) | async-done | bytes 65568 | tf_op jit(solution)/shard_map/all_to_all | solution.py:35
  76.2 0.6 grid_sum.1
  76.9 3.5 %all-to-all-start.2 = ((bf16[16,16,128]{2,1,0:T(8,128)(2,1)}), bf16[16,16,128]{2,1,0:T(8,128)(2,1)S(1)}, u32[]{:S(2)}, u32[]{:S(2)}) async-start(bf16[16,16,128]{2,1,0:T(8,128)(2,1)} %grid_sum.1), calls=%async_computation.2 | async-start | bytes 131072 | tf_op jit(solution)/shard_map/all_to_all | solution.py:35
  80.4 6.7 %collective-permute-start.4 = (bf16[320,640]{1,0:T(8,128)(2,1)}, bf16[320,640]{1,0:T(8,128)(2,1)}, u32[]{:S(2)}, u32[]{:S(2)}) collective-permute-start(bf16[320,640]{1,0:T(8,128)(2,1)} %copy-done.7), channel_id=1, source_target_pairs={{1,2},{3,4},{5,6},{7,8},{9,10},{11,12},{13,14},{15,16},{17,18},{19... | collective-permute-start | bytes 1228808 | tf_op jit(solution)/shard_map/ppermute | solution.py:27
  87.1 0.0 collective-permute-done.5.refs_1_
  87.1 0.0 copy-done.4
  87.1 1.1 text.1
  88.2 3.4 %all-to-all-done.2.refs_0_ = bf16[16,16,128]{2,1,0:T(8,128)(2,1)S(1)} async-done(((bf16[16,16,128]{2,1,0:T(8,128)(2,1)}), bf16[16,16,128]{2,1,0:T(8,128)(2,1)S(1)}, u32[]{:S(2)}, u32[]{:S(2)}) %all-to-all-start.2) | async-done | bytes 65568 | tf_op jit(solution)/shard_map/all_to_all | solution.py:35
  91.6 1.7 %cube_spread.1 = bf16[16,192,128]{2,1,0:T(8,128)(2,1)} custom-call(bf16[16,16,128]{2,1,0:T(8,128)(2,1)S(1)} %all-to-all-done.2.refs_0_, s32[1]{0:T(128)} %get-tuple-element.57.refs_1_), custom_call_target="tpu_custom_call" | custom-call | flops 40000000000 | bytes 65536 | tf_op jit(solution)/shard_map/cube_spread/pallas_call | solution.py:54
  93.3 0.0 copy-start.2
  93.3 3.9 %all-to-all-start.3 = ((bf16[16,192,128]{2,1,0:T(8,128)(2,1)}), bf16[16,192,128]{2,1,0:T(8,128)(2,1)S(1)}, u32[]{:S(2)}, u32[]{:S(2)}) async-start(bf16[16,192,128]{2,1,0:T(8,128)(2,1)} %cube_spread.1), calls=%async_computation.3 | async-start | bytes 1572864 | tf_op jit(solution)/shard_map/all_to_all | solution.py:35
  97.2 0.0 collective-permute-done.4.refs_1_
  97.3 0.0 copy-done.2
  97.3 0.0 copy-start.6
  97.3 1.1 copy-done.6
  98.4 3.9 %image.1 = (bf16[320,1152]{1,0:T(8,128)(2,1)}, s32[1]{0:T(128)}) custom-call(f32[320,640]{1,0:T(8,128)S(1)} %copy-done.6, bf16[320,640]{1,0:T(8,128)(2,1)} %collective-permute-done.4.refs_1_, bf16[320,1152]{1,0:T(8,128)(2,1)S(1)} %copy-done.2, bf16[1152,640]{1,0:T(8,128)(2,1)S(1)} %copy-done), custom_call_target="tpu_custom_call" | custom-call | flops 40000000000 | bytes 3440640 | tf_op jit(solution)/shard_map/image/pallas_call | solution.py:54
  102.3 3.9 %all-to-all-done.3.refs_0_ = bf16[16,192,128]{2,1,0:T(8,128)(2,1)S(1)} async-done(((bf16[16,192,128]{2,1,0:T(8,128)(2,1)}), bf16[16,192,128]{2,1,0:T(8,128)(2,1)S(1)}, u32[]{:S(2)}, u32[]{:S(2)}) %all-to-all-start.3) | async-done | bytes 786464 | tf_op jit(solution)/shard_map/all_to_all | solution.py:35
  106.3 0.7 pass.1.refs_1_
  107.0 7.5 %collective-permute-start.6 = (bf16[16,192,128]{2,1,0:T(8,128)(2,1)S(1)}, bf16[16,192,128]{2,1,0:T(8,128)(2,1)S(1)}, u32[]{:S(2)}, u32[]{:S(2)}) collective-permute-start(bf16[16,192,128]{2,1,0:T(8,128)(2,1)S(1)} %pass.1.refs_1_), channel_id=1, source_target_pairs={{0,1},{1,0},{2,3},{3,2},{4,5},{5,4},{6,7},{7,6},{8,9},{9,8},{10,11... | collective-permute-start | bytes 2359304 | tf_op jit(solution)/shard_map/ppermute | solution.py:31
  114.5 1.9 %collective-permute-done.6.refs_2_ = bf16[16,192,128]{2,1,0:T(8,128)(2,1)S(1)} collective-permute-done((bf16[16,192,128]{2,1,0:T(8,128)(2,1)S(1)}, bf16[16,192,128]{2,1,0:T(8,128)(2,1)S(1)}, u32[]{:S(2)}, u32[]{:S(2)}) %collective-permute-start.6) | collective-permute-done | bytes 786464 | tf_op jit(solution)/shard_map/ppermute | solution.py:31
  116.4 1.4 %halves.1 = bf16[1152,640]{1,0:T(8,128)(2,1)} custom-call(s32[1]{0:T(128)} %bitcast.refs_1_.refs_0_, bf16[16,192,128]{2,1,0:T(8,128)(2,1)S(1)} %pass.1.refs_1_, bf16[16,192,128]{2,1,0:T(8,128)(2,1)S(1)} %collective-permute-done.6.refs_2_), custom_call_target="tpu_custom_call" | custom-call | bytes 1572864 | tf_op jit(solution)/shard_map/halves/pallas_call | solution.py:54
Async XLA Ops:
  0.6 15.2 %collective-permute-start.1 = (bf16[320,1152]{1,0:T(8,128)(2,1)}, bf16[320,1152]{1,0:T(8,128)(2,1)S(1)}, u32[]{:S(2)}, u32[]{:S(2)}) collective-permute-start(bf16[320,1152]{1,0:T(8,128)(2,1)} %refs_2_.6), channel_id=1, source_target_pairs={{0,1},{1,0},{2,3},{3,2},{4,5},{5,4},{6,7},{7,6},{8,9},{9,8},{10,11... | collective-permute-start | bytes 2211848 | tf_op jit(solution)/shard_map/ppermute | solution.py:31
  9.4 20.4 %collective-permute-start = (bf16[320,640]{1,0:T(8,128)(2,1)}, bf16[320,640]{1,0:T(8,128)(2,1)S(1)}, u32[]{:S(2)}, u32[]{:S(2)}) collective-permute-start(bf16[320,640]{1,0:T(8,128)(2,1)} %refs_2_.7), channel_id=1, source_target_pairs={{0,2},{1,3},{2,4},{3,5},{4,6},{5,7},{6,8},{7,9},{8,10},{9,11},{10,... | collective-permute-start | bytes 1228808 | tf_op jit(solution)/shard_map/ppermute | solution.py:27
  11.4 22.2 %collective-permute-start.2 = (bf16[320,1152]{1,0:T(8,128)(2,1)}, bf16[320,1152]{1,0:T(8,128)(2,1)S(1)}, u32[]{:S(2)}, u32[]{:S(2)}) collective-permute-start(bf16[320,1152]{1,0:T(8,128)(2,1)} %refs_2_.6), channel_id=1, source_target_pairs={{0,511},{2,1},{4,3},{6,5},{8,7},{10,9},{12,11},{14,13},{16,15},{18... | collective-permute-start | bytes 2211848 | tf_op jit(solution)/shard_map/ppermute | solution.py:27
  14.1 1.0 copy-start.3
  15.1 1.4 %copy-start = (bf16[1152,640]{1,0:T(8,128)(2,1)S(1)}, bf16[1152,640]{1,0:T(8,128)(2,1)}, u32[]{:S(2)}) copy-start(bf16[1152,640]{1,0:T(8,128)(2,1)} %refs_3_.3) | copy-start | bytes 4423684
  15.1 1.6 %copy-start.1 = (bf16[320,1152]{1,0:T(8,128)(2,1)S(1)}, bf16[320,1152]{1,0:T(8,128)(2,1)}, u32[]{:S(2)}) copy-start(bf16[320,1152]{1,0:T(8,128)(2,1)} %refs_2_.6) | copy-start | bytes 2211844
  36.6 4.9 %collective-permute-start.3 = (bf16[896,640]{1,0:T(8,128)(2,1)S(1)}, bf16[896,640]{1,0:T(8,128)(2,1)S(1)}, u32[]{:S(2)}, u32[]{:S(2)}) collective-permute-start(bf16[896,640]{1,0:T(8,128)(2,1)S(1)} %get-tuple-element.48), channel_id=1, source_target_pairs={{0,1},{1,0},{2,3},{3,2},{4,5},{5,4},{6,7},{7,6},{8,9},{9,8},{10,11... | collective-permute-start | bytes 3440648 | tf_op jit(solution)/shard_map/ppermute | solution.py:31
  40.6 1.1 copy-start.7
  40.6 1.1 copy-start.8
  41.7 0.9 copy-start.5
  58.4 17.9 %all-to-all-start.1 = ((bf16[16,16,128]{2,1,0:T(8,128)(2,1)}), bf16[16,16,128]{2,1,0:T(8,128)(2,1)S(1)}, u32[]{:S(2)}, u32[]{:S(2)}) async-start(bf16[16,16,128]{2,1,0:T(8,128)(2,1)} %cube_sum.1), calls=%async_computation.1 | async-start | bytes 131072 | tf_op jit(solution)/shard_map/all_to_all | solution.py:35
  64.9 22.3 %copy-start.4 = (bf16[320,640]{1,0:T(8,128)(2,1)S(1)}, bf16[320,640]{1,0:T(8,128)(2,1)}, u32[]{:S(2)}) copy-start(bf16[320,640]{1,0:T(8,128)(2,1)} %refs_2_.7) | copy-start | bytes 1228804
  64.9 22.2 %collective-permute-start.5 = (bf16[320,640]{1,0:T(8,128)(2,1)}, bf16[320,640]{1,0:T(8,128)(2,1)S(1)}, u32[]{:S(2)}, u32[]{:S(2)}) collective-permute-start(bf16[320,640]{1,0:T(8,128)(2,1)} %copy-done.8), channel_id=1, source_target_pairs={{0,510},{1,511},{2,0},{3,1},{4,2},{5,3},{6,4},{7,5},{8,6},{9,7},{1... | collective-permute-start | bytes 1228808 | tf_op jit(solution)/shard_map/ppermute | solution.py:27
  76.9 14.7 %all-to-all-start.2 = ((bf16[16,16,128]{2,1,0:T(8,128)(2,1)}), bf16[16,16,128]{2,1,0:T(8,128)(2,1)S(1)}, u32[]{:S(2)}, u32[]{:S(2)}) async-start(bf16[16,16,128]{2,1,0:T(8,128)(2,1)} %grid_sum.1), calls=%async_computation.2 | async-start | bytes 131072 | tf_op jit(solution)/shard_map/all_to_all | solution.py:35
  80.4 16.9 %collective-permute-start.4 = (bf16[320,640]{1,0:T(8,128)(2,1)}, bf16[320,640]{1,0:T(8,128)(2,1)}, u32[]{:S(2)}, u32[]{:S(2)}) collective-permute-start(bf16[320,640]{1,0:T(8,128)(2,1)} %copy-done.7), channel_id=1, source_target_pairs={{1,2},{3,4},{5,6},{7,8},{9,10},{11,12},{13,14},{15,16},{17,18},{19... | collective-permute-start | bytes 1228808 | tf_op jit(solution)/shard_map/ppermute | solution.py:27
  93.3 4.0 %copy-start.2 = (bf16[320,1152]{1,0:T(8,128)(2,1)S(1)}, bf16[320,1152]{1,0:T(8,128)(2,1)}, u32[]{:S(2)}) copy-start(bf16[320,1152]{1,0:T(8,128)(2,1)} %refs_2_.6) | copy-start | bytes 2211844
  93.3 13.0 %all-to-all-start.3 = ((bf16[16,192,128]{2,1,0:T(8,128)(2,1)}), bf16[16,192,128]{2,1,0:T(8,128)(2,1)S(1)}, u32[]{:S(2)}, u32[]{:S(2)}) async-start(bf16[16,192,128]{2,1,0:T(8,128)(2,1)} %cube_spread.1), calls=%async_computation.3 | async-start | bytes 1572864 | tf_op jit(solution)/shard_map/all_to_all | solution.py:35
  97.3 1.1 copy-start.6
  107.0 9.4 %collective-permute-start.6 = (bf16[16,192,128]{2,1,0:T(8,128)(2,1)S(1)}, bf16[16,192,128]{2,1,0:T(8,128)(2,1)S(1)}, u32[]{:S(2)}, u32[]{:S(2)}) collective-permute-start(bf16[16,192,128]{2,1,0:T(8,128)(2,1)S(1)} %pass.1.refs_1_), channel_id=1, source_target_pairs={{0,1},{1,0},{2,3},{3,2},{4,5},{5,4},{6,7},{7,6},{8,9},{9,8},{10,11... | collective-permute-start | bytes 2359304 | tf_op jit(solution)/shard_map/ppermute | solution.py:31

commit v6 on v5

--- a/solution.py
+++ b/solution.py
@@ -193,12 +193,36 @@
     out[...] = parts[...]
 
 
-def halves_body(core, mine, got, out):
-    first = core[0] * HALF
-    second = HALF - first
+def put_half(parts, out, start, half, sem):
     for row, cols, p, rows in tiles_of():
-        out[pl.ds(pl.multiple_of(first + row, 16), 16), cols] = mine[p, rows, :]
-        out[pl.ds(pl.multiple_of(second + row, 16), 16), cols] = got[p, rows, :]
+        half[row : row + 16, cols] = parts[p, rows, :]
+    rows = pl.ds(pl.multiple_of(start, HALF), HALF)
+    copy = pltpu.make_async_copy(half, out.at[rows, :], sem)
+    copy.start()
+    copy.wait()
+
+
+def first_body(core, parts, out, half, sem):
+    put_half(parts, out, core[0] * HALF, half, sem)
+
+
+def second_body(core, parts, held, out, half, sem):
+    put_half(parts, out, (1 - core[0]) * HALF, half, sem)
+
+
+def halves(core, mine, got):
+    anywhere = pl.BlockSpec(memory_space=pl.ANY)
+    common = dict(
+        out_shape=jax.ShapeDtypeStruct((D, E), bf16),
+        out_specs=anywhere,
+        scratch_shapes=[pltpu.VMEM((HALF, E), bf16), pltpu.SemaphoreType.DMA],
+        compiler_params=pltpu.CompilerParams(vmem_limit_bytes=16_000_000),
+        cost_estimate=pl.CostEstimate(flops=0, bytes_accessed=HALF * E * 4, transcendentals=0),
+    )
+    held = pl.pallas_call(first_body, in_specs=[SMEM, VMEM], name="first_half", **common)(core, mine)
+    return pl.pallas_call(
+        second_body, in_specs=[SMEM, VMEM, anywhere], input_output_aliases={2: 0}, name="second_half", **common
+    )(core, got, held)
 
 
 def shards(images, texts, head, log_scale, bias):
@@ -252,8 +276,7 @@
         ((VMEM, (ROWS, D), bf16),), flops=40_000_000_000, mark=True)
     part = call(
         pass_body, "pass", ((VMEM, exchange(part, CUBE)),), ((VMEM, (SIDE, TILES * 16, 128), bf16),), after=(mark,))
-    grad_head = call(
-        halves_body, "halves", ((SMEM, core), (VMEM, part), (VMEM, swapped(part))), ((VMEM, (D, E), bf16),))
+    grad_head = halves(core, part, swapped(part))
     return (grad_image, grad_text, grad_head)
 
 

time: 118 us -> 118 us (level)
    pallas_call x0 -> x2, Pallas kernels: none -> 1.96 us  [the longest x1 0.98 us: halves(): pl.pallas_call(first_body, in_specs=[SMEM, VMEM], name='first_half', **co...]
    pallas_call x13 -> x12, Pallas kernels: 22.9 us -> 21.5 us  [call(): pl.pallas_call(run, out_shape=tuple((jax.ShapeDtypeStruct(dims, dtype) fo...]
  transfers between devices with their start and end apart: 10 -> 10, of which waited for: 6 -> 6; matrix products, arithmetic and copies ran while one was open for 0% -> 0% of each run, Pallas kernels for 14% -> 15%
where the time goes in v6:
time: 118 us; the launch traced here: 117 us
  starting transfers between devices  50.8 us (43%)
  Pallas kernels  23.5 us (20%)
  waiting for transfers between devices  21.9 us (19%)
  blocking collectives  15 us (13%)
  local copies, waits for them, and re-layouts  3.89 us (3%)
  between operations  2.19 us (2%)
    pallas_call x12, Pallas kernels, call(): pl.pallas_call(run, out_shape=tuple((jax.ShapeDtypeStruct(dims, dtype) fo...  21.5 us
    ppermute x3, starting transfers between devices, swapped(): return lax.ppermute(value, 'c', [(0, 1), (1, 0)])  18.8 us
    ppermute x4, starting transfers between devices, shifted(): lax.ppermute(value, AXES, [(s, (s + steps) % COUNT) for s in sources])  18.1 us
    all_to_all x1, blocking collectives, exchange(): return lax.all_to_all(value, axes, 0, 0)  15 us
    all_to_all x3, starting transfers between devices, exchange(): return lax.all_to_all(value, axes, 0, 0)  13.9 us
    all_to_all x3, waiting for transfers between devices, exchange(): return lax.all_to_all(value, axes, 0, 0)  10.5 us
    ppermute x4, waiting for transfers between devices, shifted(): lax.ppermute(value, AXES, [(s, (s + steps) % COUNT) for s in sources])  9.57 us
    unnamed x18, local copies, waits for them, and re-layouts  3.89 us
  transfers between devices with their start and end apart: 10, of which 6 were waited for; matrix products, arithmetic and copies ran while one was open for 0% of the time, Pallas kernels for 15%

profile of v6, /device:TPU:1, one launch (start us, length us, event | category | flops | bytes accessed | tf_op | source)
XLA Modules:
  0.0 117.4 jit_solution(14556134600077250093)
XLA Ops:
  0.6 8.8 %collective-permute-start.1 = (bf16[320,1152]{1,0:T(8,128)(2,1)}, bf16[320,1152]{1,0:T(8,128)(2,1)S(1)}, u32[]{:S(2)}, u32[]{:S(2)}) collective-permute-start(bf16[320,1152]{1,0:T(8,128)(2,1)} %refs_2_.6), channel_id=1, source_target_pairs={{0,1},{1,0},{2,3},{3,2},{4,5},{5,4},{6,7},{7,6},{8,9},{9,8},{10,11... | collective-permute-start | bytes 2211848 | tf_op jit(solution)/shard_map/ppermute | solution.py:31
  9.4 1.9 %collective-permute-start = (bf16[320,640]{1,0:T(8,128)(2,1)}, bf16[320,640]{1,0:T(8,128)(2,1)S(1)}, u32[]{:S(2)}, u32[]{:S(2)}) collective-permute-start(bf16[320,640]{1,0:T(8,128)(2,1)} %refs_2_.7), channel_id=1, source_target_pairs={{0,2},{1,3},{2,4},{3,5},{4,6},{5,7},{6,8},{7,9},{8,10},{9,11},{10,... | collective-permute-start | bytes 1228808 | tf_op jit(solution)/shard_map/ppermute | solution.py:27
  11.4 1.3 %collective-permute-start.2 = (bf16[320,1152]{1,0:T(8,128)(2,1)}, bf16[320,1152]{1,0:T(8,128)(2,1)S(1)}, u32[]{:S(2)}, u32[]{:S(2)}) collective-permute-start(bf16[320,1152]{1,0:T(8,128)(2,1)} %refs_2_.6), channel_id=1, source_target_pairs={{0,511},{2,1},{4,3},{6,5},{8,7},{10,9},{12,11},{14,13},{16,15},{18... | collective-permute-start | bytes 2211848 | tf_op jit(solution)/shard_map/ppermute | solution.py:27
  14.0 0.1 pad_maximum_fusion.refs_0_
  14.1 0.0 copy-start.3
  14.1 1.0 copy-done.3
  15.1 0.0 copy-start
  15.1 0.0 copy-start.1
  15.1 0.7 words.1.refs_4_
  15.8 0.0 collective-permute-done.1.refs_3_
  15.8 0.7 copy-done
  16.4 0.2 copy-done.1
  16.6 3.7 %near.1 = (f32[640,640]{1,0:T(8,128)S(1)}, f32[640,1]{1,0:T(8,128)S(1)}, bf16[640,640]{1,0:T(8,128)(2,1)S(1)}, f32[640,640]{1,0:T(8,128)S(1)}, bf16[640,320]{1,0...) custom-call(f32[2]{0:T(128)S(1)} %pad_maximum_fusion.refs_0_, s32[1]{0:T(128)} %bitcast.refs_1_.refs_0_.core, ...), custom_call_target="tpu_custom_call" | custom-call | flops 100000000 | bytes 3358720 | tf_op jit(solution)/shard_map/near/pallas_call | solution.py:54
  20.3 9.6 %collective-permute-done.refs_2_ = bf16[320,640]{1,0:T(8,128)(2,1)S(1)} collective-permute-done((bf16[320,640]{1,0:T(8,128)(2,1)}, bf16[320,640]{1,0:T(8,128)(2,1)S(1)}, u32[]{:S(2)}, u32[]{:S(2)}) %collective-permute-start) | collective-permute-done | bytes 409632 | tf_op jit(solution)/shard_map/ppermute | solution.py:27
  29.9 3.6 %prev.1 = (f32[576,640]{1,0:T(8,128)S(1)}, bf16[640,640]{1,0:T(8,128)(2,1)S(1)}, f32[320,640]{1,0:T(8,128)S(1)}, bf16[320,640]{1,0:T(8,128)(2,1)S(1)}, bf16[320,...) custom-call(f32[2]{0:T(128)S(1)} %pad_maximum_fusion.refs_0_, s32[1]{0:T(128)} %bitcast.refs_1_.refs_0_.core, ...), custom_call_target="tpu_custom_call" | custom-call | flops 40000000000 | bytes 6392320 | tf_op jit(solution)/shard_map/prev/pallas_call | solution.py:54
  33.5 0.0 collective-permute-done.2.refs_2_
  33.5 3.1 %next.1 = (bf16[896,640]{1,0:T(8,128)(2,1)S(1)}, bf16[320,640]{1,0:T(8,128)(2,1)S(1)}, bf16[1152,320]{1,0:T(8,128)(2,1)S(1)}, bf16[320,320]{1,0:T(8,128)(2,1)S(1...) custom-call(f32[2]{0:T(128)S(1)} %pad_maximum_fusion.refs_0_, s32[1]{0:T(128)} %bitcast.refs_1_.refs_0_.core, ...), custom_call_target="tpu_custom_call" | custom-call | flops 1000000000 | bytes 4505600 | tf_op jit(solution)/shard_map/next/pallas_call | solution.py:54
  36.6 2.5 %collective-permute-start.3 = (bf16[896,640]{1,0:T(8,128)(2,1)S(1)}, bf16[896,640]{1,0:T(8,128)(2,1)S(1)}, u32[]{:S(2)}, u32[]{:S(2)}) collective-permute-start(bf16[896,640]{1,0:T(8,128)(2,1)S(1)} %get-tuple-element.48), channel_id=1, source_target_pairs={{0,1},{1,0},{2,3},{3,2},{4,5},{5,4},{6,7},{7,6},{8,9},{9,8},{10,11... | collective-permute-start | bytes 3440648 | tf_op jit(solution)/shard_map/ppermute | solution.py:31
  39.1 1.5 %half.1 = (f32[576,640]{1,0:T(8,128)S(1)}, bf16[320,640]{1,0:T(8,128)(2,1)S(1)}, bf16[320,640]{1,0:T(8,128)(2,1)S(1)}) custom-call(s32[1]{0:T(128)} %bitcast.refs_1_.refs_0_.core, bf16[640,640]{1,0:T(8,128)(2,1)S(1)} %get-tuple-element.37.refs_1_, bf16[1152,640]{1,0:T(8,128)(2,1)S(1)} %get-tuple-element.36.refs_8_.refs_2_, ...), custom_call_target="tpu_custom_call" | custom-call | flops 900000000 | bytes 5283840 | tf_op jit(solution)/shard_map/half/pallas_call | solution.py:54
  40.6 0.0 copy-start.7
  40.6 0.0 copy-start.8
  40.7 0.9 collective-permute-done.3.refs_1_
  41.5 0.2 add.1
  41.7 0.0 copy-done.7
  41.7 0.0 copy-done.8
  41.7 0.0 copy-start.5
  41.8 0.9 copy-done.5
  42.6 15.0 %all_to_all.20.refs_0_ = bf16[16,192,128]{2,1,0:T(8,128)(2,1)S(1)} all-to-all(bf16[16,192,128]{2,1,0:T(8,128)(2,1)S(1)} %get-tuple-element.56), channel_id=1, replica_groups=mesh['zh'=4,'zl'=2,'x'=4,'yh'=4,'yl'=2,'c'=2] {'x','yl','zl'}, dimensions={0} | all-to-all | bytes 1572864 | tf_op jit(solution)/shard_map/all_to_all | solution.py:35
  57.6 0.7 cube_sum.1
  58.4 6.5 %all-to-all-start.1 = ((bf16[16,16,128]{2,1,0:T(8,128)(2,1)}), bf16[16,16,128]{2,1,0:T(8,128)(2,1)S(1)}, u32[]{:S(2)}, u32[]{:S(2)}) async-start(bf16[16,16,128]{2,1,0:T(8,128)(2,1)} %cube_sum.1), calls=%async_computation.1 | async-start | bytes 131072 | tf_op jit(solution)/shard_map/all_to_all | solution.py:35
  64.9 0.0 copy-start.4
  64.9 8.1 %collective-permute-start.5 = (bf16[320,640]{1,0:T(8,128)(2,1)}, bf16[320,640]{1,0:T(8,128)(2,1)S(1)}, u32[]{:S(2)}, u32[]{:S(2)}) collective-permute-start(bf16[320,640]{1,0:T(8,128)(2,1)} %copy-done.8), channel_id=1, source_target_pairs={{0,510},{1,511},{2,0},{3,1},{4,2},{5,3},{6,4},{7,5},{8,6},{9,7},{1... | collective-permute-start | bytes 1228808 | tf_op jit(solution)/shard_map/ppermute | solution.py:27
  73.0 3.2 %all-to-all-done.1.refs_0_ = bf16[16,16,128]{2,1,0:T(8,128)(2,1)S(1)} async-done(((bf16[16,16,128]{2,1,0:T(8,128)(2,1)}), bf16[16,16,128]{2,1,0:T(8,128)(2,1)S(1)}, u32[]{:S(2)}, u32[]{:S(2)}) %all-to-all-start.1) | async-done | bytes 65568 | tf_op jit(solution)/shard_map/all_to_all | solution.py:35
  76.2 0.6 grid_sum.1
  76.9 3.5 %all-to-all-start.2 = ((bf16[16,16,128]{2,1,0:T(8,128)(2,1)}), bf16[16,16,128]{2,1,0:T(8,128)(2,1)S(1)}, u32[]{:S(2)}, u32[]{:S(2)}) async-start(bf16[16,16,128]{2,1,0:T(8,128)(2,1)} %grid_sum.1), calls=%async_computation.2 | async-start | bytes 131072 | tf_op jit(solution)/shard_map/all_to_all | solution.py:35
  80.4 6.7 %collective-permute-start.4 = (bf16[320,640]{1,0:T(8,128)(2,1)}, bf16[320,640]{1,0:T(8,128)(2,1)}, u32[]{:S(2)}, u32[]{:S(2)}) collective-permute-start(bf16[320,640]{1,0:T(8,128)(2,1)} %copy-done.7), channel_id=1, source_target_pairs={{1,2},{3,4},{5,6},{7,8},{9,10},{11,12},{13,14},{15,16},{17,18},{19... | collective-permute-start | bytes 1228808 | tf_op jit(solution)/shard_map/ppermute | solution.py:27
  87.1 0.0 collective-permute-done.5.refs_1_
  87.1 0.0 copy-done.4
  87.1 1.1 text.1
  88.2 3.4 %all-to-all-done.2.refs_0_ = bf16[16,16,128]{2,1,0:T(8,128)(2,1)S(1)} async-done(((bf16[16,16,128]{2,1,0:T(8,128)(2,1)}), bf16[16,16,128]{2,1,0:T(8,128)(2,1)S(1)}, u32[]{:S(2)}, u32[]{:S(2)}) %all-to-all-start.2) | async-done | bytes 65568 | tf_op jit(solution)/shard_map/all_to_all | solution.py:35
  91.6 1.7 %cube_spread.1 = bf16[16,192,128]{2,1,0:T(8,128)(2,1)} custom-call(bf16[16,16,128]{2,1,0:T(8,128)(2,1)S(1)} %all-to-all-done.2.refs_0_, s32[1]{0:T(128)} %get-tuple-element.57.refs_1_), custom_call_target="tpu_custom_call" | custom-call | flops 40000000000 | bytes 65536 | tf_op jit(solution)/shard_map/cube_spread/pallas_call | solution.py:54
  93.3 0.0 copy-start.2
  93.3 3.9 %all-to-all-start.3 = ((bf16[16,192,128]{2,1,0:T(8,128)(2,1)}), bf16[16,192,128]{2,1,0:T(8,128)(2,1)S(1)}, u32[]{:S(2)}, u32[]{:S(2)}) async-start(bf16[16,192,128]{2,1,0:T(8,128)(2,1)} %cube_spread.1), calls=%async_computation.3 | async-start | bytes 1572864 | tf_op jit(solution)/shard_map/all_to_all | solution.py:35
  97.2 0.0 collective-permute-done.4.refs_1_
  97.3 0.0 copy-done.2
  97.3 0.0 copy-start.6
  97.3 1.1 copy-done.6
  98.4 3.9 %image.1 = (bf16[320,1152]{1,0:T(8,128)(2,1)}, s32[1]{0:T(128)}) custom-call(f32[320,640]{1,0:T(8,128)S(1)} %copy-done.6, bf16[320,640]{1,0:T(8,128)(2,1)} %collective-permute-done.4.refs_1_, bf16[320,1152]{1,0:T(8,128)(2,1)S(1)} %copy-done.2, bf16[1152,640]{1,0:T(8,128)(2,1)S(1)} %copy-done), custom_call_target="tpu_custom_call" | custom-call | flops 40000000000 | bytes 3440640 | tf_op jit(solution)/shard_map/image/pallas_call | solution.py:54
  102.3 3.9 %all-to-all-done.3.refs_0_ = bf16[16,192,128]{2,1,0:T(8,128)(2,1)S(1)} async-done(((bf16[16,192,128]{2,1,0:T(8,128)(2,1)}), bf16[16,192,128]{2,1,0:T(8,128)(2,1)S(1)}, u32[]{:S(2)}, u32[]{:S(2)}) %all-to-all-start.3) | async-done | bytes 786464 | tf_op jit(solution)/shard_map/all_to_all | solution.py:35
  106.3 0.7 pass.1.parts
  107.0 7.5 %collective-permute-start.6 = (bf16[16,192,128]{2,1,0:T(8,128)(2,1)S(1)}, bf16[16,192,128]{2,1,0:T(8,128)(2,1)S(1)}, u32[]{:S(2)}, u32[]{:S(2)}) collective-permute-start(bf16[16,192,128]{2,1,0:T(8,128)(2,1)S(1)} %pass.1.parts), channel_id=1, source_target_pairs={{0,1},{1,0},{2,3},{3,2},{4,5},{5,4},{6,7},{7,6},{8,9},{9,8},{10,11... | collective-permute-start | bytes 2359304 | tf_op jit(solution)/shard_map/ppermute | solution.py:31
  114.5 1.0 first_half.1.held
  115.5 0.9 collective-permute-done.6.parts
  116.4 1.0 second_half.1
Async XLA Ops:
  0.6 15.2 %collective-permute-start.1 = (bf16[320,1152]{1,0:T(8,128)(2,1)}, bf16[320,1152]{1,0:T(8,128)(2,1)S(1)}, u32[]{:S(2)}, u32[]{:S(2)}) collective-permute-start(bf16[320,1152]{1,0:T(8,128)(2,1)} %refs_2_.6), channel_id=1, source_target_pairs={{0,1},{1,0},{2,3},{3,2},{4,5},{5,4},{6,7},{7,6},{8,9},{9,8},{10,11... | collective-permute-start | bytes 2211848 | tf_op jit(solution)/shard_map/ppermute | solution.py:31
  9.4 20.4 %collective-permute-start = (bf16[320,640]{1,0:T(8,128)(2,1)}, bf16[320,640]{1,0:T(8,128)(2,1)S(1)}, u32[]{:S(2)}, u32[]{:S(2)}) collective-permute-start(bf16[320,640]{1,0:T(8,128)(2,1)} %refs_2_.7), channel_id=1, source_target_pairs={{0,2},{1,3},{2,4},{3,5},{4,6},{5,7},{6,8},{7,9},{8,10},{9,11},{10,... | collective-permute-start | bytes 1228808 | tf_op jit(solution)/shard_map/ppermute | solution.py:27
  11.4 22.2 %collective-permute-start.2 = (bf16[320,1152]{1,0:T(8,128)(2,1)}, bf16[320,1152]{1,0:T(8,128)(2,1)S(1)}, u32[]{:S(2)}, u32[]{:S(2)}) collective-permute-start(bf16[320,1152]{1,0:T(8,128)(2,1)} %refs_2_.6), channel_id=1, source_target_pairs={{0,511},{2,1},{4,3},{6,5},{8,7},{10,9},{12,11},{14,13},{16,15},{18... | collective-permute-start | bytes 2211848 | tf_op jit(solution)/shard_map/ppermute | solution.py:27
  14.1 1.0 copy-start.3
  15.1 1.4 %copy-start = (bf16[1152,640]{1,0:T(8,128)(2,1)S(1)}, bf16[1152,640]{1,0:T(8,128)(2,1)}, u32[]{:S(2)}) copy-start(bf16[1152,640]{1,0:T(8,128)(2,1)} %refs_3_.3) | copy-start | bytes 4423684
  15.1 1.6 %copy-start.1 = (bf16[320,1152]{1,0:T(8,128)(2,1)S(1)}, bf16[320,1152]{1,0:T(8,128)(2,1)}, u32[]{:S(2)}) copy-start(bf16[320,1152]{1,0:T(8,128)(2,1)} %refs_2_.6) | copy-start | bytes 2211844
  36.6 4.9 %collective-permute-start.3 = (bf16[896,640]{1,0:T(8,128)(2,1)S(1)}, bf16[896,640]{1,0:T(8,128)(2,1)S(1)}, u32[]{:S(2)}, u32[]{:S(2)}) collective-permute-start(bf16[896,640]{1,0:T(8,128)(2,1)S(1)} %get-tuple-element.48), channel_id=1, source_target_pairs={{0,1},{1,0},{2,3},{3,2},{4,5},{5,4},{6,7},{7,6},{8,9},{9,8},{10,11... | collective-permute-start | bytes 3440648 | tf_op jit(solution)/shard_map/ppermute | solution.py:31
  40.6 1.1 copy-start.7
  40.6 1.1 copy-start.8
  41.7 0.9 copy-start.5
  58.4 17.9 %all-to-all-start.1 = ((bf16[16,16,128]{2,1,0:T(8,128)(2,1)}), bf16[16,16,128]{2,1,0:T(8,128)(2,1)S(1)}, u32[]{:S(2)}, u32[]{:S(2)}) async-start(bf16[16,16,128]{2,1,0:T(8,128)(2,1)} %cube_sum.1), calls=%async_computation.1 | async-start | bytes 131072 | tf_op jit(solution)/shard_map/all_to_all | solution.py:35
  64.9 22.3 %copy-start.4 = (bf16[320,640]{1,0:T(8,128)(2,1)S(1)}, bf16[320,640]{1,0:T(8,128)(2,1)}, u32[]{:S(2)}) copy-start(bf16[320,640]{1,0:T(8,128)(2,1)} %refs_2_.7) | copy-start | bytes 1228804
  64.9 22.2 %collective-permute-start.5 = (bf16[320,640]{1,0:T(8,128)(2,1)}, bf16[320,640]{1,0:T(8,128)(2,1)S(1)}, u32[]{:S(2)}, u32[]{:S(2)}) collective-permute-start(bf16[320,640]{1,0:T(8,128)(2,1)} %copy-done.8), channel_id=1, source_target_pairs={{0,510},{1,511},{2,0},{3,1},{4,2},{5,3},{6,4},{7,5},{8,6},{9,7},{1... | collective-permute-start | bytes 1228808 | tf_op jit(solution)/shard_map/ppermute | solution.py:27
  76.9 14.7 %all-to-all-start.2 = ((bf16[16,16,128]{2,1,0:T(8,128)(2,1)}), bf16[16,16,128]{2,1,0:T(8,128)(2,1)S(1)}, u32[]{:S(2)}, u32[]{:S(2)}) async-start(bf16[16,16,128]{2,1,0:T(8,128)(2,1)} %grid_sum.1), calls=%async_computation.2 | async-start | bytes 131072 | tf_op jit(solution)/shard_map/all_to_all | solution.py:35
  80.4 16.9 %collective-permute-start.4 = (bf16[320,640]{1,0:T(8,128)(2,1)}, bf16[320,640]{1,0:T(8,128)(2,1)}, u32[]{:S(2)}, u32[]{:S(2)}) collective-permute-start(bf16[320,640]{1,0:T(8,128)(2,1)} %copy-done.7), channel_id=1, source_target_pairs={{1,2},{3,4},{5,6},{7,8},{9,10},{11,12},{13,14},{15,16},{17,18},{19... | collective-permute-start | bytes 1228808 | tf_op jit(solution)/shard_map/ppermute | solution.py:27
  93.3 4.0 %copy-start.2 = (bf16[320,1152]{1,0:T(8,128)(2,1)S(1)}, bf16[320,1152]{1,0:T(8,128)(2,1)}, u32[]{:S(2)}) copy-start(bf16[320,1152]{1,0:T(8,128)(2,1)} %refs_2_.6) | copy-start | bytes 2211844
  93.3 13.0 %all-to-all-start.3 = ((bf16[16,192,128]{2,1,0:T(8,128)(2,1)}), bf16[16,192,128]{2,1,0:T(8,128)(2,1)S(1)}, u32[]{:S(2)}, u32[]{:S(2)}) async-start(bf16[16,192,128]{2,1,0:T(8,128)(2,1)} %cube_spread.1), calls=%async_computation.3 | async-start | bytes 1572864 | tf_op jit(solution)/shard_map/all_to_all | solution.py:35
  97.3 1.1 copy-start.6
  107.0 9.4 %collective-permute-start.6 = (bf16[16,192,128]{2,1,0:T(8,128)(2,1)S(1)}, bf16[16,192,128]{2,1,0:T(8,128)(2,1)S(1)}, u32[]{:S(2)}, u32[]{:S(2)}) collective-permute-start(bf16[16,192,128]{2,1,0:T(8,128)(2,1)S(1)} %pass.1.parts), channel_id=1, source_target_pairs={{0,1},{1,0},{2,3},{3,2},{4,5},{5,4},{6,7},{7,6},{8,9},{9,8},{10,11... | collective-permute-start | bytes 2359304 | tf_op jit(solution)/shard_map/ppermute | solution.py:31

commit v7 on v6

--- a/solution.py
+++ b/solution.py
@@ -190,7 +190,7 @@
 
 
 def pass_body(parts, out):
-    out[...] = parts[...]
+    out[...] = parts[0 : SIDE - 1]
 
 
 def put_half(parts, out, start, half, sem):
@@ -275,7 +275,7 @@
         image_body, "image", ((VMEM, d_img), (VMEM, d_late), (VMEM, images), (VMEM, head)),
         ((VMEM, (ROWS, D), bf16),), flops=40_000_000_000, mark=True)
     part = call(
-        pass_body, "pass", ((VMEM, exchange(part, CUBE)),), ((VMEM, (SIDE, TILES * 16, 128), bf16),), after=(mark,))
+        pass_body, "pass", ((VMEM, exchange(part, CUBE)),), ((VMEM, (SIDE - 1, TILES * 16, 128), bf16),), after=(mark,))
     grad_head = halves(core, part, swapped(part))
     return (grad_image, grad_text, grad_head)
 

time: 118 us -> 118 us (level)
  no operation moved by 1% of the time
where the time goes in v7:
time: 118 us; the launch traced here: 117 us
  starting transfers between devices  50.8 us (43%)
  Pallas kernels  23.5 us (20%)
  waiting for transfers between devices  21.8 us (18%)
  blocking collectives  15 us (13%)
  local copies, waits for them, and re-layouts  3.89 us (3%)
  between operations  2.19 us (2%)
    pallas_call x12, Pallas kernels, call(): pl.pallas_call(run, out_shape=tuple((jax.ShapeDtypeStruct(dims, dtype) fo...  21.5 us
    ppermute x3, starting transfers between devices, swapped(): return lax.ppermute(value, 'c', [(0, 1), (1, 0)])  18.8 us
    ppermute x4, starting transfers between devices, shifted(): lax.ppermute(value, AXES, [(s, (s + steps) % COUNT) for s in sources])  18.1 us
    all_to_all x1, blocking collectives, exchange(): return lax.all_to_all(value, axes, 0, 0)  15 us
    all_to_all x3, starting transfers between devices, exchange(): return lax.all_to_all(value, axes, 0, 0)  13.9 us
    all_to_all x3, waiting for transfers between devices, exchange(): return lax.all_to_all(value, axes, 0, 0)  10.5 us
    ppermute x4, waiting for transfers between devices, shifted(): lax.ppermute(value, AXES, [(s, (s + steps) % COUNT) for s in sources])  9.57 us
    unnamed x18, local copies, waits for them, and re-layouts  3.89 us
  transfers between devices with their start and end apart: 10, of which 6 were waited for; matrix products, arithmetic and copies ran while one was open for 0% of the time, Pallas kernels for 15%

profile of v7, /device:TPU:1, one launch (start us, length us, event | category | flops | bytes accessed | tf_op | source)
XLA Modules:
  0.0 117.3 jit_solution(14919154548775048160)
XLA Ops:
  0.6 8.8 %collective-permute-start.1 = (bf16[320,1152]{1,0:T(8,128)(2,1)}, bf16[320,1152]{1,0:T(8,128)(2,1)S(1)}, u32[]{:S(2)}, u32[]{:S(2)}) collective-permute-start(bf16[320,1152]{1,0:T(8,128)(2,1)} %refs_2_.6), channel_id=1, source_target_pairs={{0,1},{1,0},{2,3},{3,2},{4,5},{5,4},{6,7},{7,6},{8,9},{9,8},{10,11... | collective-permute-start | bytes 2211848 | tf_op jit(solution)/shard_map/ppermute | solution.py:31
  9.4 1.9 %collective-permute-start = (bf16[320,640]{1,0:T(8,128)(2,1)}, bf16[320,640]{1,0:T(8,128)(2,1)S(1)}, u32[]{:S(2)}, u32[]{:S(2)}) collective-permute-start(bf16[320,640]{1,0:T(8,128)(2,1)} %refs_2_.7), channel_id=1, source_target_pairs={{0,2},{1,3},{2,4},{3,5},{4,6},{5,7},{6,8},{7,9},{8,10},{9,11},{10,... | collective-permute-start | bytes 1228808 | tf_op jit(solution)/shard_map/ppermute | solution.py:27
  11.4 1.3 %collective-permute-start.2 = (bf16[320,1152]{1,0:T(8,128)(2,1)}, bf16[320,1152]{1,0:T(8,128)(2,1)S(1)}, u32[]{:S(2)}, u32[]{:S(2)}) collective-permute-start(bf16[320,1152]{1,0:T(8,128)(2,1)} %refs_2_.6), channel_id=1, source_target_pairs={{0,511},{2,1},{4,3},{6,5},{8,7},{10,9},{12,11},{14,13},{16,15},{18... | collective-permute-start | bytes 2211848 | tf_op jit(solution)/shard_map/ppermute | solution.py:27
  14.0 0.1 pad_maximum_fusion.refs_0_
  14.1 0.0 copy-start.3
  14.1 1.0 copy-done.3
  15.1 0.0 copy-start
  15.1 0.0 copy-start.1
  15.1 0.7 words.1.refs_4_
  15.8 0.0 collective-permute-done.1.refs_3_
  15.8 0.7 copy-done
  16.4 0.2 copy-done.1
  16.6 3.7 %near.1 = (f32[640,640]{1,0:T(8,128)S(1)}, f32[640,1]{1,0:T(8,128)S(1)}, bf16[640,640]{1,0:T(8,128)(2,1)S(1)}, f32[640,640]{1,0:T(8,128)S(1)}, bf16[640,320]{1,0...) custom-call(f32[2]{0:T(128)S(1)} %pad_maximum_fusion.refs_0_, s32[1]{0:T(128)} %bitcast.refs_1_.refs_0_.core, ...), custom_call_target="tpu_custom_call" | custom-call | flops 100000000 | bytes 3358720 | tf_op jit(solution)/shard_map/near/pallas_call | solution.py:54
  20.3 9.6 %collective-permute-done.refs_2_ = bf16[320,640]{1,0:T(8,128)(2,1)S(1)} collective-permute-done((bf16[320,640]{1,0:T(8,128)(2,1)}, bf16[320,640]{1,0:T(8,128)(2,1)S(1)}, u32[]{:S(2)}, u32[]{:S(2)}) %collective-permute-start) | collective-permute-done | bytes 409632 | tf_op jit(solution)/shard_map/ppermute | solution.py:27
  29.9 3.6 %prev.1 = (f32[576,640]{1,0:T(8,128)S(1)}, bf16[640,640]{1,0:T(8,128)(2,1)S(1)}, f32[320,640]{1,0:T(8,128)S(1)}, bf16[320,640]{1,0:T(8,128)(2,1)S(1)}, bf16[320,...) custom-call(f32[2]{0:T(128)S(1)} %pad_maximum_fusion.refs_0_, s32[1]{0:T(128)} %bitcast.refs_1_.refs_0_.core, ...), custom_call_target="tpu_custom_call" | custom-call | flops 40000000000 | bytes 6392320 | tf_op jit(solution)/shard_map/prev/pallas_call | solution.py:54
  33.5 0.0 collective-permute-done.2.refs_2_
  33.5 3.1 %next.1 = (bf16[896,640]{1,0:T(8,128)(2,1)S(1)}, bf16[320,640]{1,0:T(8,128)(2,1)S(1)}, bf16[1152,320]{1,0:T(8,128)(2,1)S(1)}, bf16[320,320]{1,0:T(8,128)(2,1)S(1...) custom-call(f32[2]{0:T(128)S(1)} %pad_maximum_fusion.refs_0_, s32[1]{0:T(128)} %bitcast.refs_1_.refs_0_.core, ...), custom_call_target="tpu_custom_call" | custom-call | flops 1000000000 | bytes 4505600 | tf_op jit(solution)/shard_map/next/pallas_call | solution.py:54
  36.6 2.5 %collective-permute-start.3 = (bf16[896,640]{1,0:T(8,128)(2,1)S(1)}, bf16[896,640]{1,0:T(8,128)(2,1)S(1)}, u32[]{:S(2)}, u32[]{:S(2)}) collective-permute-start(bf16[896,640]{1,0:T(8,128)(2,1)S(1)} %get-tuple-element.48), channel_id=1, source_target_pairs={{0,1},{1,0},{2,3},{3,2},{4,5},{5,4},{6,7},{7,6},{8,9},{9,8},{10,11... | collective-permute-start | bytes 3440648 | tf_op jit(solution)/shard_map/ppermute | solution.py:31
  39.1 1.5 %half.1 = (f32[576,640]{1,0:T(8,128)S(1)}, bf16[320,640]{1,0:T(8,128)(2,1)S(1)}, bf16[320,640]{1,0:T(8,128)(2,1)S(1)}) custom-call(s32[1]{0:T(128)} %bitcast.refs_1_.refs_0_.core, bf16[640,640]{1,0:T(8,128)(2,1)S(1)} %get-tuple-element.37.refs_1_, bf16[1152,640]{1,0:T(8,128)(2,1)S(1)} %get-tuple-element.36.refs_8_.refs_2_, ...), custom_call_target="tpu_custom_call" | custom-call | flops 900000000 | bytes 5283840 | tf_op jit(solution)/shard_map/half/pallas_call | solution.py:54
  40.6 0.0 copy-start.7
  40.6 0.0 copy-start.8
  40.7 0.9 collective-permute-done.3.refs_1_
  41.5 0.2 add.1
  41.7 0.0 copy-done.7
  41.7 0.0 copy-done.8
  41.7 0.0 copy-start.5
  41.8 0.9 copy-done.5
  42.6 15.0 %all_to_all.20.refs_0_ = bf16[16,192,128]{2,1,0:T(8,128)(2,1)S(1)} all-to-all(bf16[16,192,128]{2,1,0:T(8,128)(2,1)S(1)} %get-tuple-element.56), channel_id=1, replica_groups=mesh['zh'=4,'zl'=2,'x'=4,'yh'=4,'yl'=2,'c'=2] {'x','yl','zl'}, dimensions={0} | all-to-all | bytes 1572864 | tf_op jit(solution)/shard_map/all_to_all | solution.py:35
  57.6 0.7 cube_sum.1
  58.4 6.5 %all-to-all-start.1 = ((bf16[16,16,128]{2,1,0:T(8,128)(2,1)}), bf16[16,16,128]{2,1,0:T(8,128)(2,1)S(1)}, u32[]{:S(2)}, u32[]{:S(2)}) async-start(bf16[16,16,128]{2,1,0:T(8,128)(2,1)} %cube_sum.1), calls=%async_computation.1 | async-start | bytes 131072 | tf_op jit(solution)/shard_map/all_to_all | solution.py:35
  64.9 0.0 copy-start.4
  64.9 8.1 %collective-permute-start.5 = (bf16[320,640]{1,0:T(8,128)(2,1)}, bf16[320,640]{1,0:T(8,128)(2,1)S(1)}, u32[]{:S(2)}, u32[]{:S(2)}) collective-permute-start(bf16[320,640]{1,0:T(8,128)(2,1)} %copy-done.8), channel_id=1, source_target_pairs={{0,510},{1,511},{2,0},{3,1},{4,2},{5,3},{6,4},{7,5},{8,6},{9,7},{1... | collective-permute-start | bytes 1228808 | tf_op jit(solution)/shard_map/ppermute | solution.py:27
  73.0 3.2 %all-to-all-done.1.refs_0_ = bf16[16,16,128]{2,1,0:T(8,128)(2,1)S(1)} async-done(((bf16[16,16,128]{2,1,0:T(8,128)(2,1)}), bf16[16,16,128]{2,1,0:T(8,128)(2,1)S(1)}, u32[]{:S(2)}, u32[]{:S(2)}) %all-to-all-start.1) | async-done | bytes 65568 | tf_op jit(solution)/shard_map/all_to_all | solution.py:35
  76.2 0.6 grid_sum.1
  76.9 3.5 %all-to-all-start.2 = ((bf16[16,16,128]{2,1,0:T(8,128)(2,1)}), bf16[16,16,128]{2,1,0:T(8,128)(2,1)S(1)}, u32[]{:S(2)}, u32[]{:S(2)}) async-start(bf16[16,16,128]{2,1,0:T(8,128)(2,1)} %grid_sum.1), calls=%async_computation.2 | async-start | bytes 131072 | tf_op jit(solution)/shard_map/all_to_all | solution.py:35
  80.4 6.7 %collective-permute-start.4 = (bf16[320,640]{1,0:T(8,128)(2,1)}, bf16[320,640]{1,0:T(8,128)(2,1)}, u32[]{:S(2)}, u32[]{:S(2)}) collective-permute-start(bf16[320,640]{1,0:T(8,128)(2,1)} %copy-done.7), channel_id=1, source_target_pairs={{1,2},{3,4},{5,6},{7,8},{9,10},{11,12},{13,14},{15,16},{17,18},{19... | collective-permute-start | bytes 1228808 | tf_op jit(solution)/shard_map/ppermute | solution.py:27
  87.1 0.0 collective-permute-done.5.refs_1_
  87.1 0.0 copy-done.4
  87.1 1.1 text.1
  88.2 3.4 %all-to-all-done.2.refs_0_ = bf16[16,16,128]{2,1,0:T(8,128)(2,1)S(1)} async-done(((bf16[16,16,128]{2,1,0:T(8,128)(2,1)}), bf16[16,16,128]{2,1,0:T(8,128)(2,1)S(1)}, u32[]{:S(2)}, u32[]{:S(2)}) %all-to-all-start.2) | async-done | bytes 65568 | tf_op jit(solution)/shard_map/all_to_all | solution.py:35
  91.6 1.7 %cube_spread.1 = bf16[16,192,128]{2,1,0:T(8,128)(2,1)} custom-call(bf16[16,16,128]{2,1,0:T(8,128)(2,1)S(1)} %all-to-all-done.2.refs_0_, s32[1]{0:T(128)} %get-tuple-element.57.refs_1_), custom_call_target="tpu_custom_call" | custom-call | flops 40000000000 | bytes 65536 | tf_op jit(solution)/shard_map/cube_spread/pallas_call | solution.py:54
  93.3 0.0 copy-start.2
  93.3 3.9 %all-to-all-start.3 = ((bf16[16,192,128]{2,1,0:T(8,128)(2,1)}), bf16[16,192,128]{2,1,0:T(8,128)(2,1)S(1)}, u32[]{:S(2)}, u32[]{:S(2)}) async-start(bf16[16,192,128]{2,1,0:T(8,128)(2,1)} %cube_spread.1), calls=%async_computation.3 | async-start | bytes 1572864 | tf_op jit(solution)/shard_map/all_to_all | solution.py:35
  97.2 0.0 collective-permute-done.4.refs_1_
  97.3 0.0 copy-done.2
  97.3 0.0 copy-start.6
  97.3 1.1 copy-done.6
  98.4 3.9 %image.1 = (bf16[320,1152]{1,0:T(8,128)(2,1)}, s32[1]{0:T(128)}) custom-call(f32[320,640]{1,0:T(8,128)S(1)} %copy-done.6, bf16[320,640]{1,0:T(8,128)(2,1)} %collective-permute-done.4.refs_1_, bf16[320,1152]{1,0:T(8,128)(2,1)S(1)} %copy-done.2, bf16[1152,640]{1,0:T(8,128)(2,1)S(1)} %copy-done), custom_call_target="tpu_custom_call" | custom-call | flops 40000000000 | bytes 3440640 | tf_op jit(solution)/shard_map/image/pallas_call | solution.py:54
  102.3 3.9 %all-to-all-done.3.refs_0_ = bf16[16,192,128]{2,1,0:T(8,128)(2,1)S(1)} async-done(((bf16[16,192,128]{2,1,0:T(8,128)(2,1)}), bf16[16,192,128]{2,1,0:T(8,128)(2,1)S(1)}, u32[]{:S(2)}, u32[]{:S(2)}) %all-to-all-start.3) | async-done | bytes 786464 | tf_op jit(solution)/shard_map/all_to_all | solution.py:35
  106.3 0.7 pass.1.parts
  107.0 7.5 %collective-permute-start.6 = (bf16[15,192,128]{2,1,0:T(8,128)(2,1)S(1)}, bf16[15,192,128]{2,1,0:T(8,128)(2,1)S(1)}, u32[]{:S(2)}, u32[]{:S(2)}) collective-permute-start(bf16[15,192,128]{2,1,0:T(8,128)(2,1)S(1)} %pass.1.parts), channel_id=1, source_target_pairs={{0,1},{1,0},{2,3},{3,2},{4,5},{5,4},{6,7},{7,6},{8,9},{9,8},{10,11... | collective-permute-start | bytes 2211848 | tf_op jit(solution)/shard_map/ppermute | solution.py:31
  114.5 1.0 first_half.1.held
  115.5 0.8 collective-permute-done.6.parts
  116.3 1.0 second_half.1
Async XLA Ops:
  0.6 15.2 %collective-permute-start.1 = (bf16[320,1152]{1,0:T(8,128)(2,1)}, bf16[320,1152]{1,0:T(8,128)(2,1)S(1)}, u32[]{:S(2)}, u32[]{:S(2)}) collective-permute-start(bf16[320,1152]{1,0:T(8,128)(2,1)} %refs_2_.6), channel_id=1, source_target_pairs={{0,1},{1,0},{2,3},{3,2},{4,5},{5,4},{6,7},{7,6},{8,9},{9,8},{10,11... | collective-permute-start | bytes 2211848 | tf_op jit(solution)/shard_map/ppermute | solution.py:31
  9.4 20.4 %collective-permute-start = (bf16[320,640]{1,0:T(8,128)(2,1)}, bf16[320,640]{1,0:T(8,128)(2,1)S(1)}, u32[]{:S(2)}, u32[]{:S(2)}) collective-permute-start(bf16[320,640]{1,0:T(8,128)(2,1)} %refs_2_.7), channel_id=1, source_target_pairs={{0,2},{1,3},{2,4},{3,5},{4,6},{5,7},{6,8},{7,9},{8,10},{9,11},{10,... | collective-permute-start | bytes 1228808 | tf_op jit(solution)/shard_map/ppermute | solution.py:27
  11.4 22.2 %collective-permute-start.2 = (bf16[320,1152]{1,0:T(8,128)(2,1)}, bf16[320,1152]{1,0:T(8,128)(2,1)S(1)}, u32[]{:S(2)}, u32[]{:S(2)}) collective-permute-start(bf16[320,1152]{1,0:T(8,128)(2,1)} %refs_2_.6), channel_id=1, source_target_pairs={{0,511},{2,1},{4,3},{6,5},{8,7},{10,9},{12,11},{14,13},{16,15},{18... | collective-permute-start | bytes 2211848 | tf_op jit(solution)/shard_map/ppermute | solution.py:27
  14.1 1.0 copy-start.3
  15.1 1.4 %copy-start = (bf16[1152,640]{1,0:T(8,128)(2,1)S(1)}, bf16[1152,640]{1,0:T(8,128)(2,1)}, u32[]{:S(2)}) copy-start(bf16[1152,640]{1,0:T(8,128)(2,1)} %refs_3_.3) | copy-start | bytes 4423684
  15.1 1.6 %copy-start.1 = (bf16[320,1152]{1,0:T(8,128)(2,1)S(1)}, bf16[320,1152]{1,0:T(8,128)(2,1)}, u32[]{:S(2)}) copy-start(bf16[320,1152]{1,0:T(8,128)(2,1)} %refs_2_.6) | copy-start | bytes 2211844
  36.6 4.9 %collective-permute-start.3 = (bf16[896,640]{1,0:T(8,128)(2,1)S(1)}, bf16[896,640]{1,0:T(8,128)(2,1)S(1)}, u32[]{:S(2)}, u32[]{:S(2)}) collective-permute-start(bf16[896,640]{1,0:T(8,128)(2,1)S(1)} %get-tuple-element.48), channel_id=1, source_target_pairs={{0,1},{1,0},{2,3},{3,2},{4,5},{5,4},{6,7},{7,6},{8,9},{9,8},{10,11... | collective-permute-start | bytes 3440648 | tf_op jit(solution)/shard_map/ppermute | solution.py:31
  40.6 1.1 copy-start.7
  40.6 1.1 copy-start.8
  41.7 0.9 copy-start.5
  58.4 17.9 %all-to-all-start.1 = ((bf16[16,16,128]{2,1,0:T(8,128)(2,1)}), bf16[16,16,128]{2,1,0:T(8,128)(2,1)S(1)}, u32[]{:S(2)}, u32[]{:S(2)}) async-start(bf16[16,16,128]{2,1,0:T(8,128)(2,1)} %cube_sum.1), calls=%async_computation.1 | async-start | bytes 131072 | tf_op jit(solution)/shard_map/all_to_all | solution.py:35
  64.9 22.3 %copy-start.4 = (bf16[320,640]{1,0:T(8,128)(2,1)S(1)}, bf16[320,640]{1,0:T(8,128)(2,1)}, u32[]{:S(2)}) copy-start(bf16[320,640]{1,0:T(8,128)(2,1)} %refs_2_.7) | copy-start | bytes 1228804
  64.9 22.2 %collective-permute-start.5 = (bf16[320,640]{1,0:T(8,128)(2,1)}, bf16[320,640]{1,0:T(8,128)(2,1)S(1)}, u32[]{:S(2)}, u32[]{:S(2)}) collective-permute-start(bf16[320,640]{1,0:T(8,128)(2,1)} %copy-done.8), channel_id=1, source_target_pairs={{0,510},{1,511},{2,0},{3,1},{4,2},{5,3},{6,4},{7,5},{8,6},{9,7},{1... | collective-permute-start | bytes 1228808 | tf_op jit(solution)/shard_map/ppermute | solution.py:27
  76.9 14.7 %all-to-all-start.2 = ((bf16[16,16,128]{2,1,0:T(8,128)(2,1)}), bf16[16,16,128]{2,1,0:T(8,128)(2,1)S(1)}, u32[]{:S(2)}, u32[]{:S(2)}) async-start(bf16[16,16,128]{2,1,0:T(8,128)(2,1)} %grid_sum.1), calls=%async_computation.2 | async-start | bytes 131072 | tf_op jit(solution)/shard_map/all_to_all | solution.py:35
  80.4 16.9 %collective-permute-start.4 = (bf16[320,640]{1,0:T(8,128)(2,1)}, bf16[320,640]{1,0:T(8,128)(2,1)}, u32[]{:S(2)}, u32[]{:S(2)}) collective-permute-start(bf16[320,640]{1,0:T(8,128)(2,1)} %copy-done.7), channel_id=1, source_target_pairs={{1,2},{3,4},{5,6},{7,8},{9,10},{11,12},{13,14},{15,16},{17,18},{19... | collective-permute-start | bytes 1228808 | tf_op jit(solution)/shard_map/ppermute | solution.py:27
  93.3 4.0 %copy-start.2 = (bf16[320,1152]{1,0:T(8,128)(2,1)S(1)}, bf16[320,1152]{1,0:T(8,128)(2,1)}, u32[]{:S(2)}) copy-start(bf16[320,1152]{1,0:T(8,128)(2,1)} %refs_2_.6) | copy-start | bytes 2211844
  93.3 13.0 %all-to-all-start.3 = ((bf16[16,192,128]{2,1,0:T(8,128)(2,1)}), bf16[16,192,128]{2,1,0:T(8,128)(2,1)S(1)}, u32[]{:S(2)}, u32[]{:S(2)}) async-start(bf16[16,192,128]{2,1,0:T(8,128)(2,1)} %cube_spread.1), calls=%async_computation.3 | async-start | bytes 1572864 | tf_op jit(solution)/shard_map/all_to_all | solution.py:35
  97.3 1.1 copy-start.6
  107.0 9.3 %collective-permute-start.6 = (bf16[15,192,128]{2,1,0:T(8,128)(2,1)S(1)}, bf16[15,192,128]{2,1,0:T(8,128)(2,1)S(1)}, u32[]{:S(2)}, u32[]{:S(2)}) collective-permute-start(bf16[15,192,128]{2,1,0:T(8,128)(2,1)S(1)} %pass.1.parts), channel_id=1, source_target_pairs={{0,1},{1,0},{2,3},{3,2},{4,5},{5,4},{6,7},{7,6},{8,9},{9,8},{10,11... | collective-permute-start | bytes 2211848 | tf_op jit(solution)/shard_map/ppermute | solution.py:31
